TPU v7x, 1024 devices: a whole 8x8x8 slice. The times are simulated.
1024 devices in a mesh: dp: 16 (over z, core), expert: 64 (over x, y).
Axes of the slice: x: 8, y: 8, z: 8, core: 2. Of those that a mesh axis runs over, the one named last changes fastest.
Arguments:
- tokens: bfloat16 [32768, 1024], P(('dp', 'expert')), may hold values from -6 to 6
- cotangent: bfloat16 [32768, 1024], P(('dp', 'expert')), may hold values from -0.59765625 to 0.59765625
- route_weight: float32 [32768, 8], P(('dp', 'expert')), may hold values from 0.1 to 1
- routed_experts: int32 [32768, 8], P(('dp', 'expert')), may hold values from 0 to 63, as said below
- gate_weights: bfloat16 [64, 1024, 384], P('expert'), may hold values from -0.1875 to 0.1875
- up_weights: bfloat16 [64, 1024, 384], P('expert'), may hold values from -0.1875 to 0.1875
- down_weights: bfloat16 [64, 384, 1024], P('expert'), may hold values from -0.3125 to 0.3125
Outputs:
- layer_out: bfloat16 [32768, 1024], P(('dp', 'expert'))
- route_gradient: float32 [32768, 8], P(('dp', 'expert'))
- gate_gradient: float32 [64, 1024, 384], P('expert', 'dp')
- up_gradient: float32 [64, 1024, 384], P('expert', 'dp')
- down_gradient: float32 [64, 384, 1024], P('expert', 'dp')
Inputs may be any that keep to these rules, and one draw needn't show every extreme that they name: `routed_experts`: each row names 8 different experts. One expert is named by every row. In each aligned block of 32 rows (the rows of one device), every other expert is named by at most 4 rows, and one expert, the same in all blocks, by exactly 4 rows.
All inputs are finite; a program needn't handle non-finite values.
Results may differ from a plain program's by a relative error of at most 0.02.
Values may be sent and summed in bfloat16 or wider, within the bound.
No kernel may reach another device: no remote copies, remote signals or barrier semaphores. Data moves between devices by JAX's collectives and lax.ppermute only.
A program may use at most 32 MiB of HBM per device.

v0:
```python
import jax
import jax.numpy as jnp
from jax import lax
from jax.sharding import PartitionSpec as P

highest = lax.Precision.HIGHEST


def from_root(value, axis, source):
    kept = jnp.where(lax.axis_index(axis) == source, value, 0).astype(value.dtype)
    return lax.psum(kept, axis)


def expert_pass(slot_rows, gate_weight, up_weight, down_weight):
    features = gate_weight.shape[0]
    inputs = slot_rows[:, :features]
    scaled = slot_rows[:, features:]
    gate_value = jnp.dot(inputs, gate_weight, preferred_element_type=jnp.float32)
    up_value = jnp.dot(inputs, up_weight, preferred_element_type=jnp.float32)
    sigmoid = jax.nn.sigmoid(gate_value)
    active = gate_value * sigmoid
    hidden = (active * up_value).astype(jnp.bfloat16)
    output = jnp.dot(hidden, down_weight, preferred_element_type=jnp.float32).astype(jnp.bfloat16)
    upstream = lax.dot_general(
        scaled, down_weight, (((1,), (1,)), ((), ())), preferred_element_type=jnp.float32
    )
    slope_term = sigmoid * (1.0 + gate_value * (1.0 - sigmoid))
    gate_delta = (upstream * up_value * slope_term).astype(jnp.bfloat16)
    up_delta = (upstream * active).astype(jnp.bfloat16)
    outer_dims = (((0,), (0,)), ((), ()))
    grad_gate = lax.dot_general(inputs, gate_delta, outer_dims, preferred_element_type=jnp.float32)
    grad_up = lax.dot_general(inputs, up_delta, outer_dims, preferred_element_type=jnp.float32)
    grad_down = lax.dot_general(hidden, scaled, outer_dims, preferred_element_type=jnp.float32)
    return (output, (grad_gate, grad_up, grad_down))


def on_device(
    tokens, cotangent, route_weight, routed_experts, gate_weights, up_weights, down_weights
):
    experts = lax.axis_size("expert")
    my_index = lax.axis_index("expert")
    tok_rows, features = tokens.shape
    fanout = routed_experts.shape[1]
    cap_hot = max(1, tok_rows // experts)
    cap_own = (tok_rows * (fanout - 1) + experts - 2) // (experts - 1)
    capacity = cap_own + cap_hot
    slot_count = experts * capacity
    route_count = tok_rows * fanout
    flat_experts = routed_experts.reshape(route_count)
    expert_range = jnp.arange(experts, dtype=jnp.int32)
    counts_table = (flat_experts[:, None] == expert_range[None, :]).astype(jnp.int32)
    busiest = jnp.argmax(jnp.sum(counts_table, axis=0))
    is_hot = flat_experts == busiest
    cold_table = counts_table * (1 - is_hot.astype(jnp.int32))[:, None]
    earlier = jnp.cumsum(cold_table, axis=0) - cold_table
    position = jnp.sum(earlier * cold_table, axis=1)
    route_token = jnp.arange(route_count, dtype=jnp.int32) // fanout
    copy_rank = (my_index * tok_rows + route_token) % experts
    holder = (busiest + copy_rank) % experts
    slot_index = jnp.where(
        is_hot,
        holder * capacity + cap_own + route_token // experts,
        flat_experts * capacity + position,
    )
    matches = (jnp.arange(slot_count, dtype=jnp.int32)[:, None] == slot_index[None, :]).reshape(
        slot_count, tok_rows, fanout
    )
    placing = jnp.any(matches, axis=2).astype(jnp.bfloat16)
    weighting = jnp.sum(jnp.where(matches, route_weight[None, :, :], 0.0), axis=2)
    token_rows = jnp.dot(placing, tokens, preferred_element_type=jnp.float32).astype(jnp.bfloat16)
    scaled_rows = jnp.dot(weighting, cotangent.astype(jnp.float32), precision=highest).astype(
        jnp.bfloat16
    )
    outgoing = jnp.concatenate([token_rows, scaled_rows], axis=1).reshape(
        experts, capacity, 2 * features
    )
    arrived = lax.all_to_all(outgoing, "expert", split_axis=0, concat_axis=0, tiled=True)
    hot_gate, hot_up, hot_down = (
        from_root(gate_weights, "expert", busiest),
        from_root(up_weights, "expert", busiest),
        from_root(down_weights, "expert", busiest),
    )
    own_rows = arrived[:, :cap_own].reshape(experts * cap_own, 2 * features)
    hot_rows = arrived[:, cap_own:].reshape(experts * cap_hot, 2 * features)
    own_out, own_terms = expert_pass(own_rows, gate_weights[0], up_weights[0], down_weights[0])
    hot_out, hot_terms = expert_pass(hot_rows, hot_gate[0], hot_up[0], hot_down[0])
    returning = jnp.concatenate(
        [own_out.reshape(experts, cap_own, features), hot_out.reshape(experts, cap_hot, features)],
        axis=1,
    )
    results = lax.all_to_all(returning, "expert", split_axis=0, concat_axis=0, tiled=True)
    flat_results = results.reshape(slot_count, features)
    layer_out = lax.dot_general(
        weighting, flat_results.astype(jnp.float32), (((0,), (0,)), ((), ())), precision=highest
    ).astype(jnp.bfloat16)
    picked = flat_results[slot_index].reshape(tok_rows, fanout, features).astype(jnp.float32)
    route_gradient = jnp.einsum(
        "tkd,td->tk", picked, cotangent.astype(jnp.float32), precision=highest
    )
    reduced = (
        lax.psum_scatter(
            own_terms[0].astype(jnp.bfloat16), "dp", scatter_dimension=0, tiled=True
        ).astype(jnp.float32),
        lax.psum_scatter(
            own_terms[1].astype(jnp.bfloat16), "dp", scatter_dimension=0, tiled=True
        ).astype(jnp.float32),
        lax.psum_scatter(
            own_terms[2].astype(jnp.bfloat16), "dp", scatter_dimension=0, tiled=True
        ).astype(jnp.float32),
        lax.psum_scatter(
            hot_terms[0].astype(jnp.bfloat16), "dp", scatter_dimension=0, tiled=True
        ).astype(jnp.float32),
        lax.psum_scatter(
            hot_terms[1].astype(jnp.bfloat16), "dp", scatter_dimension=0, tiled=True
        ).astype(jnp.float32),
        lax.psum_scatter(
            hot_terms[2].astype(jnp.bfloat16), "dp", scatter_dimension=0, tiled=True
        ).astype(jnp.float32),
    )
    hot_sums = lax.psum((reduced[3], reduced[4], reduced[5]), "expert")
    is_home = (my_index == busiest).astype(jnp.float32)
    gate_gradient = (reduced[0] + is_home * hot_sums[0])[None]
    up_gradient = (reduced[1] + is_home * hot_sums[1])[None]
    down_gradient = (reduced[2] + is_home * hot_sums[2])[None]
    return (layer_out, route_gradient, gate_gradient, up_gradient, down_gradient)


def solution(mesh):
    in_specs = (
        P(("dp", "expert"), None),
        P(("dp", "expert"), None),
        P(("dp", "expert"), None),
        P(("dp", "expert"), None),
        P("expert", None, None),
        P("expert", None, None),
        P("expert", None, None),
    )
    out_specs = (
        P(("dp", "expert"), None),
        P(("dp", "expert"), None),
        P("expert", "dp", None),
        P("expert", "dp", None),
        P("expert", "dp", None),
    )
    return jax.shard_map(
        on_device, mesh=mesh, in_specs=in_specs, out_specs=out_specs, check_vma=False
    )
```

profile of v0, /device:TPU:8, one launch (start us, length us, event | category | flops | bytes accessed | tf_op | source)
XLA Modules:
  0.0 732.3 jit_solution(15116745906409255275)
XLA Ops:
  7.2 0.8 copy.23
  10.2 0.8 copy.27
  13.2 1.2 convolution_convert_fusion.7
  15.2 1.6 reshape.343
  16.9 17.4 %all-to-all-start = ((bf16[64,5,2048]{2,1,0:T(8,128)(2,1)}), bf16[64,5,2048]{2,1,0:T(8,128)(2,1)S(1)}, u32[]{:S(2)}, u32[]{:S(2)}) async-start(bf16[64,5,2048]{2,1,0:T(8,128)(2,1)} %reshape.343), calls=%async_computation | async-start | bytes 4194304 | tf_op jit(solution)/shard_map/all_to_all | solution.py:77
  35.1 1.0 select_bitcast_fusion.1
  36.1 1.0 select_bitcast_fusion
  37.0 1.0 select_bitcast_fusion.2
  38.1 46.4 %all-to-all-done = bf16[64,5,2048]{2,1,0:T(8,128)(2,1)S(1)} async-done(((bf16[64,5,2048]{2,1,0:T(8,128)(2,1)}), bf16[64,5,2048]{2,1,0:T(8,128)(2,1)S(1)}, u32[]{:S(2)}, u32[]{:S(2)}) %all-to-all-start) | async-done | bytes 1310752 | tf_op jit(solution)/shard_map/all_to_all | solution.py:77
  85.2 156.3 %all-reduce.5.cloned.1.call-done = (bf16[1024,384]{1,0:T(8,128)(2,1)}, bf16[1024,384]{1,0:T(8,128)(2,1)}, bf16[384,1024]{1,0:T(8,128)(2,1)}) async-done(((bf16[1024,384]{1,0:T(8,128)(2,1)}, bf16[1024,384]{1,0:T(8,128)(2,1)}, bf16[384,1024]{1,0:T(8,128)(2,1)}), (bf16[1024,384]{1,0:T(8,128)(2,1)}, bf16[1024,384]{1,0:T(8,128)(2,1)}, bf16[384,1024]{1,0:T(8,128)(2,1)})) %all-reduce.5.cloned.1.call-update) | async-done | bytes 2359312 | tf_op jit(solution)/shard_map/psum | solution.py:11
  241.6 1.4 fusion.28
  243.0 1.5 fusion.21
  244.8 1.3 convolution_convert_fusion.4
  246.2 1.3 convolution_convert_fusion.2
  247.5 1.3 convolution_convert_fusion
  248.9 1.5 slice.35
  250.4 1.4 reshape.344
  253.4 1.5 convolution_convert_fusion.5
  254.9 1.4 convolution_convert_fusion.3
  258.0 1.5 pad_maximum_fusion.1
  259.5 10.3 %all-to-all-start.1 = ((bf16[64,5,1024]{2,1,0:T(8,128)(2,1)}), bf16[64,5,1024]{2,1,0:T(8,128)(2,1)S(1)}, u32[]{:S(2)}, u32[]{:S(2)}) async-start(bf16[64,5,1024]{2,1,0:T(8,128)(2,1)} %pad_maximum_fusion.1), calls=%async_computation.1 | async-start | bytes 2097152 | tf_op jit(solution)/shard_map/all_to_all | solution.py:91
  270.0 1.3 convolution_convert_fusion.1
  272.2 21.4 %all-to-all-done.1 = bf16[64,5,1024]{2,1,0:T(8,128)(2,1)S(1)} async-done(((bf16[64,5,1024]{2,1,0:T(8,128)(2,1)}), bf16[64,5,1024]{2,1,0:T(8,128)(2,1)S(1)}, u32[]{:S(2)}, u32[]{:S(2)}) %all-to-all-start.1) | async-done | bytes 655392 | tf_op jit(solution)/shard_map/all_to_all | solution.py:91
  293.9 1.2 gather_fusion
  296.1 1.1 convolution_convert_fusion.10
  297.2 13.6 %reduce-scatter.9.cloned.1.call-done = bf16[64,384]{1,0:T(8,128)(2,1)} async-done(((bf16[1024,384]{1,0:T(8,128)(2,1)}), bf16[64,384]{1,0:T(8,128)(2,1)}) %reduce-scatter.9.cloned.1.call-update) | async-done | bytes 49168 | tf_op jit(solution)/shard_map/reduce_scatter | solution.py:110
  310.8 65.1 %reduce-scatter.13.cloned.1.call-done = bf16[64,384]{1,0:T(8,128)(2,1)} async-done(((bf16[1024,384]{1,0:T(8,128)(2,1)}), bf16[64,384]{1,0:T(8,128)(2,1)}) %reduce-scatter.13.cloned.1.call-update) | async-done | bytes 49168 | tf_op jit(solution)/shard_map/reduce_scatter | solution.py:113
  375.9 64.6 %reduce-scatter.17.cloned.1.call-done = bf16[24,1024]{1,0:T(8,128)(2,1)} async-done(((bf16[384,1024]{1,0:T(8,128)(2,1)}), bf16[24,1024]{1,0:T(8,128)(2,1)}) %reduce-scatter.17.cloned.1.call-update) | async-done | bytes 49168 | tf_op jit(solution)/shard_map/reduce_scatter | solution.py:116
  440.5 280.6 %all-reduce.6 = (f32[64,384]{1,0:T(8,128)S(1)}, f32[64,384]{1,0:T(8,128)S(1)}, f32[24,1024]{1,0:T(8,128)S(1)}) all-reduce(bf16[64,384]{1,0:T(8,128)(2,1)} %reduce-scatter.9.cloned.1.call-done, bf16[64,384]{1,0:T(8,128)(2,1)} %reduce-scatter.13.cloned.1.call-done, ...), channel_id=1, replica_groups=mesh['dp'=16,'expert'=64] {'expert'}, use_global_device_ids=true, to_apply=%region_12.13 | all-reduce | flops 73728 | bytes 442368 | tf_op jit(solution)/shard_map/psum | solution.py:120
  721.1 1.5 add_bitcast_fusion.2
  722.5 1.5 add_bitcast_fusion.1
  724.0 1.5 add_bitcast_fusion
  (66 shorter events, 12.2 us)
Async XLA Ops:
  7.2 7.2 copy-start
  16.9 67.6 %all-to-all-start = ((bf16[64,5,2048]{2,1,0:T(8,128)(2,1)}), bf16[64,5,2048]{2,1,0:T(8,128)(2,1)S(1)}, u32[]{:S(2)}, u32[]{:S(2)}) async-start(bf16[64,5,2048]{2,1,0:T(8,128)(2,1)} %reshape.343), calls=%async_computation | async-start | bytes 4194304 | tf_op jit(solution)/shard_map/all_to_all | solution.py:77
  34.3 1.8 copy-start.1
  34.3 207.2 %all-reduce.5.cloned.1.call-start = ((), (), s32[]{:S(2)}) async-start(), calls=%async_computation.14 | async-start | bytes 4718592 | tf_op jit(solution)/shard_map/psum | solution.py:11
  35.1 2.0 copy-start.2
  38.1 272.7 %reduce-scatter.9.cloned.1.call-start = ((), (), s32[]{:S(2)}) async-start(), calls=%async_computation.9 | async-start | bytes 835584 | tf_op jit(solution)/shard_map/reduce_scatter | solution.py:110
  241.6 3.0 copy-start.6
  246.1 129.7 %reduce-scatter.13.cloned.1.call-start = ((), (), s32[]{:S(2)}) async-start(), calls=%async_computation.11 | async-start | bytes 835584 | tf_op jit(solution)/shard_map/reduce_scatter | solution.py:113
  247.5 193.0 %reduce-scatter.17.cloned.1.call-start = ((), (), s32[]{:S(2)}) async-start(), calls=%async_computation.13 | async-start | bytes 835584 | tf_op jit(solution)/shard_map/reduce_scatter | solution.py:116
  248.8 472.2 %reduce-scatter.7.cloned.1.call-start = ((), (), s32[]{:S(2)}) async-start(), calls=%async_computation.8 | async-start | bytes 835584 | tf_op jit(solution)/shard_map/reduce_scatter | solution.py:101
  250.4 1.4 copy-start.3
  251.8 1.1 copy-start.5
  254.9 467.7 %reduce-scatter.11.cloned.1.call-start = ((), (), s32[]{:S(2)}) async-start(), calls=%async_computation.10 | async-start | bytes 835584 | tf_op jit(solution)/shard_map/reduce_scatter | solution.py:104
  256.4 1.1 copy-start.4
  259.5 34.1 %all-to-all-start.1 = ((bf16[64,5,1024]{2,1,0:T(8,128)(2,1)}), bf16[64,5,1024]{2,1,0:T(8,128)(2,1)S(1)}, u32[]{:S(2)}, u32[]{:S(2)}) async-start(bf16[64,5,1024]{2,1,0:T(8,128)(2,1)} %pad_maximum_fusion.1), calls=%async_computation.1 | async-start | bytes 2097152 | tf_op jit(solution)/shard_map/all_to_all | solution.py:91
  269.8 454.2 %reduce-scatter.15.cloned.1.call-start = ((), (), s32[]{:S(2)}) async-start(), calls=%async_computation.12 | async-start | bytes 835584 | tf_op jit(solution)/shard_map/reduce_scatter | solution.py:107
Sparse Core Ops, SparseCore 0:
  38.7 202.7 all-reduce.4
  246.3 64.4 reduce-scatter.8
  314.5 61.2 reduce-scatter.12
  379.1 61.3 reduce-scatter.16
  444.1 62.0 reduce-scatter.6
  509.4 61.7 reduce-scatter.10
  575.0 61.3 reduce-scatter.14
where the time goes:
time: 733 us; the launch traced here: 732 us
  waiting for transfers between devices  368 us (50%)
  blocking collectives  281 us (38%)
  starting transfers between devices  28.2 us (4%)
  matrix products  16.7 us (2%)
  between operations  15.1 us (2%)
  other arithmetic  13.5 us (2%)
  local copies, waits for them, and re-layouts  10.7 us (1%)
    psum x1, blocking collectives, on_device(): hot_sums = lax.psum((reduced[3], reduced[4], reduced[5]), 'expert')  281 us
    psum x1, waiting for transfers between devices, from_root(): return lax.psum(kept, axis)  156 us
    reduce_scatter x1, waiting for transfers between devices, on_device(): lax.psum_scatter(hot_terms[1].astype(jnp.bfloat16), 'dp', scatter_dimensi...  65.1 us
    reduce_scatter x1, waiting for transfers between devices, on_device(): lax.psum_scatter(hot_terms[2].astype(jnp.bfloat16), 'dp', scatter_dimensi...  64.6 us
    all_to_all x1, waiting for transfers between devices, on_device(): lax.all_to_all(outgoing, 'expert', split_axis=0, concat_axis=0, tiled=True)  46.4 us
    all_to_all x1, waiting for transfers between devices, on_device(): lax.all_to_all(returning, 'expert', split_axis=0, concat_axis=0, tiled=True)  21.4 us
    all_to_all x1, starting transfers between devices, on_device(): lax.all_to_all(outgoing, 'expert', split_axis=0, concat_axis=0, tiled=True)  17.4 us
  transfers between devices with their start and end apart: 9, of which 6 were waited for; matrix products, arithmetic and copies ran while one was open for 3% of the time, Pallas kernels for 0%

commit v1 on v0

v1 whole, which is shorter than its diff:
```python
import jax
import jax.numpy as jnp
import numpy as np
from jax import lax
from jax.sharding import PartitionSpec as P

f32 = jnp.float32
bf16 = jnp.bfloat16
highest = lax.Precision.HIGHEST


def dot(lhs, rhs, lhs_dim, rhs_dim, precision=None):
    dims = (((lhs_dim,), (rhs_dim,)), ((), ()))
    return lax.dot_general(lhs, rhs, dims, precision=precision, preferred_element_type=f32)


def plane_exchange(blocks):
    return lax.all_to_all(blocks, "expert", split_axis=0, concat_axis=0, tiled=True)


def core_swap(block):
    size = lax.axis_size("dp")
    return lax.ppermute(block, "dp", [(i, i ^ 1) for i in range(size)])


def z_exchange(blocks):
    size = lax.axis_size("dp")
    groups = [list(range(core, size, 2)) for core in range(2)]
    return lax.all_to_all(
        blocks, "dp", split_axis=0, concat_axis=0, tiled=True, axis_index_groups=groups
    )


def pad_blocks(blocks, count):
    return jnp.pad(blocks, ((0, count - blocks.shape[0]),) + ((0, 0),) * (blocks.ndim - 1))


def deltas(gate_value, up_value, upstream):
    sigmoid = jax.nn.sigmoid(gate_value)
    active = gate_value * sigmoid
    hidden = (active * up_value).astype(bf16)
    gate_delta = (upstream * up_value * (sigmoid * (1.0 + gate_value * (1.0 - sigmoid)))).astype(bf16)
    up_delta = (upstream * active).astype(bf16)
    return hidden, gate_delta, up_delta


def routing(routed, weight, experts):
    rows = routed.shape[1]
    names = jnp.arange(experts, dtype=jnp.int32)
    hits = routed[None] == names[:, None, None]
    named = jnp.any(hits, axis=1)
    busiest = jnp.argmax(jnp.sum(named.astype(jnp.int32), axis=1)).astype(jnp.int32)
    table = jnp.sum(jnp.where(hits, weight[None], 0.0), axis=1)
    cold = named & (names != busiest)[:, None]
    before = jnp.arange(rows)[:, None] < jnp.arange(rows)[None, :]
    rank = dot(cold.astype(bf16), before.astype(bf16), 1, 0).astype(jnp.int32)
    slot = jnp.arange(8, dtype=jnp.int32) % 4
    place = cold[:, None, :] & (rank[:, None, :] == slot[None, :, None])
    return busiest, hits, table, place


def own_expert(arrived, gate, up, down):
    experts, _, features = arrived.shape
    hidden_units = gate.shape[1]
    rows = experts * 4
    inputs = arrived[:, :4].reshape(rows, features)
    scaled = arrived[:, 4:].reshape(rows, features)
    gate_value = dot(inputs, gate, 1, 0)
    up_value = dot(inputs, up, 1, 0)
    upstream = dot(scaled, down, 1, 1)
    hidden, gate_delta, up_delta = deltas(gate_value, up_value, upstream)
    output = dot(hidden, down, 1, 0).astype(bf16)
    output = output.reshape(experts, 4, 2, features // 2).transpose(0, 2, 1, 3)
    output = output.reshape(experts, 8, features // 2)
    size = lax.axis_size("dp")

    def stripes(matrix):
        height, width = matrix.shape
        striped = matrix.astype(bf16).reshape(size, height // size, width // 128, 128)
        return striped.transpose(0, 2, 1, 3).reshape(size, -1, 128)

    partial = jnp.concatenate(
        [
            stripes(dot(inputs, gate_delta, 0, 0)),
            stripes(dot(inputs, up_delta, 0, 0)),
            stripes(dot(hidden, scaled, 0, 0)),
        ],
        axis=1,
    )
    return output, partial


def hot_expert(gathered, sliced, core):
    features = sliced.shape[1]
    units = sliced.shape[0] // 3
    inputs = gathered[:, :features]
    scaled = gathered[:, features:]
    both = dot(sliced[: 2 * units], inputs, 1, 1)
    upstream = dot(sliced[2 * units :], scaled, 1, 1)
    hidden, gate_delta, up_delta = deltas(both[:units], both[units:], upstream)
    output = dot(hidden, sliced[2 * units :], 0, 0).astype(bf16)
    pair = jnp.concatenate([gate_delta, up_delta], axis=0)
    empty = jnp.zeros_like(pair)
    spread = jnp.concatenate(
        [
            jnp.where(core == 0, pair, empty),
            jnp.where(core == 1, pair, empty),
            jnp.zeros((128 - 4 * units, pair.shape[1]), bf16),
        ],
        axis=0,
    )
    pair_gradient = dot(inputs, spread, 0, 1).astype(bf16)
    down_gradient = dot(hidden, scaled, 1, 0).astype(bf16)
    return output, pair_gradient, down_gradient


def on_device(
    tokens, cotangent, route_weight, routed_experts, gate_weights, up_weights, down_weights
):
    experts = lax.axis_size("expert")
    size = lax.axis_size("dp")
    depth = size // 2
    mine = lax.axis_index("expert")
    shard = lax.axis_index("dp")
    core = shard % 2
    rows, features = tokens.shape
    half = features // 2
    gate, up, down = gate_weights[0], up_weights[0], down_weights[0]
    width = gate.shape[1]
    units = width // size

    busiest, hits, table, place = routing(routed_experts.T, route_weight.T, experts)
    hot_weight = lax.dynamic_index_in_dim(table, busiest, 0, keepdims=False)
    wide_cotangent = cotangent.astype(f32)
    hot_scaled = (hot_weight[:, None] * wide_cotangent).astype(bf16)
    gathered = lax.all_gather(
        jnp.concatenate([tokens, hot_scaled], axis=1), "dp", axis=0, tiled=True
    )

    is_token = (jnp.arange(8) < 4)[None, :, None]
    picks = jnp.concatenate([place & is_token, place & ~is_token], axis=2)
    slot_weight = jnp.sum(jnp.where(place, table[:, None, :], 0.0), axis=2)
    factor = jnp.where(jnp.arange(8)[None, :] < 4, 1.0, slot_weight).reshape(experts * 8, 1)
    stacked = jnp.concatenate([tokens, cotangent], axis=0)
    picked = dot(picks.astype(bf16).reshape(experts * 8, 2 * rows), stacked, 1, 0)
    outgoing = (picked * factor).astype(bf16).reshape(experts, 8, features)

    unit = shard * units + jnp.arange(units, dtype=jnp.int32)
    choose = (jnp.arange(width, dtype=jnp.int32)[None, :] == unit[:, None]).astype(bf16)
    pieces = jnp.concatenate(
        [dot(choose, gate, 1, 1), dot(choose, up, 1, 1), dot(choose, down, 1, 0)], axis=0
    ).astype(bf16)
    bands, spans = 3 * units // 8, features // 256
    pieces = pieces.reshape(bands, 8, spans, 256).transpose(0, 2, 1, 3)
    pieces = pad_blocks(pieces.reshape(bands * spans, 8, 256), experts)

    arrived = plane_exchange(jnp.concatenate([outgoing, pieces], axis=2))
    piece = lax.dynamic_index_in_dim(arrived[:, :, features:], busiest, 0, keepdims=True)
    sliced = plane_exchange(jnp.broadcast_to(piece, (experts, 8, 256)))
    sliced = sliced[: bands * spans].reshape(bands, spans, 8, 256).transpose(0, 2, 1, 3)
    sliced = sliced.reshape(3 * units, features)

    returning, partial = own_expert(arrived[:, :, :features], gate, up, down)
    own_sum = lax.psum_scatter(partial, "dp", scatter_dimension=0, tiled=True)[0].astype(f32)

    hot_part, pair_gradient, hot_down = hot_expert(gathered, sliced, core)
    strip = features // size
    pair_blocks = pair_gradient.reshape(depth, 2, 2, strip // 2, 128).transpose(0, 1, 3, 2, 4)
    both = jnp.concatenate(
        [
            hot_part.reshape(depth, 2, rows, features),
            pair_blocks.reshape(depth, 2, rows, 256),
        ],
        axis=3,
    )
    kept = jnp.where(core == 0, both[:, 0], both[:, 1])
    passed = jnp.where(core == 0, both[:, 1], both[:, 0])
    joined = (kept.astype(f32) + core_swap(passed).astype(f32)).astype(bf16)
    joined = z_exchange(joined)
    hot_out = jnp.sum(joined[:, :, :features].astype(f32), axis=0).astype(bf16)
    pair_tiles = joined[:, :, features:].reshape(depth, 4, 8, 2, 128).transpose(0, 3, 1, 2, 4)
    pair_tiles = pad_blocks(pair_tiles.reshape(depth * 8, 8, 128), experts)
    down_tiles = hot_down.reshape(units // 8, 8, features // 128, 128).transpose(0, 2, 1, 3)
    down_tiles = down_tiles.reshape(-1, 8, 128)
    down_count = down_tiles.shape[0]
    down_tiles = pad_blocks(down_tiles, experts)

    back = plane_exchange(jnp.concatenate([returning, pair_tiles, down_tiles], axis=2))
    hot_piece = jnp.sum(back[:, :, half:].astype(f32), axis=0).astype(bf16)
    hot_blocks = plane_exchange(jnp.broadcast_to(hot_piece[None], (experts, 8, 256)))

    results = back[:, :, :half].reshape(experts * 8, half)
    weighting = jnp.where(place, table[:, None, :], 0.0)
    halves = jnp.concatenate(
        [jnp.where(is_token, weighting, 0.0), jnp.where(is_token, 0.0, weighting)], axis=2
    ).reshape(experts * 8, 2 * rows)
    summed = dot(halves, results.astype(f32), 0, 0, highest)
    wide_hot = hot_out.astype(f32)
    layer_out = jnp.concatenate([summed[:rows], summed[rows:]], axis=1)
    layer_out = (layer_out + hot_weight[:, None] * wide_hot).astype(bf16)

    products = jnp.where(
        is_token,
        dot(results, cotangent[:, :half], 1, 1).reshape(experts, 8, rows),
        dot(results, cotangent[:, half:], 1, 1).reshape(experts, 8, rows),
    )
    by_expert = jnp.sum(jnp.where(place, products, 0.0), axis=1)
    hot_product = jnp.sum(wide_hot * wide_cotangent, axis=1)
    is_busiest = jnp.arange(experts, dtype=jnp.int32)[:, None] == busiest
    by_expert = by_expert + jnp.where(is_busiest, hot_product[None], 0.0)
    route_gradient = jnp.sum(jnp.where(hits, by_expert[:, None, :], 0.0), axis=0).T

    lane = np.arange(depth * 128)
    within = lane % 128
    column = (within % (2 * units)) // units * width
    column = column + (lane // 128 * 2 + within // (2 * units)) * units + within % units
    column = np.where(within < 4 * units, column, -1).astype(np.int32)
    spread = (jnp.asarray(column)[:, None] == jnp.arange(2 * width, dtype=jnp.int32)).astype(bf16)
    hot_pair = hot_blocks[: depth * 8, :, :128].reshape(depth, strip, 128).transpose(1, 0, 2)
    hot_pair = dot(hot_pair.reshape(strip, depth * 128), spread, 1, 0)
    hot_down = hot_blocks[:down_count, :, 128:].reshape(units // 8, features // 128, 8, 128)
    hot_down = hot_down.transpose(0, 2, 1, 3).reshape(units, features).astype(f32)

    def unstripe(block, height):
        return block.reshape(-1, height, 128).transpose(1, 0, 2).reshape(height, -1)

    count = strip * width // 128
    home = mine == busiest
    gate_gradient = unstripe(own_sum[:count], strip) + jnp.where(home, hot_pair[:, :width], 0.0)
    up_gradient = unstripe(own_sum[count : 2 * count], strip) + jnp.where(
        home, hot_pair[:, width:], 0.0
    )
    down_gradient = unstripe(own_sum[2 * count :], units) + jnp.where(home, hot_down, 0.0)
    return (layer_out, route_gradient, gate_gradient[None], up_gradient[None], down_gradient[None])


def solution(mesh):
    in_specs = (
        P(("dp", "expert"), None),
        P(("dp", "expert"), None),
        P(("dp", "expert"), None),
        P(("dp", "expert"), None),
        P("expert", None, None),
        P("expert", None, None),
        P("expert", None, None),
    )
    out_specs = (
        P(("dp", "expert"), None),
        P(("dp", "expert"), None),
        P("expert", "dp", None),
        P("expert", "dp", None),
        P("expert", "dp", None),
    )
    return jax.shard_map(
        on_device, mesh=mesh, in_specs=in_specs, out_specs=out_specs, check_vma=False
    )
```

time: 733 us -> 213 us (0.29)
  the two profiles are of different devices: /device:TPU:8 before, /device:TPU:1 now
where the time goes in v1:
time: 213 us; the launch traced here: 211 us
  waiting for transfers between devices  84.2 us (40%)
  starting transfers between devices  57.7 us (27%)
  matrix products  18.9 us (9%)
  between operations  17.4 us (8%)
  local copies, waits for them, and re-layouts  17.3 us (8%)
  other arithmetic  15.8 us (7%)
    all_to_all x4, waiting for transfers between devices, plane_exchange(): lax.all_to_all(blocks, 'expert', split_axis=0, concat_axis=0, tiled=True)  58.4 us
    all_to_all x4, starting transfers between devices, plane_exchange(): lax.all_to_all(blocks, 'expert', split_axis=0, concat_axis=0, tiled=True)  41.5 us
    dot_general x21, matrix products, dot(): lax.dot_general(lhs, rhs, dims, precision=precision, preferred_element_ty...  18.9 us
    all_to_all x1, waiting for transfers between devices, z_exchange(): lax.all_to_all(blocks, 'dp', split_axis=0, concat_axis=0, tiled=True, axi...  18.8 us
    all_to_all x1, starting transfers between devices, z_exchange(): lax.all_to_all(blocks, 'dp', split_axis=0, concat_axis=0, tiled=True, axi...  13.9 us
    all_gather x1, waiting for transfers between devices, on_device(): lax.all_gather(jnp.concatenate([tokens, hot_scaled], axis=1), 'dp', axis=...  6.99 us
    reshape x3, local copies, waits for them, and re-layouts, stripes(): matrix.astype(bf16).reshape(size, height // size, width // 128, 128)  5.84 us
  transfers between devices with their start and end apart: 8, of which 6 were waited for; matrix products, arithmetic and copies ran while one was open for 15% of the time, Pallas kernels for 0%

profile of v1, /device:TPU:1, one launch (start us, length us, event | category | flops | bytes accessed | tf_op | source)
XLA Modules:
  0.0 211.4 jit_solution(11633520575202396609)
XLA Ops:
  11.0 1.5 convolution_convert_fusion.9
  12.5 1.5 convolution_convert_fusion.8
  16.1 1.2 fusion.5
  17.2 14.0 %all-to-all-start = ((bf16[64,8,1280]{2,1,0:T(8,128)(2,1)}), bf16[64,8,1280]{2,1,0:T(8,128)(2,1)S(1)}, u32[]{:S(2)}, u32[]{:S(2)}) async-start(bf16[64,8,1280]{2,1,0:T(8,128)(2,1)} %fusion.5), calls=%async_computation | async-start | bytes 2621440 | tf_op jit(solution)/shard_map/all_to_all | solution.py:18
  34.8 25.5 %all-to-all-done = bf16[64,8,1280]{2,1,0:T(8,128)(2,1)S(1)} async-done(((bf16[64,8,1280]{2,1,0:T(8,128)(2,1)}), bf16[64,8,1280]{2,1,0:T(8,128)(2,1)S(1)}, u32[]{:S(2)}, u32[]{:S(2)}) %all-to-all-start) | async-done | bytes 1310752 | tf_op jit(solution)/shard_map/all_to_all | solution.py:18
  61.1 11.6 %all-to-all-start.1 = ((bf16[64,8,256]{2,1,0:T(8,128)(2,1)}), bf16[64,8,256]{2,1,0:T(8,128)(2,1)}, u32[]{:S(2)}, u32[]{:S(2)}) async-start(bf16[64,8,256]{2,1,0:T(8,128)(2,1)} %broadcast_in_dim.168), calls=%async_computation.1 | async-start | bytes 524288 | tf_op jit(solution)/shard_map/all_to_all | solution.py:18
  72.8 1.3 fusion.78
  74.1 1.2 reshape.262
  75.7 2.5 %multiply_convert_fusion.3 = (bf16[256,384]{1,0:T(8,128)(2,1)S(1)}, f32[256,384]{1,0:T(8,128)}) fusion(f32[256,384]{1,0:T(8,128)S(1)} %fusion.24, bf16[256,1024]{1,0:T(8,128)(2,1)S(1)} %reshape.262, bf16[1,1024,384]{2,1,0:T(8,128)(2,1)} %param.13), kind=kOutput, calls=%fused_computation.61 | convolution fusion | flops 201916416 | bytes 2293760 | tf_op jit(solution)/shard_map/dot_general | solution.py:14
  79.0 1.0 copy.107
  80.5 4.6 %all-to-all-done.1 = bf16[64,8,256]{2,1,0:T(8,128)(2,1)} async-done(((bf16[64,8,256]{2,1,0:T(8,128)(2,1)}), bf16[64,8,256]{2,1,0:T(8,128)(2,1)}, u32[]{:S(2)}, u32[]{:S(2)}) %all-to-all-start.1) | async-done | bytes 262176 | tf_op jit(solution)/shard_map/all_to_all | solution.py:18
  85.0 0.9 slice.127
  86.0 7.0 %all-gather.2.cloned.1.call-done = bf16[512,2048]{1,0:T(8,128)(2,1)} async-done(((bf16[32,2048]{1,0:T(8,128)(2,1)}), bf16[512,2048]{1,0:T(8,128)(2,1)}) %all-gather.2.cloned.1.call-update) | async-done | bytes 2097168 | tf_op jit(solution)/shard_map/all_gather | solution.py:136
  93.0 1.8 fusion.14
  94.8 1.6 multiply_convert_fusion.7
  97.5 1.1 fusion.27
  98.6 2.2 %collective-permute-start = (bf16[8,32,1280]{2,1,0:T(8,128)(2,1)}, bf16[8,32,1280]{2,1,0:T(8,128)(2,1)}, u32[]{:S(2)}, u32[]{:S(2)}) collective-permute-start(bf16[8,32,1280]{2,1,0:T(8,128)(2,1)} %fusion.27), channel_id=1, source_target_pairs={{0,64},{64,0},{128,192},{192,128},{256,320},{320,256},{384,448},{4... | collective-permute-start | bytes 1966088 | tf_op jit(solution)/shard_map/ppermute | solution.py:23
  100.8 1.4 convolution_convert_fusion.2
  102.2 2.4 %reshape.276 = bf16[16,64,3,128]{3,2,1,0:T(4,128)(2,1)S(1)} reshape(bf16[1024,384]{1,0:T(8,128)(2,1)} %convolution_convert_fusion.2) | data formatting | bytes 1572864 | tf_op jit(solution)/shard_map/reshape | solution.py:79
  104.7 1.1 copy.106
  106.3 1.5 convolution_convert_fusion.3
  107.8 2.4 %reshape.274 = bf16[16,64,3,128]{3,2,1,0:T(4,128)(2,1)S(1)} reshape(bf16[1024,384]{1,0:T(8,128)(2,1)} %convolution_convert_fusion.3) | data formatting | bytes 1572864 | tf_op jit(solution)/shard_map/reshape | solution.py:79
  111.6 1.6 pad_maximum_fusion
  113.2 2.3 %fusion.6 = bf16[8,32,1280]{2,1,0:T(8,128)(2,1)} fusion(bf16[8,32,1280]{2,1,0:T(8,128)(2,1)} %collective-permute-done, pred[]{:T(512)S(6)} %eq.104, bf16[8,2,32,256]{3,2,1,0:T(8,128)(2,1)S(1)} %bitcast.169, bf16[8,2,32,1024]{3,2,1,0:T(8,128)(2,1)S(1)} %bitcast.161), kind=kLoop, calls=%fused_computation.18 | loop fusion | flops 4259840 | bytes 2621441 | tf_op jit(solution)/shard_map/convert_element_type | solution.py:178
  115.5 13.9 %all-to-all-start.2 = ((bf16[8,32,1280]{2,1,0:T(8,128)(2,1)}), bf16[8,32,1280]{2,1,0:T(8,128)(2,1)S(1)}, u32[]{:S(2)}, u32[]{:S(2)}) async-start(bf16[8,32,1280]{2,1,0:T(8,128)(2,1)} %fusion.6), calls=%async_computation.2 | async-start | bytes 1310720 | tf_op jit(solution)/shard_map/all_to_all | solution.py:29
  130.6 1.5 convolution_convert_fusion.6
  132.1 18.8 %all-to-all-done.2 = bf16[8,32,1280]{2,1,0:T(8,128)(2,1)S(1)} async-done(((bf16[8,32,1280]{2,1,0:T(8,128)(2,1)}), bf16[8,32,1280]{2,1,0:T(8,128)(2,1)S(1)}, u32[]{:S(2)}, u32[]{:S(2)}) %all-to-all-start.2) | async-done | bytes 655392 | tf_op jit(solution)/shard_map/all_to_all | solution.py:29
  150.9 0.9 fusion.16
  151.8 6.4 %all-to-all-start.3 = ((bf16[64,8,768]{2,1,0:T(8,128)(2,1)}), bf16[64,8,768]{2,1,0:T(8,128)(2,1)S(1)}, u32[]{:S(2)}, u32[]{:S(2)}) async-start(bf16[64,8,768]{2,1,0:T(8,128)(2,1)} %fusion.16), calls=%async_computation.3 | async-start | bytes 1572864 | tf_op jit(solution)/shard_map/all_to_all | solution.py:18
  159.7 19.6 %all-to-all-done.3 = bf16[64,8,768]{2,1,0:T(8,128)(2,1)S(1)} async-done(((bf16[64,8,768]{2,1,0:T(8,128)(2,1)}), bf16[64,8,768]{2,1,0:T(8,128)(2,1)S(1)}, u32[]{:S(2)}, u32[]{:S(2)}) %all-to-all-start.3) | async-done | bytes 786464 | tf_op jit(solution)/shard_map/all_to_all | solution.py:18
  180.1 9.4 %all-to-all-start.4 = ((bf16[64,8,256]{2,1,0:T(8,128)(2,1)}), bf16[64,8,256]{2,1,0:T(8,128)(2,1)S(1)}, u32[]{:S(2)}, u32[]{:S(2)}) async-start(bf16[64,8,256]{2,1,0:T(8,128)(2,1)} %broadcast_in_dim.175), calls=%async_computation.5 | async-start | bytes 524288 | tf_op jit(solution)/shard_map/all_to_all | solution.py:18
  193.6 8.7 %all-to-all-done.4 = bf16[64,8,256]{2,1,0:T(8,128)(2,1)S(1)} async-done(((bf16[64,8,256]{2,1,0:T(8,128)(2,1)}), bf16[64,8,256]{2,1,0:T(8,128)(2,1)S(1)}, u32[]{:S(2)}, u32[]{:S(2)}) %all-to-all-start.4) | async-done | bytes 262176 | tf_op jit(solution)/shard_map/all_to_all | solution.py:18
  (137 shorter events, 21.5 us)
Async XLA Ops:
  7.2 6.8 %copy-start = (bf16[1,384,1024]{2,1,0:T(8,128)(2,1)S(1)}, bf16[1,384,1024]{2,1,0:T(8,128)(2,1)}, u32[]{:S(2)}) copy-start(bf16[1,384,1024]{2,1,0:T(8,128)(2,1)} %param.14) | copy-start | bytes 2359300
  7.2 7.9 %copy-start.24 = (pred[8]{0:T(512)(128)(4,1)}, pred[8]{0:T(512)(128)(4,1)S(1)}, u32[]{:S(2)}) copy-start(pred[8]{0:T(512)(128)(4,1)S(1)} %iota_compare_fusion.13) | copy-start | bytes 28
  7.2 7.9 %copy-start.22 = (s32[8]{0:T(128)}, s32[8]{0:T(128)S(1)}, u32[]{:S(2)}) copy-start(s32[8]{0:T(128)S(1)} %and_select_fusion) | copy-start | bytes 100
  9.7 5.3 %copy-start.19 = (s32[64,32]{0,1:T(8,128)}, s32[64,32]{0,1:T(8,128)S(1)}, u32[]{:S(2)}) copy-start(s32[64,32]{0,1:T(8,128)S(1)} %convolution_convert_fusion.10) | copy-start | bytes 24580
  11.0 4.6 %copy-start.10 = (bf16[32,1024]{1,0:T(8,128)(2,1)S(1)}, bf16[32,1024]{1,0:T(8,128)(2,1)}, u32[]{:S(2)}) copy-start(bf16[32,1024]{1,0:T(8,128)(2,1)} %param.9) | copy-start | bytes 196612
  11.0 4.6 %copy-start.18 = (bf16[32,1024]{1,0:T(8,128)(2,1)S(1)}, bf16[32,1024]{1,0:T(8,128)(2,1)}, u32[]{:S(2)}) copy-start(bf16[32,1024]{1,0:T(8,128)(2,1)} %param.8) | copy-start | bytes 196612
  17.2 43.1 %all-to-all-start = ((bf16[64,8,1280]{2,1,0:T(8,128)(2,1)}), bf16[64,8,1280]{2,1,0:T(8,128)(2,1)S(1)}, u32[]{:S(2)}, u32[]{:S(2)}) async-start(bf16[64,8,1280]{2,1,0:T(8,128)(2,1)} %fusion.5), calls=%async_computation | async-start | bytes 2621440 | tf_op jit(solution)/shard_map/all_to_all | solution.py:18
  31.3 61.7 %all-gather.2.cloned.1.call-start = ((), (), s32[]{:S(2)}) async-start(), calls=%async_computation.6 | async-start | bytes 2228224 | tf_op jit(solution)/shard_map/all_gather | solution.py:136
  61.1 23.9 %all-to-all-start.1 = ((bf16[64,8,256]{2,1,0:T(8,128)(2,1)}), bf16[64,8,256]{2,1,0:T(8,128)(2,1)}, u32[]{:S(2)}, u32[]{:S(2)}) async-start(bf16[64,8,256]{2,1,0:T(8,128)(2,1)} %broadcast_in_dim.168), calls=%async_computation.1 | async-start | bytes 524288 | tf_op jit(solution)/shard_map/all_to_all | solution.py:18
  72.7 2.6 %copy-start.3 = (bf16[1,1024,384]{2,1,0:T(8,128)(2,1)S(1)}, bf16[1,1024,384]{2,1,0:T(8,128)(2,1)}, u32[]{:S(2)}) copy-start(bf16[1,1024,384]{2,1,0:T(8,128)(2,1)} %param.12) | copy-start | bytes 2359300
  72.7 119.9 %reduce-scatter.2.cloned.1.call-start = ((), (), s32[]{:S(2)}) async-start(), calls=%async_computation.7 | async-start | bytes 2506752 | tf_op jit(solution)/shard_map/reduce_scatter | solution.py:164
  75.3 25.5 %copy-start.5 = (bf16[256,1024]{1,0:T(8,128)(2,1)}, bf16[256,1024]{1,0:T(8,128)(2,1)S(1)}, u32[]{:S(2)}) copy-start(bf16[256,1024]{1,0:T(8,128)(2,1)S(1)} %reshape.262) | copy-start | bytes 1572868
  75.7 2.5 %copy-start.13 = (f32[256,384]{1,0:T(8,128)}, f32[256,384]{1,0:T(8,128)S(1)}, u32[]{:S(2)}) copy-start(f32[256,384]{1,0:T(8,128)S(1)} %fusion.24) | copy-start | bytes 1179652
  75.7 2.5 %copy-start.7 = (bf16[64,4,1024]{2,1,0:T(4,128)(2,1)S(1)}, bf16[64,4,1024]{2,1,0:T(4,128)(2,1)}, u32[]{:S(2)}) copy-start(bf16[64,4,1024]{2,1,0:T(4,128)(2,1)} %get-tuple-element.7) | copy-start | bytes 1572868
  80.4 20.4 %copy-start.16 = (f32[256,384]{1,0:T(8,128)}, f32[256,384]{1,0:T(8,128)S(1)}, u32[]{:S(2)}) copy-start(f32[256,384]{1,0:T(8,128)S(1)} %fusion.17) | copy-start | bytes 1179652
  86.0 10.5 %copy-start.26 = (bf16[128]{0:T(256)(128)(2,1)S(1)}, bf16[128]{0:T(256)(128)(2,1)}, u32[]{:S(2)}) copy-start(bf16[128]{0:T(256)(128)(2,1)} %pad.22.clone) | copy-start | bytes 772
  93.0 3.5 %copy-start.4 = (bf16[512,2048]{1,0:T(8,128)(2,1)S(1)}, bf16[512,2048]{1,0:T(8,128)(2,1)}, u32[]{:S(2)}) copy-start(bf16[512,2048]{1,0:T(8,128)(2,1)} %all-gather.2.cloned.1.call-done) | copy-start | bytes 6291460
  97.0 3.8 %copy-start.14 = (f32[256,384]{1,0:T(8,128)S(1)}, f32[256,384]{1,0:T(8,128)}, u32[]{:S(2)}) copy-start(f32[256,384]{1,0:T(8,128)} %copy-done.13) | copy-start | bytes 1179652
  98.6 14.6 %collective-permute-start = (bf16[8,32,1280]{2,1,0:T(8,128)(2,1)}, bf16[8,32,1280]{2,1,0:T(8,128)(2,1)}, u32[]{:S(2)}, u32[]{:S(2)}) collective-permute-start(bf16[8,32,1280]{2,1,0:T(8,128)(2,1)} %fusion.27), channel_id=1, source_target_pairs={{0,64},{64,0},{128,192},{192,128},{256,320},{320,256},{384,448},{4... | collective-permute-start | bytes 1966088 | tf_op jit(solution)/shard_map/ppermute | solution.py:23
  104.7 1.5 copy-start.17
  104.7 1.6 copy-start.28
  113.2 16.2 %copy-start.9 = (bf16[256,384]{1,0:T(8,128)(2,1)S(1)}, bf16[256,384]{1,0:T(8,128)(2,1)}, u32[]{:S(2)}) copy-start(bf16[256,384]{1,0:T(8,128)(2,1)} %copy-done.8) | copy-start | bytes 589828
  115.5 35.4 %all-to-all-start.2 = ((bf16[8,32,1280]{2,1,0:T(8,128)(2,1)}), bf16[8,32,1280]{2,1,0:T(8,128)(2,1)S(1)}, u32[]{:S(2)}, u32[]{:S(2)}) async-start(bf16[8,32,1280]{2,1,0:T(8,128)(2,1)} %fusion.6), calls=%async_computation.2 | async-start | bytes 1310720 | tf_op jit(solution)/shard_map/all_to_all | solution.py:29
  151.8 27.5 %all-to-all-start.3 = ((bf16[64,8,768]{2,1,0:T(8,128)(2,1)}), bf16[64,8,768]{2,1,0:T(8,128)(2,1)S(1)}, u32[]{:S(2)}, u32[]{:S(2)}) async-start(bf16[64,8,768]{2,1,0:T(8,128)(2,1)} %fusion.16), calls=%async_computation.3 | async-start | bytes 1572864 | tf_op jit(solution)/shard_map/all_to_all | solution.py:18
  158.3 31.3 %copy-start.11 = (f32[64,8,32]{0,2,1:T(8,128)S(1)}, f32[64,8,32]{0,2,1:T(8,128)}, u32[]{:S(2)}) copy-start(f32[64,8,32]{0,2,1:T(8,128)} %get-tuple-element.25) | copy-start | bytes 196612
  158.3 31.3 %copy-start.12 = (f32[64,8,32]{0,2,1:T(8,128)S(1)}, f32[64,8,32]{0,2,1:T(8,128)}, u32[]{:S(2)}) copy-start(f32[64,8,32]{0,2,1:T(8,128)} %get-tuple-element.26) | copy-start | bytes 196612
  180.1 10.4 %copy-start.20 = (s32[64,32]{0,1:T(8,128)S(1)}, s32[64,32]{0,1:T(8,128)}, u32[]{:S(2)}) copy-start(s32[64,32]{0,1:T(8,128)} %copy-done.19) | copy-start | bytes 24580
  180.1 10.4 %copy-start.23 = (s32[8]{0:T(128)S(1)}, s32[8]{0:T(128)}, u32[]{:S(2)}) copy-start(s32[8]{0:T(128)} %copy-done.22) | copy-start | bytes 100
  180.1 10.4 %copy-start.25 = (pred[8]{0:T(512)(128)(4,1)S(1)}, pred[8]{0:T(512)(128)(4,1)}, u32[]{:S(2)}) copy-start(pred[8]{0:T(512)(128)(4,1)} %copy-done.24) | copy-start | bytes 28
  180.1 22.2 %all-to-all-start.4 = ((bf16[64,8,256]{2,1,0:T(8,128)(2,1)}), bf16[64,8,256]{2,1,0:T(8,128)(2,1)S(1)}, u32[]{:S(2)}, u32[]{:S(2)}) async-start(bf16[64,8,256]{2,1,0:T(8,128)(2,1)} %broadcast_in_dim.175), calls=%async_computation.5 | async-start | bytes 524288 | tf_op jit(solution)/shard_map/all_to_all | solution.py:18
  189.6 2.3 %copy-start.21 = (s32[32,8]{0,1:T(8,128)S(1)}, s32[32,8]{0,1:T(8,128)}, u32[]{:S(2)}) copy-start(s32[32,8]{0,1:T(8,128)} %param.11) | copy-start | bytes 3076
  190.6 12.5 %copy-start.27 = (s32[1024]{0:T(1024)S(1)}, s32[1024]{0:T(1024)}, u32[]{:S(2)}) copy-start(s32[1024]{0:T(1024)} %constant.73.clone) | copy-start | bytes 12292
  (5 other events, 5.5 us)
Sparse Core Ops, SparseCore 0:
  34.8 58.1 all-gather.1
  113.3 71.7 reduce-scatter.1

commit v2 on v1

v2 whole, which is shorter than its diff:
```python
import functools

import jax
import jax.numpy as jnp
from jax import lax
from jax.experimental import pallas as pl
from jax.experimental.pallas import tpu as pltpu
from jax.sharding import PartitionSpec as P

f32 = jnp.float32
bf16 = jnp.bfloat16
highest = lax.Precision.HIGHEST


def dot(lhs, rhs, lhs_dim, rhs_dim, precision=None):
    dims = (((lhs_dim,), (rhs_dim,)), ((), ()))
    return lax.dot_general(lhs, rhs, dims, precision=precision, preferred_element_type=f32)


def plane_exchange(blocks):
    return lax.all_to_all(blocks, "expert", split_axis=0, concat_axis=0, tiled=True)


def core_swap(block):
    size = lax.axis_size("dp")
    return lax.ppermute(block, "dp", [(i, i ^ 1) for i in range(size)])


def z_exchange(blocks):
    size = lax.axis_size("dp")
    groups = [list(range(core, size, 2)) for core in range(2)]
    return lax.all_to_all(
        blocks, "dp", split_axis=0, concat_axis=0, tiled=True, axis_index_groups=groups
    )


def z_reduce_scatter(blocks):
    size = lax.axis_size("dp")
    groups = [list(range(core, size, 2)) for core in range(2)]
    return lax.psum_scatter(
        blocks, "dp", scatter_dimension=0, tiled=True, axis_index_groups=groups
    )


def add(one, other):
    return (one.astype(f32) + other.astype(f32)).astype(bf16)


def pad_blocks(blocks, count):
    return jnp.pad(blocks, ((0, count - blocks.shape[0]),) + ((0, 0),) * (blocks.ndim - 1))


def routing(routed, weight, experts):
    rows = routed.shape[1]
    names = jnp.arange(experts, dtype=jnp.int32)
    hits = routed[None] == names[:, None, None]
    named = jnp.any(hits, axis=1)
    busiest = jnp.argmax(jnp.sum(named.astype(jnp.int32), axis=1)).astype(jnp.int32)
    table = jnp.sum(jnp.where(hits, weight[None], 0.0), axis=1)
    cold = named & (names != busiest)[:, None]
    before = jnp.arange(rows)[:, None] < jnp.arange(rows)[None, :]
    rank = dot(cold.astype(bf16), before.astype(bf16), 1, 0).astype(jnp.int32)
    slot = jnp.arange(8, dtype=jnp.int32) % 4
    place = cold[:, None, :] & (rank[:, None, :] == slot[None, :, None])
    return busiest, hits, table, place


def in_vmem(count):
    return [pl.BlockSpec(memory_space=pltpu.VMEM)] * count


def own_kernel(
    core_ref, rows_ref, gate_ref, up_ref, down_ref, out_ref, kept_ref, passed_ref, grads, down_grads
):
    features, width = gate_ref.shape
    depth = kept_ref.shape[0]
    half = features // 2
    strip = features // (2 * depth)
    units = width // (2 * depth)
    lanes = width // 128
    core = core_ref[0]
    sides = ((kept_ref, core), (passed_ref, 1 - core))
    rows = rows_ref[:, :features]
    down = down_ref[...]
    gate_value = dot(rows, gate_ref[...], 1, 0)
    up_value = dot(rows, up_ref[...], 1, 0)
    upstream = dot(rows, down, 1, 1)
    count = gate_value.shape[0]
    upstream = pltpu.roll(upstream, count - 4, 0)
    sigmoid = jax.nn.sigmoid(gate_value)
    active = gate_value * sigmoid
    slope = sigmoid * (1.0 + gate_value * (1.0 - sigmoid))
    is_token = lax.broadcasted_iota(jnp.int32, (count, width), 0) % 8 < 4
    hidden = jnp.where(is_token, active * up_value, 0.0)
    shifted = pltpu.roll(hidden, 4, 0).astype(bf16)
    hidden = hidden.astype(bf16)
    gate_delta = jnp.where(is_token, upstream * up_value * slope, 0.0).astype(bf16)
    up_delta = jnp.where(is_token, upstream * active, 0.0).astype(bf16)
    for index, delta in enumerate((gate_delta, up_delta)):
        grads[...] = dot(rows, delta, 0, 0)
        for z in range(depth):
            for ref, side in sides:
                start = pl.multiple_of((2 * z + side) * strip, strip)
                block = grads[pl.ds(start, strip), :].astype(bf16)
                for lane in range(lanes):
                    at = (index * lanes + lane) * strip
                    ref[z, at : at + strip, :] = block[:, lane * 128 : lane * 128 + 128]
    down_grads[...] = dot(shifted, rows, 0, 0)
    base = 2 * lanes * strip
    for z in range(depth):
        for ref, side in sides:
            start = pl.multiple_of((2 * z + side) * units, 8)
            block = down_grads[pl.ds(start, units), :]
            for lane in range(0, features // 128, 2):
                at = base + lane * units
                pair = [block[:, i * 128 : i * 128 + 128] for i in (lane, lane + 1)]
                ref[z, at : at + 2 * units, :] = jnp.concatenate(pair, axis=0).astype(bf16)
    output = dot(hidden, down[:, :half], 1, 0) + dot(shifted, down[:, half:], 1, 0)
    out_ref[...] = output.astype(bf16)


def own_expert(core, rows, gate, up, down, depth):
    features, width = gate.shape
    side = jax.ShapeDtypeStruct((depth, 3 * features * width // (2 * depth) // 128, 128), bf16)
    return pl.pallas_call(
        own_kernel,
        out_shape=(jax.ShapeDtypeStruct((rows.shape[0], features // 2), bf16), side, side),
        in_specs=[pl.BlockSpec(memory_space=pltpu.SMEM)] + in_vmem(4),
        out_specs=tuple(in_vmem(3)),
        scratch_shapes=[pltpu.VMEM((features, width), f32), pltpu.VMEM((width, features), f32)],
        compiler_params=pltpu.CompilerParams(vmem_limit_bytes=48 * 2**20),
    )(core, rows, gate, up, down)


def hot_kernel(units, core_ref, rows_ref, blocks_ref, kept_ref, passed_ref, grads_ref, part):
    features = part.shape[1]
    depth = kept_ref.shape[0]
    group = part.shape[0] // (2 * depth)
    spans = features // 256
    height = -(-3 * units // 16) * 16
    core = core_ref[0]
    inputs = rows_ref[:, :features]
    scaled = rows_ref[:, features:]
    sliced = jnp.concatenate(
        [blocks_ref[span * height : span * height + height, :] for span in range(spans)], axis=1
    )
    down = sliced[2 * units :]
    both = dot(sliced[: 2 * units], inputs, 1, 1)
    upstream = dot(down, scaled, 1, 1)[:units]
    gate_value, up_value = both[:units], both[units:]
    sigmoid = jax.nn.sigmoid(gate_value)
    active = gate_value * sigmoid
    slope = sigmoid * (1.0 + gate_value * (1.0 - sigmoid))
    pair = jnp.concatenate([upstream * up_value * slope, upstream * active], axis=0).astype(bf16)
    spare = jnp.zeros((height - 3 * units, gate_value.shape[1]), f32)
    hidden = active * up_value
    if spare.shape[0]:
        hidden = jnp.concatenate([hidden, spare], axis=0)
    hidden = hidden.astype(bf16)
    part[...] = dot(hidden, down, 0, 0)
    for z in range(depth):
        for ref, side in ((kept_ref, core), (passed_ref, 1 - core)):
            start = pl.multiple_of((2 * z + side) * group, group)
            block = part[pl.ds(start, group), :].astype(bf16)
            for lane in range(features // 128):
                ref[z, lane * group : lane * group + group, :] = block[
                    :, lane * 128 : lane * 128 + 128
                ]
    grads = jnp.concatenate([dot(pair, inputs, 1, 0), dot(hidden, scaled, 1, 0)], axis=0)
    grads = grads.astype(bf16)
    for span in range(spans):
        grads_ref[span * height : span * height + height, :] = grads[
            :, span * 256 : span * 256 + 256
        ]
    used = spans * height
    grads_ref[used:, :] = jnp.zeros((grads_ref.shape[0] - used, 256), bf16)


def hot_expert(core, gathered, blocks, units, depth):
    total, features = gathered.shape[0], gathered.shape[1] // 2
    side = jax.ShapeDtypeStruct((depth, total // (2 * depth) * features // 128, 128), bf16)
    return pl.pallas_call(
        functools.partial(hot_kernel, units),
        out_shape=(side, side, jax.ShapeDtypeStruct(blocks.shape, bf16)),
        in_specs=[pl.BlockSpec(memory_space=pltpu.SMEM)] + in_vmem(2),
        out_specs=tuple(in_vmem(3)),
        scratch_shapes=[pltpu.VMEM((total, features), f32)],
        compiler_params=pltpu.CompilerParams(vmem_limit_bytes=48 * 2**20),
    )(core, gathered, blocks)


def on_device(
    tokens, cotangent, route_weight, routed_experts, gate_weights, up_weights, down_weights
):
    experts = lax.axis_size("expert")
    size = lax.axis_size("dp")
    depth = size // 2
    mine = lax.axis_index("expert")
    shard = lax.axis_index("dp")
    core = shard % 2
    core_word = core.astype(jnp.int32).reshape(1)
    rows, features = tokens.shape
    half = features // 2
    gate, up, down = gate_weights[0], up_weights[0], down_weights[0]
    width = gate.shape[1]
    units = width // size
    strip = features // size

    busiest, hits, table, place = routing(routed_experts.T, route_weight.T, experts)
    hot_weight = lax.dynamic_index_in_dim(table, busiest, 0, keepdims=False)
    wide_cotangent = cotangent.astype(f32)
    hot_scaled = (hot_weight[:, None] * wide_cotangent).astype(bf16)
    gathered = lax.all_gather(
        jnp.concatenate([tokens, hot_scaled], axis=1), "dp", axis=0, tiled=True
    )

    is_token = (jnp.arange(8) < 4)[None, :, None]
    picks = jnp.concatenate([place & is_token, place & ~is_token], axis=2)
    slot_weight = jnp.sum(jnp.where(place, table[:, None, :], 0.0), axis=2)
    factor = jnp.where(jnp.arange(8)[None, :] < 4, 1.0, slot_weight).reshape(experts * 8, 1)
    stacked = jnp.concatenate([tokens, cotangent], axis=0)
    picked = dot(picks.astype(bf16).reshape(experts * 8, 2 * rows), stacked, 1, 0)
    outgoing = (picked * factor).astype(bf16).reshape(experts, 8, features)

    unit = shard * units + jnp.arange(units, dtype=jnp.int32)
    choose = (jnp.arange(width, dtype=jnp.int32)[None, :] == unit[:, None]).astype(bf16)
    height, spans = -(-3 * units // 16) * 16, features // 256
    pieces = jnp.concatenate(
        [
            dot(choose, gate, 1, 1).astype(bf16),
            dot(choose, up, 1, 1).astype(bf16),
            dot(choose, down, 1, 0).astype(bf16),
            jnp.zeros((height - 3 * units, features), bf16),
        ],
        axis=0,
    )
    pieces = pieces.reshape(height // 8, 8, spans, 256).transpose(2, 0, 1, 3)
    pieces = pad_blocks(pieces.reshape(height // 8 * spans, 8, 256), experts)

    arrived = plane_exchange(jnp.concatenate([outgoing, pieces], axis=2))
    piece = lax.dynamic_index_in_dim(arrived[:, :, features:], busiest, 0, keepdims=True)
    blocks = plane_exchange(jnp.broadcast_to(piece, (experts, 8, 256)))

    returning, own_kept, own_passed = own_expert(
        core_word, arrived.reshape(experts * 8, features + 256), gate, up, down, depth
    )
    own_came = core_swap(own_passed)
    hot_kept, hot_passed, hot_grads = hot_expert(
        core_word, gathered, blocks.reshape(experts * 8, 256), units, depth
    )
    hot_came = core_swap(hot_passed)
    joined = jnp.concatenate([add(own_kept, own_came), add(hot_kept, hot_came)], axis=1)
    summed = z_reduce_scatter(joined)[0]
    own_rows = own_kept.shape[1]
    own_sum = summed[:own_rows].astype(f32)
    hot_out = summed[own_rows:].reshape(features // 128, rows, 128)
    hot_out = hot_out.transpose(1, 0, 2).reshape(rows, features)

    back = plane_exchange(
        jnp.concatenate(
            [returning.reshape(experts, 8, half), hot_grads.reshape(experts, 8, 256)], axis=2
        )
    )
    hot_piece = jnp.sum(back[:, :, half:].astype(f32), axis=0).astype(bf16)
    hot_blocks = plane_exchange(jnp.broadcast_to(hot_piece[None], (experts, 8, 256)))
    hot_rows = hot_blocks.reshape(experts * 8, 256)[: spans * height]
    hot_rows = hot_rows.reshape(spans, height, 256).transpose(1, 0, 2).reshape(height, features)
    hot_down = hot_rows[2 * units : 3 * units].astype(f32)
    pair = hot_rows[: 2 * units].reshape(2 * units, depth, 2, strip).transpose(1, 2, 0, 3)
    pair_kept = jnp.where(core == 0, pair[:, 0], pair[:, 1])
    pair_came = core_swap(jnp.where(core == 0, pair[:, 1], pair[:, 0]))
    pair = jnp.concatenate(
        [
            jnp.where(core == 0, pair_kept, pair_came),
            jnp.where(core == 0, pair_came, pair_kept),
        ],
        axis=2,
    )
    pair = z_exchange(pair).reshape(depth, 2, units, 2, strip)
    pair = pair.transpose(1, 4, 0, 3, 2).reshape(2, strip, width).astype(f32)

    results = back[:, :, :half].reshape(experts * 8, half)
    weighting = jnp.where(place, table[:, None, :], 0.0)
    halves = jnp.concatenate(
        [jnp.where(is_token, weighting, 0.0), jnp.where(is_token, 0.0, weighting)], axis=2
    ).reshape(experts * 8, 2 * rows)
    weighed = dot(halves, results.astype(f32), 0, 0, highest)
    wide_hot = hot_out.astype(f32)
    layer_out = jnp.concatenate([weighed[:rows], weighed[rows:]], axis=1)
    layer_out = (layer_out + hot_weight[:, None] * wide_hot).astype(bf16)

    products = jnp.where(
        is_token,
        dot(results, cotangent[:, :half], 1, 1).reshape(experts, 8, rows),
        dot(results, cotangent[:, half:], 1, 1).reshape(experts, 8, rows),
    )
    by_expert = jnp.sum(jnp.where(place, products, 0.0), axis=1)
    hot_product = jnp.sum(wide_hot * wide_cotangent, axis=1)
    is_busiest = jnp.arange(experts, dtype=jnp.int32)[:, None] == busiest
    by_expert = by_expert + jnp.where(is_busiest, hot_product[None], 0.0)
    route_gradient = jnp.sum(jnp.where(hits, by_expert[:, None, :], 0.0), axis=0).T

    def unstripe(block, tall):
        return block.reshape(-1, tall, 128).transpose(1, 0, 2).reshape(tall, -1)

    count = strip * width // 128
    home = mine == busiest
    gate_gradient = unstripe(own_sum[:count], strip) + jnp.where(home, pair[0], 0.0)
    up_gradient = unstripe(own_sum[count : 2 * count], strip) + jnp.where(home, pair[1], 0.0)
    down_gradient = unstripe(own_sum[2 * count :], units) + jnp.where(home, hot_down, 0.0)
    return (layer_out, route_gradient, gate_gradient[None], up_gradient[None], down_gradient[None])


def solution(mesh):
    in_specs = (
        P(("dp", "expert"), None),
        P(("dp", "expert"), None),
        P(("dp", "expert"), None),
        P(("dp", "expert"), None),
        P("expert", None, None),
        P("expert", None, None),
        P("expert", None, None),
    )
    out_specs = (
        P(("dp", "expert"), None),
        P(("dp", "expert"), None),
        P("expert", "dp", None),
        P("expert", "dp", None),
        P("expert", "dp", None),
    )
    return jax.shard_map(
        on_device, mesh=mesh, in_specs=in_specs, out_specs=out_specs, check_vma=False
    )
```

time: 213 us -> 207 us (0.972)
  blocking collectives: 0 us -> 19.6 us
  waiting for transfers between devices: 84.2 us -> 65.7 us
  matrix products: 18.9 us -> 5.11 us
  local copies, waits for them, and re-layouts: 17.3 us -> 6.45 us
  Pallas kernels: 0 us -> 7.31 us
  starting transfers between devices: 57.7 us -> 63.8 us
  other arithmetic: 15.8 us -> 20.6 us
    all_to_all x0 -> x1, blocking collectives: none -> 19.6 us  [plane_exchange(): lax.all_to_all(blocks, 'expert', split_axis=0, concat_axis=0, tiled=True)]
    ppermute x1 -> x3, starting transfers between devices: 2.16 us -> 19.7 us  [core_swap(): return lax.ppermute(block, 'dp', [(i, i ^ 1) for i in range(size)])]
    all_to_all x4 -> x3, starting transfers between devices: 41.5 us -> 26.4 us  [plane_exchange(): lax.all_to_all(blocks, 'expert', split_axis=0, concat_axis=0, tiled=True)]
    dot_general x21 -> x8, matrix products: 18.9 us -> 5.11 us  [dot(): lax.dot_general(lhs, rhs, dims, precision=precision, preferred_element_ty...]
    all_to_all x1, waiting for transfers between devices: 18.8 us -> 7.31 us  [z_exchange(): lax.all_to_all(blocks, 'dp', split_axis=0, concat_axis=0, tiled=True, axi...]
    pallas_call x0 -> x2, Pallas kernels: none -> 7.31 us  [the longest x1 5.94 us: own_expert(): pl.pallas_call(own_kernel, out_shape=(jax.ShapeDtypeStruct((rows.shape[0]...]
    reshape x11 -> x6, local copies, waits for them, and re-layouts: 7.71 us -> 0.42 us  [the longest x5 0.27 us: unstripe(): return block.reshape(-1, tall, 128).transpose(1, 0, 2).reshape(tall, -1)]
    all_gather x1, waiting for transfers between devices: 6.99 us -> 0.01 us  [on_device(): lax.all_gather(jnp.concatenate([tokens, hot_scaled], axis=1), 'dp', axis=...]
  transfers between devices with their start and end apart: 8 -> 9, of which waited for: 6 -> 5; matrix products, arithmetic and copies ran while one was open for 15% -> 10% of each run, Pallas kernels for 0% -> 4%
where the time goes in v2:
time: 207 us; the launch traced here: 206 us
  waiting for transfers between devices  65.7 us (32%)
  starting transfers between devices  63.8 us (31%)
  other arithmetic  20.6 us (10%)
  blocking collectives  19.6 us (9%)
  between operations  17.4 us (8%)
  Pallas kernels  7.31 us (4%)
  local copies, waits for them, and re-layouts  6.45 us (3%)
  matrix products  5.11 us (2%)
    all_to_all x3, waiting for transfers between devices, plane_exchange(): lax.all_to_all(blocks, 'expert', split_axis=0, concat_axis=0, tiled=True)  57.8 us
    all_to_all x3, starting transfers between devices, plane_exchange(): lax.all_to_all(blocks, 'expert', split_axis=0, concat_axis=0, tiled=True)  26.4 us
    ppermute x3, starting transfers between devices, core_swap(): return lax.ppermute(block, 'dp', [(i, i ^ 1) for i in range(size)])  19.7 us
    all_to_all x1, blocking collectives, plane_exchange(): lax.all_to_all(blocks, 'expert', split_axis=0, concat_axis=0, tiled=True)  19.6 us
    all_to_all x1, starting transfers between devices, z_exchange(): lax.all_to_all(blocks, 'dp', split_axis=0, concat_axis=0, tiled=True, axi...  17.6 us
    all_to_all x1, waiting for transfers between devices, z_exchange(): lax.all_to_all(blocks, 'dp', split_axis=0, concat_axis=0, tiled=True, axi...  7.31 us
    pallas_call x1, Pallas kernels, own_expert(): pl.pallas_call(own_kernel, out_shape=(jax.ShapeDtypeStruct((rows.shape[0]...  5.94 us
    dot_general x8, matrix products, dot(): lax.dot_general(lhs, rhs, dims, precision=precision, preferred_element_ty...  5.11 us
  transfers between devices with their start and end apart: 9, of which 5 were waited for; matrix products, arithmetic and copies ran while one was open for 10% of the time, Pallas kernels for 4%

profile of v2, /device:TPU:1, one launch (start us, length us, event | category | flops | bytes accessed | tf_op | source)
XLA Modules:
  0.0 206.0 jit_solution(9674268282536325298)
XLA Ops:
  7.2 0.9 fusion.25
  8.1 0.8 select_reduce_fusion.2
  11.7 0.9 fusion.18
  12.7 1.5 pad_maximum_fusion.2
  15.2 1.4 convolution_convert_fusion
  16.7 1.5 convolution_convert_fusion.1
  18.9 0.8 select_select_fusion.1
  20.9 1.2 fusion.2
  22.1 14.4 %all-to-all-start = ((bf16[64,8,1280]{2,1,0:T(8,128)(2,1)}), bf16[64,8,1280]{2,1,0:T(8,128)(2,1)}, u32[]{:S(2)}, u32[]{:S(2)}) async-start(bf16[64,8,1280]{2,1,0:T(8,128)(2,1)} %fusion.2), calls=%async_computation | async-start | bytes 2621440 | tf_op jit(solution)/shard_map/all_to_all | solution.py:21
  36.5 27.5 %all-to-all-done = bf16[64,8,1280]{2,1,0:T(8,128)(2,1)} async-done(((bf16[64,8,1280]{2,1,0:T(8,128)(2,1)}), bf16[64,8,1280]{2,1,0:T(8,128)(2,1)}, u32[]{:S(2)}, u32[]{:S(2)}) %all-to-all-start) | async-done | bytes 1310752 | tf_op jit(solution)/shard_map/all_to_all | solution.py:21
  64.0 5.9 %shard_map.110 = (bf16[512,512]{1,0:T(8,128)(2,1)S(1)}, bf16[8,576,128]{2,1,0:T(8,128)(2,1)S(1)}, bf16[8,576,128]{2,1,0:T(8,128)(2,1)}) custom-call(s32[1]{0:T(128)} %bitcast.2.core_ref, bf16[512,1280]{1,0:T(8,128)(2,1)} %bitcast.12.rows_ref, bf16[1024,384]{1,0:T(8,128)(2,1)S(1)} %bitcast.85, bf16[1024,384]{1,0:T(8,128)(2,1)S(1)} %bitcast.84, ...), custom_call_target="tpu_custom_call" | custom-call | tf_op jit(solution)/shard_map/pallas_call | solution.py:125
  69.9 10.3 %collective-permute-start = (bf16[8,576,128]{2,1,0:T(8,128)(2,1)}, bf16[8,576,128]{2,1,0:T(8,128)(2,1)}, u32[]{:S(2)}, u32[]{:S(2)}) collective-permute-start(bf16[8,576,128]{2,1,0:T(8,128)(2,1)} %get-tuple-element.16), channel_id=1, source_target_pairs={{0,64},{64,0},{128,192},{192,128},{256,320},{320,256},{384,448},{4... | collective-permute-start | bytes 3538952 | tf_op jit(solution)/shard_map/ppermute | solution.py:26
  80.2 1.0 slice.88
  81.2 19.6 %all_to_all.25 = bf16[64,8,256]{2,1,0:T(8,128)(2,1)S(1)} all-to-all(bf16[64,8,256]{2,1,0:T(8,128)(2,1)S(1)} %broadcast_in_dim.160), channel_id=1, replica_groups=mesh['dp'=16,'expert'=64] {'expert'}, dimensions={0} | all-to-all | bytes 524288 | tf_op jit(solution)/shard_map/all_to_all | solution.py:21
  100.9 1.6 copy-done.3
  102.5 1.4 shard_map.111
  103.8 4.0 %collective-permute-start.1 = (bf16[8,256,128]{2,1,0:T(8,128)(2,1)S(1)}, bf16[8,256,128]{2,1,0:T(8,128)(2,1)}, u32[]{:S(2)}, u32[]{:S(2)}) collective-permute-start(bf16[8,256,128]{2,1,0:T(8,128)(2,1)S(1)} %get-tuple-element.18), channel_id=1, source_target_pairs={{0,64},{64,0},{128,192},{192,128},{256,320},{320,256},{384,448},{4... | collective-permute-start | bytes 1572872 | tf_op jit(solution)/shard_map/ppermute | solution.py:26
  107.8 2.7 %add_convert_fusion = bf16[8,576,128]{2,1,0:T(8,128)(2,1)} fusion(bf16[8,576,128]{2,1,0:T(8,128)(2,1)} %collective-permute-done, bf16[8,576,128]{2,1,0:T(8,128)(2,1)S(1)} %get-tuple-element.15), kind=kLoop, calls=%fused_computation.2 | loop fusion | flops 2359296 | bytes 3538944 | tf_op jit(solution)/shard_map/convert_element_type | solution.py:46
  110.5 0.9 pad_maximum_fusion.1
  111.4 4.8 %all-to-all-start.2 = ((bf16[64,8,768]{2,1,0:T(8,128)(2,1)}), bf16[64,8,768]{2,1,0:T(8,128)(2,1)S(1)}, u32[]{:S(2)}, u32[]{:S(2)}) async-start(bf16[64,8,768]{2,1,0:T(8,128)(2,1)} %pad_maximum_fusion.1), calls=%async_computation.2 | async-start | bytes 1572864 | tf_op jit(solution)/shard_map/all_to_all | solution.py:21
  116.3 1.2 add_convert_fusion.1
  117.5 1.3 pad_maximum_fusion
  120.2 19.1 %all-to-all-done.2 = bf16[64,8,768]{2,1,0:T(8,128)(2,1)S(1)} async-done(((bf16[64,8,768]{2,1,0:T(8,128)(2,1)}), bf16[64,8,768]{2,1,0:T(8,128)(2,1)S(1)}, u32[]{:S(2)}, u32[]{:S(2)}) %all-to-all-start.2) | async-done | bytes 786464 | tf_op jit(solution)/shard_map/all_to_all | solution.py:21
  140.1 7.2 %all-to-all-start.3 = ((bf16[64,8,256]{2,1,0:T(8,128)(2,1)}), bf16[64,8,256]{2,1,0:T(8,128)(2,1)S(1)}, u32[]{:S(2)}, u32[]{:S(2)}) async-start(bf16[64,8,256]{2,1,0:T(8,128)(2,1)} %broadcast_in_dim.165), calls=%async_computation.4 | async-start | bytes 524288 | tf_op jit(solution)/shard_map/all_to_all | solution.py:21
  148.3 11.2 %all-to-all-done.3 = bf16[64,8,256]{2,1,0:T(8,128)(2,1)S(1)} async-done(((bf16[64,8,256]{2,1,0:T(8,128)(2,1)}), bf16[64,8,256]{2,1,0:T(8,128)(2,1)S(1)}, u32[]{:S(2)}, u32[]{:S(2)}) %all-to-all-start.3) | async-done | bytes 262176 | tf_op jit(solution)/shard_map/all_to_all | solution.py:21
  160.3 5.5 %collective-permute-start.2 = (bf16[8,48,64]{2,1,0:T(8,128)(2,1)S(1)}, bf16[8,48,64]{2,1,0:T(8,128)(2,1)S(1)}, u32[]{:S(2)}, u32[]{:S(2)}) collective-permute-start(bf16[8,48,64]{2,1,0:T(8,128)(2,1)S(1)} %bitcast.104), channel_id=1, source_target_pairs={{0,64},{64,0},{128,192},{192,128},{256,320},{320,256},{384,448},{4... | collective-permute-start | bytes 147464 | tf_op jit(solution)/shard_map/ppermute | solution.py:26
  167.5 17.6 %all-to-all-start.4 = ((bf16[8,48,128]{2,1,0:T(8,128)(2,1)}), bf16[8,48,128]{2,1,0:T(8,128)(2,1)S(1)}, u32[]{:S(2)}, u32[]{:S(2)}) async-start(bf16[8,48,128]{2,1,0:T(8,128)(2,1)} %pad_maximum_fusion.3), calls=%async_computation.5 | async-start | bytes 196608 | tf_op jit(solution)/shard_map/all_to_all | solution.py:32
  185.3 7.3 %all-to-all-done.4 = bf16[8,48,128]{2,1,0:T(8,128)(2,1)S(1)} async-done(((bf16[8,48,128]{2,1,0:T(8,128)(2,1)}), bf16[8,48,128]{2,1,0:T(8,128)(2,1)S(1)}, u32[]{:S(2)}, u32[]{:S(2)}) %all-to-all-start.4) | async-done | bytes 98336 | tf_op jit(solution)/shard_map/all_to_all | solution.py:32
  193.3 0.8 slice.92
  194.2 0.8 fusion.19
  195.1 0.8 select_reduce_fusion.1
  195.9 0.9 slice_convert_fusion
  (117 shorter events, 11.9 us)
Async XLA Ops:
  7.2 11.0 %copy-start.2 = (bf16[1,1024,384]{2,1,0:T(8,128)(2,1)S(1)}, bf16[1,1024,384]{2,1,0:T(8,128)(2,1)}, u32[]{:S(2)}) copy-start(bf16[1,1024,384]{2,1,0:T(8,128)(2,1)} %param.11) | copy-start | bytes 2359300
  7.2 93.7 %all-gather.2.cloned.1.call-start = ((), (), s32[]{:S(2)}) async-start(), calls=%async_computation.6 | async-start | bytes 2228224 | tf_op jit(solution)/shard_map/all_gather | solution.py:213
  11.7 3.5 %copy-start.15 = (f32[32]{0:T(128)}, f32[32]{0:T(128)S(1)}, u32[]{:S(2)}) copy-start(f32[32]{0:T(128)S(1)} %dynamic-slice_reduce_fusion) | copy-start | bytes 388
  14.2 5.5 %copy-start.19 = (pred[8]{0:T(512)(128)(4,1)}, pred[8]{0:T(512)(128)(4,1)S(1)}, u32[]{:S(2)}) copy-start(pred[8]{0:T(512)(128)(4,1)S(1)} %iota_compare_fusion.10) | copy-start | bytes 28
  14.9 5.0 %copy-start.17 = (s32[8]{0:T(128)}, s32[8]{0:T(128)S(1)}, u32[]{:S(2)}) copy-start(s32[8]{0:T(128)S(1)} %and_select_fusion) | copy-start | bytes 100
  14.9 4.8 %copy-start.12 = (pred[64,32]{0,1:T(8,128)(4,1)}, pred[64,32]{0,1:T(8,128)(4,1)S(1)}, u32[]{:S(2)}) copy-start(pred[64,32]{0,1:T(8,128)(4,1)S(1)} %broadcast_and_fusion) | copy-start | bytes 6148
  16.6 3.8 %copy-start.7 = (bf16[32,1024]{1,0:T(8,128)(2,1)S(1)}, bf16[32,1024]{1,0:T(8,128)(2,1)}, u32[]{:S(2)}) copy-start(bf16[32,1024]{1,0:T(8,128)(2,1)} %param.8) | copy-start | bytes 196612
  16.6 3.8 %copy-start.11 = (bf16[32,1024]{1,0:T(8,128)(2,1)S(1)}, bf16[32,1024]{1,0:T(8,128)(2,1)}, u32[]{:S(2)}) copy-start(bf16[32,1024]{1,0:T(8,128)(2,1)} %param.7) | copy-start | bytes 196612
  22.1 41.9 %copy-start = (bf16[1,384,1024]{2,1,0:T(8,128)(2,1)S(1)}, bf16[1,384,1024]{2,1,0:T(8,128)(2,1)}, u32[]{:S(2)}) copy-start(bf16[1,384,1024]{2,1,0:T(8,128)(2,1)} %param.13) | copy-start | bytes 2359300
  22.1 41.9 %copy-start.1 = (bf16[1,1024,384]{2,1,0:T(8,128)(2,1)S(1)}, bf16[1,1024,384]{2,1,0:T(8,128)(2,1)}, u32[]{:S(2)}) copy-start(bf16[1,1024,384]{2,1,0:T(8,128)(2,1)} %param.12) | copy-start | bytes 2359300
  22.1 41.9 %all-to-all-start = ((bf16[64,8,1280]{2,1,0:T(8,128)(2,1)}), bf16[64,8,1280]{2,1,0:T(8,128)(2,1)}, u32[]{:S(2)}, u32[]{:S(2)}) async-start(bf16[64,8,1280]{2,1,0:T(8,128)(2,1)} %fusion.2), calls=%async_computation | async-start | bytes 2621440 | tf_op jit(solution)/shard_map/all_to_all | solution.py:21
  69.9 11.3 %copy-start.4 = (bf16[512,512]{1,0:T(8,128)(2,1)}, bf16[512,512]{1,0:T(8,128)(2,1)S(1)}, u32[]{:S(2)}) copy-start(bf16[512,512]{1,0:T(8,128)(2,1)S(1)} %get-tuple-element.13) | copy-start | bytes 1572868
  69.9 37.9 %collective-permute-start = (bf16[8,576,128]{2,1,0:T(8,128)(2,1)}, bf16[8,576,128]{2,1,0:T(8,128)(2,1)}, u32[]{:S(2)}, u32[]{:S(2)}) collective-permute-start(bf16[8,576,128]{2,1,0:T(8,128)(2,1)} %get-tuple-element.16), channel_id=1, source_target_pairs={{0,64},{64,0},{128,192},{192,128},{256,320},{320,256},{384,448},{4... | collective-permute-start | bytes 3538952 | tf_op jit(solution)/shard_map/ppermute | solution.py:26
  100.9 1.6 copy-start.3
  103.8 12.4 %collective-permute-start.1 = (bf16[8,256,128]{2,1,0:T(8,128)(2,1)S(1)}, bf16[8,256,128]{2,1,0:T(8,128)(2,1)}, u32[]{:S(2)}, u32[]{:S(2)}) collective-permute-start(bf16[8,256,128]{2,1,0:T(8,128)(2,1)S(1)} %get-tuple-element.18), channel_id=1, source_target_pairs={{0,64},{64,0},{128,192},{192,128},{256,320},{320,256},{384,448},{4... | collective-permute-start | bytes 1572872 | tf_op jit(solution)/shard_map/ppermute | solution.py:26
  107.8 2.7 %copy-start.5 = (bf16[512,512]{1,0:T(8,128)(2,1)S(1)}, bf16[512,512]{1,0:T(8,128)(2,1)}, u32[]{:S(2)}) copy-start(bf16[512,512]{1,0:T(8,128)(2,1)} %copy-done.4) | copy-start | bytes 1572868
  111.4 6.0 %copy-start.6 = (bf16[8,576,128]{2,1,0:T(8,128)(2,1)S(1)}, bf16[8,576,128]{2,1,0:T(8,128)(2,1)}, u32[]{:S(2)}) copy-start(bf16[8,576,128]{2,1,0:T(8,128)(2,1)} %add_convert_fusion) | copy-start | bytes 3538948
  111.4 27.8 %all-to-all-start.2 = ((bf16[64,8,768]{2,1,0:T(8,128)(2,1)}), bf16[64,8,768]{2,1,0:T(8,128)(2,1)S(1)}, u32[]{:S(2)}, u32[]{:S(2)}) async-start(bf16[64,8,768]{2,1,0:T(8,128)(2,1)} %pad_maximum_fusion.1), calls=%async_computation.2 | async-start | bytes 1572864 | tf_op jit(solution)/shard_map/all_to_all | solution.py:21
  116.2 77.1 %reduce-scatter.2.cloned.1.call-start = ((), (), s32[]{:S(2)}) async-start(), calls=%async_computation.7 | async-start | bytes 1916928 | tf_op jit(solution)/shard_map/reduce_scatter | solution.py:40
  118.8 28.6 %copy-start.9 = (f32[64,8,32]{0,2,1:T(8,128)S(1)}, f32[64,8,32]{0,2,1:T(8,128)}, u32[]{:S(2)}) copy-start(f32[64,8,32]{0,2,1:T(8,128)} %get-tuple-element.34) | copy-start | bytes 196612
  118.8 28.6 %copy-start.10 = (f32[64,8,32]{0,2,1:T(8,128)S(1)}, f32[64,8,32]{0,2,1:T(8,128)}, u32[]{:S(2)}) copy-start(f32[64,8,32]{0,2,1:T(8,128)} %get-tuple-element.35) | copy-start | bytes 196612
  118.8 29.1 %copy-start.8 = (bf16[32,1024]{1,0:T(8,128)(2,1)S(1)}, bf16[32,1024]{1,0:T(8,128)(2,1)}, u32[]{:S(2)}) copy-start(bf16[32,1024]{1,0:T(8,128)(2,1)} %param.8) | copy-start | bytes 196612
  140.1 19.5 %all-to-all-start.3 = ((bf16[64,8,256]{2,1,0:T(8,128)(2,1)}), bf16[64,8,256]{2,1,0:T(8,128)(2,1)S(1)}, u32[]{:S(2)}, u32[]{:S(2)}) async-start(bf16[64,8,256]{2,1,0:T(8,128)(2,1)} %broadcast_in_dim.165), calls=%async_computation.4 | async-start | bytes 524288 | tf_op jit(solution)/shard_map/all_to_all | solution.py:21
  147.9 17.9 %copy-start.13 = (pred[64,32]{0,1:T(8,128)(4,1)S(1)}, pred[64,32]{0,1:T(8,128)(4,1)}, u32[]{:S(2)}) copy-start(pred[64,32]{0,1:T(8,128)(4,1)} %copy-done.12) | copy-start | bytes 6148
  147.9 17.9 %copy-start.18 = (s32[8]{0:T(128)S(1)}, s32[8]{0:T(128)}, u32[]{:S(2)}) copy-start(s32[8]{0:T(128)} %copy-done.17) | copy-start | bytes 100
  147.9 17.9 %copy-start.20 = (pred[8]{0:T(512)(128)(4,1)S(1)}, pred[8]{0:T(512)(128)(4,1)}, u32[]{:S(2)}) copy-start(pred[8]{0:T(512)(128)(4,1)} %copy-done.19) | copy-start | bytes 28
  160.3 6.4 %collective-permute-start.2 = (bf16[8,48,64]{2,1,0:T(8,128)(2,1)S(1)}, bf16[8,48,64]{2,1,0:T(8,128)(2,1)S(1)}, u32[]{:S(2)}, u32[]{:S(2)}) collective-permute-start(bf16[8,48,64]{2,1,0:T(8,128)(2,1)S(1)} %bitcast.104), channel_id=1, source_target_pairs={{0,64},{64,0},{128,192},{192,128},{256,320},{320,256},{384,448},{4... | collective-permute-start | bytes 147464 | tf_op jit(solution)/shard_map/ppermute | solution.py:26
  167.5 25.1 %all-to-all-start.4 = ((bf16[8,48,128]{2,1,0:T(8,128)(2,1)}), bf16[8,48,128]{2,1,0:T(8,128)(2,1)S(1)}, u32[]{:S(2)}, u32[]{:S(2)}) async-start(bf16[8,48,128]{2,1,0:T(8,128)(2,1)} %pad_maximum_fusion.3), calls=%async_computation.5 | async-start | bytes 196608 | tf_op jit(solution)/shard_map/all_to_all | solution.py:32
  185.1 9.1 %copy-start.16 = (f32[32]{0:T(128)S(1)}, f32[32]{0:T(128)}, u32[]{:S(2)}) copy-start(f32[32]{0:T(128)} %copy-done.15) | copy-start | bytes 388
  185.3 9.9 %copy-start.14 = (s32[32,8]{0,1:T(8,128)S(1)}, s32[32,8]{0,1:T(8,128)}, u32[]{:S(2)}) copy-start(s32[32,8]{0,1:T(8,128)} %param.10) | copy-start | bytes 3076
Sparse Core Ops, SparseCore 0:
  14.3 59.3 all-gather.1
  120.5 55.0 reduce-scatter.1

commit v3 on v2

--- a/solution.py
+++ b/solution.py
@@ -2,6 +2,7 @@
 
 import jax
 import jax.numpy as jnp
+import numpy as np
 from jax import lax
 from jax.experimental import pallas as pl
 from jax.experimental.pallas import tpu as pltpu
@@ -67,6 +68,148 @@
 
 def in_vmem(count):
     return [pl.BlockSpec(memory_space=pltpu.VMEM)] * count
+
+
+def pack_kernel(
+    shard_ref, tokens_ref, cotangent_ref, weight_ref, routed_ref, gate_ref, up_ref, down_ref,
+    out_ref, hot_ref, busiest_ref, size
+):
+    rows, features = tokens_ref.shape
+    width = gate_ref.shape[1]
+    units = width // size
+    height, spans = -(-3 * units // 16) * 16, features // 256
+    total = out_ref.shape[0]
+    experts = total // 8
+    names = lax.broadcasted_iota(jnp.int32, (experts, rows), 0)
+    named = jnp.zeros((experts, rows), f32)
+    table = jnp.zeros((experts, rows), f32)
+    for k in range(routed_ref.shape[0]):
+        hit = routed_ref[k : k + 1, :] == names
+        named = jnp.where(hit, 1.0, named)
+        table = jnp.where(hit, weight_ref[k : k + 1, :], table)
+    counts = jnp.sum(named, axis=1, keepdims=True)
+    busy = counts == jnp.max(counts, axis=0, keepdims=True)
+    busiest = jnp.max(jnp.where(busy, names, 0)[:, :1], axis=0, keepdims=True)
+    busiest_ref[...] = jnp.broadcast_to(busiest, busiest_ref.shape)
+    cold = jnp.where(busy, 0.0, named)
+    square = (rows, rows)
+    first = lax.broadcasted_iota(jnp.int32, square, 0)
+    second = lax.broadcasted_iota(jnp.int32, square, 1)
+    before = jnp.where(first < second, 1.0, 0.0)
+    rank = dot(cold.astype(bf16), before.astype(bf16), 1, 0)
+    code = jnp.where(cold > 0.0, rank + 1.0, 0.0)
+    hot_row = jnp.sum(jnp.where(busy, table, 0.0), axis=0, keepdims=True)
+    hot_weight = jnp.sum(jnp.where(first == second, hot_row, 0.0), axis=1, keepdims=True)
+    tokens = tokens_ref[...]
+    cotangent = cotangent_ref[...]
+    hot_ref[:, :features] = tokens
+    hot_ref[:, features:] = (hot_weight * cotangent.astype(f32)).astype(bf16)
+
+    owner = lax.broadcasted_iota(jnp.int32, (total, experts), 0) // 8
+    spread = owner == lax.broadcasted_iota(jnp.int32, (total, experts), 1)
+    spread = jnp.where(spread, 1.0, 0.0)
+    code = dot(spread.astype(bf16), code.astype(bf16), 1, 0)
+    table = dot(spread, table, 1, 0, highest)
+    row = lax.broadcasted_iota(jnp.int32, (total, rows), 0)
+    is_token = row % 8 < 4
+    place = code == (row % 4 + 1).astype(f32)
+    slot_weight = jnp.sum(jnp.where(place, table, 0.0), axis=1, keepdims=True)
+    factor = jnp.where(is_token[:, :1], 1.0, slot_weight)
+    place = jnp.where(place, 1.0, 0.0)
+    picked = dot(jnp.where(is_token, place, 0.0).astype(bf16), tokens, 1, 0)
+    picked = picked + dot(jnp.where(is_token, 0.0, place).astype(bf16), cotangent, 1, 0)
+    out_ref[:, :features] = (picked * factor).astype(bf16)
+
+    unit = shard_ref[0] * units + lax.broadcasted_iota(jnp.int32, (units, width), 0)
+    choose = unit == lax.broadcasted_iota(jnp.int32, (units, width), 1)
+    choose = jnp.where(choose, 1.0, 0.0).astype(bf16)
+    pieces = [
+        dot(choose, gate_ref[...], 1, 1),
+        dot(choose, up_ref[...], 1, 1),
+        dot(choose, down_ref[...], 1, 0),
+    ]
+    if height > 3 * units:
+        pieces.append(jnp.zeros((height - 3 * units, features), f32))
+    pieces = jnp.concatenate(pieces, axis=0).astype(bf16)
+    for span in range(spans):
+        out_ref[span * height : span * height + height, features:] = pieces[
+            :, span * 256 : span * 256 + 256
+        ]
+    used = spans * height
+    out_ref[used:, features:] = jnp.zeros((total - used, 256), bf16)
+
+
+def pack(shard, tokens, cotangent, weight, routed, gate, up, down, experts, size):
+    rows, features = tokens.shape
+    return pl.pallas_call(
+        functools.partial(pack_kernel, size=size),
+        out_shape=(
+            jax.ShapeDtypeStruct((experts * 8, features + 256), bf16),
+            jax.ShapeDtypeStruct((rows, 2 * features), bf16),
+            jax.ShapeDtypeStruct((8, 128), jnp.int32),
+        ),
+        in_specs=[pl.BlockSpec(memory_space=pltpu.SMEM)] + in_vmem(7),
+        out_specs=tuple(in_vmem(3)),
+        compiler_params=pltpu.CompilerParams(vmem_limit_bytes=48 * 2**20),
+    )(shard, tokens, cotangent, weight, routed, gate, up, down)
+
+
+def join_kernel(own_kept, own_came, hot_kept, hot_came, joined_ref, pair_ref):
+    own_rows = own_kept.shape[1]
+    rows = joined_ref.shape[1] - own_rows
+    joined_ref[:, :own_rows, :] = add(own_kept[...], own_came[...])
+    hot = add(hot_kept[...], hot_came[...])
+    joined_ref[:, own_rows:, :] = hot[:, :rows]
+    pair_ref[...] = hot[:, rows:]
+
+
+def join(own_kept, own_came, hot_kept, hot_came, strip):
+    depth, own_rows, _ = own_kept.shape
+    rows = own_rows + hot_kept.shape[1] - strip
+    return pl.pallas_call(
+        join_kernel,
+        out_shape=(
+            jax.ShapeDtypeStruct((depth, rows, 128), bf16),
+            jax.ShapeDtypeStruct((depth, strip, 128), bf16),
+        ),
+        in_specs=in_vmem(4),
+        out_specs=tuple(in_vmem(2)),
+        compiler_params=pltpu.CompilerParams(vmem_limit_bytes=48 * 2**20),
+    )(own_kept, own_came, hot_kept, hot_came)
+
+
+def pick_kernel(busiest_ref, piece_ref, out_ref):
+    out_ref[...] = jnp.broadcast_to(piece_ref[...], out_ref.shape)
+
+
+def pick(busiest, arrived, features):
+    experts = arrived.shape[0]
+    shape = (experts, 8, 256)
+    grid_spec = pltpu.PrefetchScalarGridSpec(
+        num_scalar_prefetch=1,
+        grid=(1,),
+        in_specs=[pl.BlockSpec((1, 8, 256), lambda i, chosen: (chosen[0], 0, features // 256))],
+        out_specs=pl.BlockSpec(shape, lambda i, chosen: (0, 0, 0)),
+    )
+    return pl.pallas_call(
+        pick_kernel, grid_spec=grid_spec, out_shape=jax.ShapeDtypeStruct(shape, bf16)
+    )(busiest, arrived)
+
+
+def total_kernel(parts_ref, out_ref):
+    total = jnp.sum(parts_ref[...].astype(f32), axis=0, keepdims=True).astype(bf16)
+    out_ref[...] = jnp.broadcast_to(total, out_ref.shape)
+
+
+def total(back, half):
+    shape = (back.shape[0], 8, 256)
+    return pl.pallas_call(
+        total_kernel,
+        grid=(1,),
+        in_specs=[pl.BlockSpec(shape, lambda i: (0, 0, half // 256))],
+        out_specs=pl.BlockSpec(shape, lambda i: (0, 0, 0)),
+        out_shape=jax.ShapeDtypeStruct(shape, bf16),
+    )(back)
 
 
 def own_kernel(
@@ -132,7 +275,7 @@
     )(core, rows, gate, up, down)
 
 
-def hot_kernel(units, core_ref, rows_ref, blocks_ref, kept_ref, passed_ref, grads_ref, part):
+def hot_kernel(units, core_ref, rows_ref, blocks_ref, kept_ref, passed_ref, grads_ref, part, pair_part):
     features = part.shape[1]
     depth = kept_ref.shape[0]
     group = part.shape[0] // (2 * depth)
@@ -151,13 +294,21 @@
     sigmoid = jax.nn.sigmoid(gate_value)
     active = gate_value * sigmoid
     slope = sigmoid * (1.0 + gate_value * (1.0 - sigmoid))
-    pair = jnp.concatenate([upstream * up_value * slope, upstream * active], axis=0).astype(bf16)
+    pair = jnp.concatenate([upstream * up_value * slope, upstream * active], axis=0)
     spare = jnp.zeros((height - 3 * units, gate_value.shape[1]), f32)
     hidden = active * up_value
     if spare.shape[0]:
         hidden = jnp.concatenate([hidden, spare], axis=0)
     hidden = hidden.astype(bf16)
     part[...] = dot(hidden, down, 0, 0)
+    empty = jnp.zeros_like(pair)
+    spread = [jnp.where(core == 0, pair, empty), jnp.where(core == 1, pair, empty)]
+    if 4 * units < 128:
+        spread.append(jnp.zeros((128 - 4 * units, pair.shape[1]), f32))
+    spread = jnp.concatenate(spread, axis=0).astype(bf16)
+    pair_part[...] = dot(inputs, spread, 0, 1)
+    strip = features // (2 * depth)
+    wide = group * (features // 128)
     for z in range(depth):
         for ref, side in ((kept_ref, core), (passed_ref, 1 - core)):
             start = pl.multiple_of((2 * z + side) * group, group)
@@ -166,25 +317,26 @@
                 ref[z, lane * group : lane * group + group, :] = block[
                     :, lane * 128 : lane * 128 + 128
                 ]
-    grads = jnp.concatenate([dot(pair, inputs, 1, 0), dot(hidden, scaled, 1, 0)], axis=0)
-    grads = grads.astype(bf16)
-    for span in range(spans):
-        grads_ref[span * height : span * height + height, :] = grads[
-            :, span * 256 : span * 256 + 256
-        ]
-    used = spans * height
-    grads_ref[used:, :] = jnp.zeros((grads_ref.shape[0] - used, 256), bf16)
+            start = pl.multiple_of((2 * z + side) * strip, strip)
+            ref[z, wide:, :] = pair_part[pl.ds(start, strip), :].astype(bf16)
+    grads = dot(hidden, scaled, 1, 0)[:units]
+    for lane in range(0, features // 128, 2):
+        both = [grads[:, i * 128 : i * 128 + 128] for i in (lane, lane + 1)]
+        grads_ref[lane * units : (lane + 2) * units, :] = jnp.concatenate(both, 0).astype(bf16)
+    used = features // 128 * units
+    grads_ref[used:, :] = jnp.zeros((grads_ref.shape[0] - used, 128), bf16)
 
 
 def hot_expert(core, gathered, blocks, units, depth):
     total, features = gathered.shape[0], gathered.shape[1] // 2
-    side = jax.ShapeDtypeStruct((depth, total // (2 * depth) * features // 128, 128), bf16)
+    height = total // (2 * depth) * features // 128 + features // (2 * depth)
+    side = jax.ShapeDtypeStruct((depth, height, 128), bf16)
     return pl.pallas_call(
         functools.partial(hot_kernel, units),
-        out_shape=(side, side, jax.ShapeDtypeStruct(blocks.shape, bf16)),
+        out_shape=(side, side, jax.ShapeDtypeStruct((blocks.shape[0], 128), bf16)),
         in_specs=[pl.BlockSpec(memory_space=pltpu.SMEM)] + in_vmem(2),
         out_specs=tuple(in_vmem(3)),
-        scratch_shapes=[pltpu.VMEM((total, features), f32)],
+        scratch_shapes=[pltpu.VMEM((total, features), f32), pltpu.VMEM((features, 128), f32)],
         compiler_params=pltpu.CompilerParams(vmem_limit_bytes=48 * 2**20),
     )(core, gathered, blocks)
 
@@ -206,78 +358,65 @@
     units = width // size
     strip = features // size
 
-    busiest, hits, table, place = routing(routed_experts.T, route_weight.T, experts)
+    shard_word = shard.astype(jnp.int32).reshape(1)
+    outgoing, hot_rows, found = pack(
+        shard_word,
+        tokens,
+        cotangent,
+        route_weight.T,
+        routed_experts.T,
+        gate,
+        up,
+        down,
+        experts,
+        size,
+    )
+    gathered = lax.all_gather(hot_rows, "dp", axis=0, tiled=True)
+    arrived = plane_exchange(outgoing.reshape(experts, 8, features + 256))
+    picked = pick(found[0, :1], arrived, features)
+    arrived, picked, routed, weight = lax.optimization_barrier(
+        (arrived, picked, routed_experts.T, route_weight.T)
+    )
+    blocks = plane_exchange(picked)
+    busiest, hits, table, place = routing(routed, weight, experts)
+    is_token = (jnp.arange(8) < 4)[None, :, None]
     hot_weight = lax.dynamic_index_in_dim(table, busiest, 0, keepdims=False)
     wide_cotangent = cotangent.astype(f32)
-    hot_scaled = (hot_weight[:, None] * wide_cotangent).astype(bf16)
-    gathered = lax.all_gather(
-        jnp.concatenate([tokens, hot_scaled], axis=1), "dp", axis=0, tiled=True
-    )
-
-    is_token = (jnp.arange(8) < 4)[None, :, None]
-    picks = jnp.concatenate([place & is_token, place & ~is_token], axis=2)
-    slot_weight = jnp.sum(jnp.where(place, table[:, None, :], 0.0), axis=2)
-    factor = jnp.where(jnp.arange(8)[None, :] < 4, 1.0, slot_weight).reshape(experts * 8, 1)
-    stacked = jnp.concatenate([tokens, cotangent], axis=0)
-    picked = dot(picks.astype(bf16).reshape(experts * 8, 2 * rows), stacked, 1, 0)
-    outgoing = (picked * factor).astype(bf16).reshape(experts, 8, features)
-
-    unit = shard * units + jnp.arange(units, dtype=jnp.int32)
-    choose = (jnp.arange(width, dtype=jnp.int32)[None, :] == unit[:, None]).astype(bf16)
-    height, spans = -(-3 * units // 16) * 16, features // 256
-    pieces = jnp.concatenate(
-        [
-            dot(choose, gate, 1, 1).astype(bf16),
-            dot(choose, up, 1, 1).astype(bf16),
-            dot(choose, down, 1, 0).astype(bf16),
-            jnp.zeros((height - 3 * units, features), bf16),
-        ],
-        axis=0,
-    )
-    pieces = pieces.reshape(height // 8, 8, spans, 256).transpose(2, 0, 1, 3)
-    pieces = pad_blocks(pieces.reshape(height // 8 * spans, 8, 256), experts)
-
-    arrived = plane_exchange(jnp.concatenate([outgoing, pieces], axis=2))
-    piece = lax.dynamic_index_in_dim(arrived[:, :, features:], busiest, 0, keepdims=True)
-    blocks = plane_exchange(jnp.broadcast_to(piece, (experts, 8, 256)))
-
     returning, own_kept, own_passed = own_expert(
         core_word, arrived.reshape(experts * 8, features + 256), gate, up, down, depth
     )
+    blocks, own_passed = lax.optimization_barrier((blocks, own_passed))
     own_came = core_swap(own_passed)
     hot_kept, hot_passed, hot_grads = hot_expert(
         core_word, gathered, blocks.reshape(experts * 8, 256), units, depth
     )
     hot_came = core_swap(hot_passed)
-    joined = jnp.concatenate([add(own_kept, own_came), add(hot_kept, hot_came)], axis=1)
+    joined, pair = join(own_kept, own_came, hot_kept, hot_came, strip)
     summed = z_reduce_scatter(joined)[0]
     own_rows = own_kept.shape[1]
     own_sum = summed[:own_rows].astype(f32)
     hot_out = summed[own_rows:].reshape(features // 128, rows, 128)
     hot_out = hot_out.transpose(1, 0, 2).reshape(rows, features)
+    pair = pad_blocks(z_exchange(pair).reshape(depth * strip // 8, 8, 128), experts)
 
     back = plane_exchange(
         jnp.concatenate(
-            [returning.reshape(experts, 8, half), hot_grads.reshape(experts, 8, 256)], axis=2
+            [returning.reshape(experts, 8, half), pair, hot_grads.reshape(experts, 8, 128)], axis=2
         )
     )
-    hot_piece = jnp.sum(back[:, :, half:].astype(f32), axis=0).astype(bf16)
-    hot_blocks = plane_exchange(jnp.broadcast_to(hot_piece[None], (experts, 8, 256)))
-    hot_rows = hot_blocks.reshape(experts * 8, 256)[: spans * height]
-    hot_rows = hot_rows.reshape(spans, height, 256).transpose(1, 0, 2).reshape(height, features)
-    hot_down = hot_rows[2 * units : 3 * units].astype(f32)
-    pair = hot_rows[: 2 * units].reshape(2 * units, depth, 2, strip).transpose(1, 2, 0, 3)
-    pair_kept = jnp.where(core == 0, pair[:, 0], pair[:, 1])
-    pair_came = core_swap(jnp.where(core == 0, pair[:, 1], pair[:, 0]))
-    pair = jnp.concatenate(
-        [
-            jnp.where(core == 0, pair_kept, pair_came),
-            jnp.where(core == 0, pair_came, pair_kept),
-        ],
-        axis=2,
-    )
-    pair = z_exchange(pair).reshape(depth, 2, units, 2, strip)
-    pair = pair.transpose(1, 4, 0, 3, 2).reshape(2, strip, width).astype(f32)
+    hot_blocks = plane_exchange(total(back, half))
+
+    lane = np.arange(depth * 128)
+    within = lane % 128
+    column = (within % (2 * units)) // units * width
+    column = column + (lane // 128 * 2 + within // (2 * units)) * units + within % units
+    column = np.where(within < 4 * units, column, -1).astype(np.int32)
+    spread = (jnp.asarray(column)[:, None] == jnp.arange(2 * width, dtype=jnp.int32)).astype(bf16)
+    hot_pair = hot_blocks[: depth * strip // 8, :, :128].reshape(depth, strip, 128)
+    hot_pair = dot(hot_pair.transpose(1, 0, 2).reshape(strip, depth * 128), spread, 1, 0)
+    hot_down = hot_blocks.reshape(experts * 8, 256)[: features // 128 * units, 128:]
+    hot_down = hot_down.reshape(features // 128, units, 128).transpose(1, 0, 2)
+    hot_down = hot_down.reshape(units, features).astype(f32)
 
     results = back[:, :, :half].reshape(experts * 8, half)
     weighting = jnp.where(place, table[:, None, :], 0.0)
@@ -305,8 +444,12 @@
 
     count = strip * width // 128
     home = mine == busiest
-    gate_gradient = unstripe(own_sum[:count], strip) + jnp.where(home, pair[0], 0.0)
-    up_gradient = unstripe(own_sum[count : 2 * count], strip) + jnp.where(home, pair[1], 0.0)
+    gate_gradient = unstripe(own_sum[:count], strip) + jnp.where(
+        home, hot_pair[:, :width], 0.0
+    )
+    up_gradient = unstripe(own_sum[count : 2 * count], strip) + jnp.where(
+        home, hot_pair[:, width:], 0.0
+    )
     down_gradient = unstripe(own_sum[2 * count :], units) + jnp.where(home, hot_down, 0.0)
     return (layer_out, route_gradient, gate_gradient[None], up_gradient[None], down_gradient[None])
 

time: 207 us -> 195 us (0.942)
  other arithmetic: 20.6 us -> 6.68 us
  starting transfers between devices: 63.8 us -> 50.2 us
  Pallas kernels: 7.31 us -> 16 us
  local copies, waits for them, and re-layouts: 6.45 us -> 13.5 us
  blocking collectives: 19.6 us -> 25.5 us
  waiting for transfers between devices: 65.7 us -> 60.2 us
    all_to_all x1 -> x0, starting transfers between devices: 17.6 us -> none  [z_exchange(): lax.all_to_all(blocks, 'dp', split_axis=0, concat_axis=0, tiled=True, axi...]
    all_to_all x3 -> x4, starting transfers between devices: 26.4 us -> 42.8 us  [plane_exchange(): lax.all_to_all(blocks, 'expert', split_axis=0, concat_axis=0, tiled=True)]
    ppermute x3 -> x2, starting transfers between devices: 19.7 us -> 7.4 us  [core_swap(): return lax.ppermute(block, 'dp', [(i, i ^ 1) for i in range(size)])]
    unnamed x44 -> x40, local copies, waits for them, and re-layouts: 1.88 us -> 10.8 us
    pallas_call x0 -> x4, Pallas kernels: none -> 8.13 us  [the longest x1 2.77 us: pack(): pl.pallas_call(functools.partial(pack_kernel, size=size), out_shape=(jax....]
    all_to_all x1 -> x0, waiting for transfers between devices: 7.31 us -> none  [z_exchange(): lax.all_to_all(blocks, 'dp', split_axis=0, concat_axis=0, tiled=True, axi...]
    all_to_all x1, blocking collectives: 19.6 us -> 25.5 us  [z_exchange(): lax.all_to_all(blocks, 'dp', split_axis=0, concat_axis=0, tiled=True, axi...]
    concatenate x6 -> x1, other arithmetic: 5.75 us -> 0.94 us  [on_device(): jnp.concatenate([returning.reshape(experts, 8, half), pair, hot_grads.res...]
  transfers between devices with their start and end apart: 9 -> 8, of which waited for: 5 -> 5; matrix products, arithmetic and copies ran while one was open for 10% -> 3% of each run, Pallas kernels for 4% -> 6%
where the time goes in v3:
time: 195 us; the launch traced here: 192 us
  waiting for transfers between devices  60.2 us (31%)
  starting transfers between devices  50.2 us (26%)
  blocking collectives  25.5 us (13%)
  between operations  17 us (9%)
  Pallas kernels  16 us (8%)
  local copies, waits for them, and re-layouts  13.5 us (7%)
  other arithmetic  6.68 us (3%)
  matrix products  3.09 us (2%)
    all_to_all x4, waiting for transfers between devices, plane_exchange(): lax.all_to_all(blocks, 'expert', split_axis=0, concat_axis=0, tiled=True)  58 us
    all_to_all x4, starting transfers between devices, plane_exchange(): lax.all_to_all(blocks, 'expert', split_axis=0, concat_axis=0, tiled=True)  42.8 us
    all_to_all x1, blocking collectives, z_exchange(): lax.all_to_all(blocks, 'dp', split_axis=0, concat_axis=0, tiled=True, axi...  25.5 us
    unnamed x40, local copies, waits for them, and re-layouts  10.8 us
    ppermute x2, starting transfers between devices, core_swap(): return lax.ppermute(block, 'dp', [(i, i ^ 1) for i in range(size)])  7.4 us
    pallas_call x1, Pallas kernels, own_expert(): pl.pallas_call(own_kernel, out_shape=(jax.ShapeDtypeStruct((rows.shape[0]...  5.41 us
  transfers between devices with their start and end apart: 8, of which 5 were waited for; matrix products, arithmetic and copies ran while one was open for 3% of the time, Pallas kernels for 6%

profile of v3, /device:TPU:1, one launch (start us, length us, event | category | flops | bytes accessed | tf_op | source)
XLA Modules:
  0.0 192.2 jit_solution(6445429815469327134)
XLA Ops:
  7.2 1.1 copy-done
  8.4 1.1 copy-done.2
  9.5 1.1 copy-done.4
  10.6 0.8 copy-done.7
  11.5 0.8 copy-done.11
  13.7 2.8 %shard_map.119 = (bf16[512,1280]{1,0:T(8,128)(2,1)}, bf16[32,2048]{1,0:T(8,128)(2,1)}, s32[8,128]{1,0:T(8,128)S(1)}) custom-call(s32[1]{0:T(128)} %bitcast.shard_ref, bf16[32,1024]{1,0:T(8,128)(2,1)S(1)} %copy-done.11, bf16[32,1024]{1,0:T(8,128)(2,1)S(1)} %copy-done.7, f32[8,32]{1,0:T(8,128)S(1)} %bitcast.80, s32[8,32]{1,0:T(8,128)S(1)} %bitcast.77, ...), custom_call_target="tpu_custom_call" | custom-call | tf_op jit(solution)/shard_map/pallas_call | solution.py:144
  16.5 14.4 %all-to-all-start = ((bf16[64,8,1280]{2,1,0:T(8,128)(2,1)}), bf16[64,8,1280]{2,1,0:T(8,128)(2,1)}, u32[]{:S(2)}, u32[]{:S(2)}) async-start(bf16[64,8,1280]{2,1,0:T(8,128)(2,1)} %bitcast.6), calls=%async_computation | async-start | bytes 2621440 | tf_op jit(solution)/shard_map/all_to_all | solution.py:22
  31.4 27.0 %all-to-all-done.piece_ref = bf16[64,8,1280]{2,1,0:T(8,128)(2,1)} async-done(((bf16[64,8,1280]{2,1,0:T(8,128)(2,1)}), bf16[64,8,1280]{2,1,0:T(8,128)(2,1)}, u32[]{:S(2)}, u32[]{:S(2)}) %all-to-all-start) | async-done | bytes 1310752 | tf_op jit(solution)/shard_map/all_to_all | solution.py:22
  58.4 2.0 %shard_map.120 = bf16[64,8,256]{2,1,0:T(8,128)(2,1)} custom-call(s32[1]{0:T(128)} %bitcast.7.busiest_ref, bf16[64,8,1280]{2,1,0:T(8,128)(2,1)} %all-to-all-done.piece_ref), custom_call_target="tpu_custom_call" | custom-call | tf_op jit(solution)/shard_map/pallas_call | solution.py:194
  60.4 13.3 %all-to-all-start.1 = ((bf16[64,8,256]{2,1,0:T(8,128)(2,1)}), bf16[64,8,256]{2,1,0:T(8,128)(2,1)}, u32[]{:S(2)}, u32[]{:S(2)}) async-start(bf16[64,8,256]{2,1,0:T(8,128)(2,1)} %shard_map.120), calls=%async_computation.1 | async-start | bytes 524288 | tf_op jit(solution)/shard_map/all_to_all | solution.py:22
  73.8 5.4 %shard_map.121 = (bf16[512,512]{1,0:T(8,128)(2,1)S(1)}, bf16[8,576,128]{2,1,0:T(8,128)(2,1)S(1)}, bf16[8,576,128]{2,1,0:T(8,128)(2,1)S(1)}) custom-call(s32[1]{0:T(128)} %bitcast.8.core_ref, bf16[512,1280]{1,0:T(8,128)(2,1)} %bitcast.9.rows_ref, bf16[1024,384]{1,0:T(8,128)(2,1)S(1)} %bitcast.70, bf16[1024,384]{1,0:T(8,128)(2,1)S(1)} %bitcast.72, ...), custom_call_target="tpu_custom_call" | custom-call | tf_op jit(solution)/shard_map/pallas_call | solution.py:268
  80.1 1.0 copy-done.16
  81.1 5.0 %all-to-all-done.1 = bf16[64,8,256]{2,1,0:T(8,128)(2,1)} async-done(((bf16[64,8,256]{2,1,0:T(8,128)(2,1)}), bf16[64,8,256]{2,1,0:T(8,128)(2,1)}, u32[]{:S(2)}, u32[]{:S(2)}) %all-to-all-start.1) | async-done | bytes 262176 | tf_op jit(solution)/shard_map/all_to_all | solution.py:22
  86.1 5.5 %collective-permute-start = (bf16[8,576,128]{2,1,0:T(8,128)(2,1)}, bf16[8,576,128]{2,1,0:T(8,128)(2,1)S(1)}, u32[]{:S(2)}, u32[]{:S(2)}) collective-permute-start(bf16[8,576,128]{2,1,0:T(8,128)(2,1)} %copy-done.16), channel_id=1, source_target_pairs={{0,64},{64,0},{128,192},{192,128},{256,320},{320,256},{384,448},{4... | collective-permute-start | bytes 3538952 | tf_op jit(solution)/shard_map/ppermute | solution.py:27
  91.6 1.6 copy-done.6
  93.2 2.5 %shard_map.122 = (bf16[8,320,128]{2,1,0:T(8,128)(2,1)S(1)}, bf16[8,320,128]{2,1,0:T(8,128)(2,1)S(1)}, bf16[512,128]{1,0:T(8,128)(2,1)S(1)}) custom-call(s32[1]{0:T(128)} %bitcast.8.core_ref, bf16[512,2048]{1,0:T(8,128)(2,1)S(1)} %copy-done.6, bf16[512,256]{1,0:T(8,128)(2,1)} %bitcast.11.blocks_ref), custom_call_target="tpu_custom_call" | custom-call | tf_op jit(solution)/shard_map/pallas_call | solution.py:334
  95.6 1.9 %collective-permute-start.1 = (bf16[8,320,128]{2,1,0:T(8,128)(2,1)S(1)}, bf16[8,320,128]{2,1,0:T(8,128)(2,1)S(1)}, u32[]{:S(2)}, u32[]{:S(2)}) collective-permute-start(bf16[8,320,128]{2,1,0:T(8,128)(2,1)S(1)} %get-tuple-element.37), channel_id=1, source_target_pairs={{0,64},{64,0},{128,192},{192,128},{256,320},{320,256},{384,448},{4... | collective-permute-start | bytes 1966088 | tf_op jit(solution)/shard_map/ppermute | solution.py:27
  97.6 2.0 %collective-permute-done.1.hot_came = bf16[8,320,128]{2,1,0:T(8,128)(2,1)S(1)} collective-permute-done((bf16[8,320,128]{2,1,0:T(8,128)(2,1)S(1)}, bf16[8,320,128]{2,1,0:T(8,128)(2,1)S(1)}, u32[]{:S(2)}, u32[]{:S(2)}) %collective-permute-start.1) | collective-permute-done | bytes 655392 | tf_op jit(solution)/shard_map/ppermute | solution.py:27
  99.6 1.6 shard_map.123
  101.3 25.5 %all_to_all.25 = bf16[8,64,128]{2,1,0:T(8,128)(2,1)S(1)} all-to-all(bf16[8,64,128]{2,1,0:T(8,128)(2,1)S(1)} %get-tuple-element.38), channel_id=1, replica_groups={{0,128,256,384,512,640,768,896},{64,192,320,448,576,704,832,960},{1,129..., dimensions={0} | all-to-all | bytes 262144 | tf_op jit(solution)/shard_map/all_to_all | solution.py:33
  126.8 0.9 pad_maximum_fusion
  127.7 6.2 %all-to-all-start.3 = ((bf16[64,8,768]{2,1,0:T(8,128)(2,1)}), bf16[64,8,768]{2,1,0:T(8,128)(2,1)S(1)}, u32[]{:S(2)}, u32[]{:S(2)}) async-start(bf16[64,8,768]{2,1,0:T(8,128)(2,1)} %pad_maximum_fusion), calls=%async_computation.3 | async-start | bytes 1572864 | tf_op jit(solution)/shard_map/all_to_all | solution.py:22
  138.9 15.8 %all-to-all-done.3.parts_ref = bf16[64,8,768]{2,1,0:T(8,128)(2,1)S(1)} async-done(((bf16[64,8,768]{2,1,0:T(8,128)(2,1)}), bf16[64,8,768]{2,1,0:T(8,128)(2,1)S(1)}, u32[]{:S(2)}, u32[]{:S(2)}) %all-to-all-start.3) | async-done | bytes 786464 | tf_op jit(solution)/shard_map/all_to_all | solution.py:22
  154.6 0.9 copy-done.17
  155.5 1.7 shard_map.124
  157.2 8.9 %all-to-all-start.4 = ((bf16[64,8,256]{2,1,0:T(8,128)(2,1)}), bf16[64,8,256]{2,1,0:T(8,128)(2,1)S(1)}, u32[]{:S(2)}, u32[]{:S(2)}) async-start(bf16[64,8,256]{2,1,0:T(8,128)(2,1)} %shard_map.124), calls=%async_computation.5 | async-start | bytes 524288 | tf_op jit(solution)/shard_map/all_to_all | solution.py:22
  166.1 1.3 fusion.16
  168.1 10.3 %all-to-all-done.4 = bf16[64,8,256]{2,1,0:T(8,128)(2,1)S(1)} async-done(((bf16[64,8,256]{2,1,0:T(8,128)(2,1)}), bf16[64,8,256]{2,1,0:T(8,128)(2,1)S(1)}, u32[]{:S(2)}, u32[]{:S(2)}) %all-to-all-start.4) | async-done | bytes 262176 | tf_op jit(solution)/shard_map/all_to_all | solution.py:22
  178.6 0.8 fusion
  179.4 1.0 slice_convert_fusion
  181.3 0.8 slice.68
  182.4 0.8 select_reduce_fusion
  (72 shorter events, 9.2 us)
Async XLA Ops:
  7.2 84.4 %all-gather.2.cloned.1.call-start = ((), (), s32[]{:S(2)}) async-start(), calls=%async_computation.6 | async-start | bytes 2228224 | tf_op jit(solution)/shard_map/all_gather | solution.py:374
  7.2 1.1 copy-start
  8.4 1.1 copy-start.2
  9.5 1.1 copy-start.4
  10.6 0.8 copy-start.7
  11.5 0.8 copy-start.11
  12.3 0.7 copy-start.12
  13.0 0.7 copy-start.14
  16.5 57.3 %copy-start.5 = (bf16[1,384,1024]{2,1,0:T(8,128)(2,1)S(1)}, bf16[1,384,1024]{2,1,0:T(8,128)(2,1)}, u32[]{:S(2)}) copy-start(bf16[1,384,1024]{2,1,0:T(8,128)(2,1)} %param.14) | copy-start | bytes 2359300
  16.5 41.9 %all-to-all-start = ((bf16[64,8,1280]{2,1,0:T(8,128)(2,1)}), bf16[64,8,1280]{2,1,0:T(8,128)(2,1)}, u32[]{:S(2)}, u32[]{:S(2)}) async-start(bf16[64,8,1280]{2,1,0:T(8,128)(2,1)} %bitcast.6), calls=%async_computation | async-start | bytes 2621440 | tf_op jit(solution)/shard_map/all_to_all | solution.py:22
  30.9 42.9 %copy-start.1 = (bf16[1,1024,384]{2,1,0:T(8,128)(2,1)S(1)}, bf16[1,1024,384]{2,1,0:T(8,128)(2,1)}, u32[]{:S(2)}) copy-start(bf16[1,1024,384]{2,1,0:T(8,128)(2,1)} %param.12) | copy-start | bytes 2359300
  30.9 42.9 %copy-start.3 = (bf16[1,1024,384]{2,1,0:T(8,128)(2,1)S(1)}, bf16[1,1024,384]{2,1,0:T(8,128)(2,1)}, u32[]{:S(2)}) copy-start(bf16[1,1024,384]{2,1,0:T(8,128)(2,1)} %param.13) | copy-start | bytes 2359300
  60.4 25.6 %all-to-all-start.1 = ((bf16[64,8,256]{2,1,0:T(8,128)(2,1)}), bf16[64,8,256]{2,1,0:T(8,128)(2,1)}, u32[]{:S(2)}, u32[]{:S(2)}) async-start(bf16[64,8,256]{2,1,0:T(8,128)(2,1)} %shard_map.120), calls=%async_computation.1 | async-start | bytes 524288 | tf_op jit(solution)/shard_map/all_to_all | solution.py:22
  73.8 105.7 %reduce-scatter.2.cloned.1.call-start = ((), (), s32[]{:S(2)}) async-start(), calls=%async_computation.7 | async-start | bytes 1916928 | tf_op jit(solution)/shard_map/reduce_scatter | solution.py:41
  79.3 0.8 copy-start.9
  80.1 1.0 copy-start.16
  86.1 11.5 %collective-permute-start = (bf16[8,576,128]{2,1,0:T(8,128)(2,1)}, bf16[8,576,128]{2,1,0:T(8,128)(2,1)S(1)}, u32[]{:S(2)}, u32[]{:S(2)}) collective-permute-start(bf16[8,576,128]{2,1,0:T(8,128)(2,1)} %copy-done.16), channel_id=1, source_target_pairs={{0,64},{64,0},{128,192},{192,128},{256,320},{320,256},{384,448},{4... | collective-permute-start | bytes 3538952 | tf_op jit(solution)/shard_map/ppermute | solution.py:27
  91.6 1.6 copy-start.6
  95.6 4.0 %collective-permute-start.1 = (bf16[8,320,128]{2,1,0:T(8,128)(2,1)S(1)}, bf16[8,320,128]{2,1,0:T(8,128)(2,1)S(1)}, u32[]{:S(2)}, u32[]{:S(2)}) collective-permute-start(bf16[8,320,128]{2,1,0:T(8,128)(2,1)S(1)} %get-tuple-element.37), channel_id=1, source_target_pairs={{0,64},{64,0},{128,192},{192,128},{256,320},{320,256},{384,448},{4... | collective-permute-start | bytes 1966088 | tf_op jit(solution)/shard_map/ppermute | solution.py:27
  101.2 25.6 %copy-start.10 = (bf16[512,512]{1,0:T(8,128)(2,1)S(1)}, bf16[512,512]{1,0:T(8,128)(2,1)}, u32[]{:S(2)}) copy-start(bf16[512,512]{1,0:T(8,128)(2,1)} %copy-done.9) | copy-start | bytes 1572868
  126.8 7.2 %copy-start.13 = (s32[32,8]{0,1:T(8,128)S(1)}, s32[32,8]{0,1:T(8,128)}, u32[]{:S(2)}) copy-start(s32[32,8]{0,1:T(8,128)} %param.11) | copy-start | bytes 3076
  127.7 38.4 %copy-start.8 = (bf16[32,1024]{1,0:T(8,128)(2,1)S(1)}, bf16[32,1024]{1,0:T(8,128)(2,1)}, u32[]{:S(2)}) copy-start(bf16[32,1024]{1,0:T(8,128)(2,1)} %cotangent_ref.1) | copy-start | bytes 196612
  127.7 26.9 %all-to-all-start.3 = ((bf16[64,8,768]{2,1,0:T(8,128)(2,1)}), bf16[64,8,768]{2,1,0:T(8,128)(2,1)S(1)}, u32[]{:S(2)}, u32[]{:S(2)}) async-start(bf16[64,8,768]{2,1,0:T(8,128)(2,1)} %pad_maximum_fusion), calls=%async_computation.3 | async-start | bytes 1572864 | tf_op jit(solution)/shard_map/all_to_all | solution.py:22
  154.6 0.9 copy-start.17
  157.2 10.3 %copy-start.18 = (bf16[64,8,768]{2,1,0:T(8,128)(2,1)S(1)}, bf16[64,8,768]{2,1,0:T(8,128)(2,1)}, u32[]{:S(2)}) copy-start(bf16[64,8,768]{2,1,0:T(8,128)(2,1)} %copy-done.17) | copy-start | bytes 2359300
  157.2 21.2 %all-to-all-start.4 = ((bf16[64,8,256]{2,1,0:T(8,128)(2,1)}), bf16[64,8,256]{2,1,0:T(8,128)(2,1)S(1)}, u32[]{:S(2)}, u32[]{:S(2)}) async-start(bf16[64,8,256]{2,1,0:T(8,128)(2,1)} %shard_map.124), calls=%async_computation.5 | async-start | bytes 524288 | tf_op jit(solution)/shard_map/all_to_all | solution.py:22
  167.6 11.0 %copy-start.19 = (s32[1024]{0:T(1024)S(1)}, s32[1024]{0:T(1024)}, u32[]{:S(2)}) copy-start(s32[1024]{0:T(1024)} %constant.55.clone) | copy-start | bytes 12292
  178.6 3.8 %copy-start.15 = (f32[32,8]{0,1:T(8,128)S(1)}, f32[32,8]{0,1:T(8,128)}, u32[]{:S(2)}) copy-start(f32[32,8]{0,1:T(8,128)} %param.10) | copy-start | bytes 3076
  179.4 4.1 %slice-start = ((bf16[64,8,768]{2,1,0:T(8,128)(2,1)}), bf16[64,8,512]{2,1,0:T(8,128)(2,1)S(1)}, s32[]{:S(2)}) async-start(bf16[64,8,768]{2,1,0:T(8,128)(2,1)} %copy-done.17), calls=%async_computation.8 | async-start | bytes 1048576 | tf_op jit(solution)/shard_map/slice | solution.py:421
Sparse Core Ops, SparseCore 0:
  16.6 59.4 all-gather.1
  101.4 48.6 reduce-scatter.1

commit v4 on v3

--- a/solution.py
+++ b/solution.py
@@ -2,7 +2,6 @@
 
 import jax
 import jax.numpy as jnp
-import numpy as np
 from jax import lax
 from jax.experimental import pallas as pl
 from jax.experimental.pallas import tpu as pltpu
@@ -51,35 +50,13 @@
     return jnp.pad(blocks, ((0, count - blocks.shape[0]),) + ((0, 0),) * (blocks.ndim - 1))
 
 
-def routing(routed, weight, experts):
-    rows = routed.shape[1]
-    names = jnp.arange(experts, dtype=jnp.int32)
-    hits = routed[None] == names[:, None, None]
-    named = jnp.any(hits, axis=1)
-    busiest = jnp.argmax(jnp.sum(named.astype(jnp.int32), axis=1)).astype(jnp.int32)
-    table = jnp.sum(jnp.where(hits, weight[None], 0.0), axis=1)
-    cold = named & (names != busiest)[:, None]
-    before = jnp.arange(rows)[:, None] < jnp.arange(rows)[None, :]
-    rank = dot(cold.astype(bf16), before.astype(bf16), 1, 0).astype(jnp.int32)
-    slot = jnp.arange(8, dtype=jnp.int32) % 4
-    place = cold[:, None, :] & (rank[:, None, :] == slot[None, :, None])
-    return busiest, hits, table, place
-
-
 def in_vmem(count):
     return [pl.BlockSpec(memory_space=pltpu.VMEM)] * count
 
 
-def pack_kernel(
-    shard_ref, tokens_ref, cotangent_ref, weight_ref, routed_ref, gate_ref, up_ref, down_ref,
-    out_ref, hot_ref, busiest_ref, size
-):
-    rows, features = tokens_ref.shape
-    width = gate_ref.shape[1]
-    units = width // size
-    height, spans = -(-3 * units // 16) * 16, features // 256
-    total = out_ref.shape[0]
-    experts = total // 8
+def tables(routed_ref, weight_ref, experts):
+    rows = routed_ref.shape[1]
+    total = experts * 8
     names = lax.broadcasted_iota(jnp.int32, (experts, rows), 0)
     named = jnp.zeros((experts, rows), f32)
     table = jnp.zeros((experts, rows), f32)
@@ -90,21 +67,14 @@
     counts = jnp.sum(named, axis=1, keepdims=True)
     busy = counts == jnp.max(counts, axis=0, keepdims=True)
     busiest = jnp.max(jnp.where(busy, names, 0)[:, :1], axis=0, keepdims=True)
-    busiest_ref[...] = jnp.broadcast_to(busiest, busiest_ref.shape)
     cold = jnp.where(busy, 0.0, named)
-    square = (rows, rows)
-    first = lax.broadcasted_iota(jnp.int32, square, 0)
-    second = lax.broadcasted_iota(jnp.int32, square, 1)
+    first = lax.broadcasted_iota(jnp.int32, (rows, rows), 0)
+    second = lax.broadcasted_iota(jnp.int32, (rows, rows), 1)
     before = jnp.where(first < second, 1.0, 0.0)
     rank = dot(cold.astype(bf16), before.astype(bf16), 1, 0)
     code = jnp.where(cold > 0.0, rank + 1.0, 0.0)
     hot_row = jnp.sum(jnp.where(busy, table, 0.0), axis=0, keepdims=True)
     hot_weight = jnp.sum(jnp.where(first == second, hot_row, 0.0), axis=1, keepdims=True)
-    tokens = tokens_ref[...]
-    cotangent = cotangent_ref[...]
-    hot_ref[:, :features] = tokens
-    hot_ref[:, features:] = (hot_weight * cotangent.astype(f32)).astype(bf16)
-
     owner = lax.broadcasted_iota(jnp.int32, (total, experts), 0) // 8
     spread = owner == lax.broadcasted_iota(jnp.int32, (total, experts), 1)
     spread = jnp.where(spread, 1.0, 0.0)
@@ -113,7 +83,37 @@
     row = lax.broadcasted_iota(jnp.int32, (total, rows), 0)
     is_token = row % 8 < 4
     place = code == (row % 4 + 1).astype(f32)
-    slot_weight = jnp.sum(jnp.where(place, table, 0.0), axis=1, keepdims=True)
+    return hot_weight, busiest, place, is_token, jnp.where(place, table, 0.0)
+
+
+def pack_kernel(
+    shard_ref, routed_hbm, weight_hbm, tokens_hbm, cotangent_hbm, gate_hbm, up_hbm, down_hbm, out_ref, hot_ref, busiest_ref,
+    tokens_ref, cotangent_ref, weight_ref, routed_ref, gate_ref, up_ref, down_ref, sems, size
+):
+    moves = []
+    sources = (routed_hbm, weight_hbm, tokens_hbm, cotangent_hbm, gate_hbm, up_hbm, down_hbm)
+    targets = (routed_ref, weight_ref, tokens_ref, cotangent_ref, gate_ref, up_ref, down_ref)
+    for index, (source, target) in enumerate(zip(sources, targets)):
+        moves.append(pltpu.make_async_copy(source, target, sems.at[index]))
+        moves[index].start()
+    rows, features = tokens_ref.shape
+    width = gate_ref.shape[1]
+    units = width // size
+    height, spans = -(-3 * units // 16) * 16, features // 256
+    total = out_ref.shape[0]
+    experts = total // 8
+    moves[0].wait()
+    moves[1].wait()
+    hot_weight, busiest, place, is_token, spots = tables(routed_ref, weight_ref, experts)
+    busiest_ref[...] = jnp.broadcast_to(busiest, busiest_ref.shape)
+    moves[2].wait()
+    moves[3].wait()
+    tokens = tokens_ref[...]
+    cotangent = cotangent_ref[...]
+    hot_ref[:, :features] = tokens
+    hot_ref[:, features:] = (hot_weight * cotangent.astype(f32)).astype(bf16)
+
+    slot_weight = jnp.sum(spots, axis=1, keepdims=True)
     factor = jnp.where(is_token[:, :1], 1.0, slot_weight)
     place = jnp.where(place, 1.0, 0.0)
     picked = dot(jnp.where(is_token, place, 0.0).astype(bf16), tokens, 1, 0)
@@ -123,6 +123,8 @@
     unit = shard_ref[0] * units + lax.broadcasted_iota(jnp.int32, (units, width), 0)
     choose = unit == lax.broadcasted_iota(jnp.int32, (units, width), 1)
     choose = jnp.where(choose, 1.0, 0.0).astype(bf16)
+    for move in moves[4:]:
+        move.wait()
     pieces = [
         dot(choose, gate_ref[...], 1, 1),
         dot(choose, up_ref[...], 1, 1),
@@ -148,10 +150,21 @@
             jax.ShapeDtypeStruct((rows, 2 * features), bf16),
             jax.ShapeDtypeStruct((8, 128), jnp.int32),
         ),
-        in_specs=[pl.BlockSpec(memory_space=pltpu.SMEM)] + in_vmem(7),
+        in_specs=[pl.BlockSpec(memory_space=pltpu.SMEM)]
+        + [pl.BlockSpec(memory_space=pl.ANY)] * 7,
         out_specs=tuple(in_vmem(3)),
+        scratch_shapes=[
+            pltpu.VMEM((rows, features), bf16),
+            pltpu.VMEM((rows, features), bf16),
+            pltpu.VMEM(weight.shape, f32),
+            pltpu.VMEM(routed.shape, jnp.int32),
+            pltpu.VMEM(gate.shape, bf16),
+            pltpu.VMEM(up.shape, bf16),
+            pltpu.VMEM(down.shape, bf16),
+            pltpu.SemaphoreType.DMA((7,)),
+        ],
         compiler_params=pltpu.CompilerParams(vmem_limit_bytes=48 * 2**20),
-    )(shard, tokens, cotangent, weight, routed, gate, up, down)
+    )(shard, routed, weight, tokens, cotangent, gate, up, down)
 
 
 def join_kernel(own_kept, own_came, hot_kept, hot_came, joined_ref, pair_ref):
@@ -197,18 +210,17 @@
 
 
 def total_kernel(parts_ref, out_ref):
-    total = jnp.sum(parts_ref[...].astype(f32), axis=0, keepdims=True).astype(bf16)
-    out_ref[...] = jnp.broadcast_to(total, out_ref.shape)
-
-
-def total(back, half):
-    shape = (back.shape[0], 8, 256)
+    half = parts_ref.shape[2] - 256
+    sums = jnp.sum(parts_ref[:, :, half:].astype(f32), axis=0, keepdims=True).astype(bf16)
+    out_ref[...] = jnp.broadcast_to(sums, out_ref.shape)
+
+
+def total(back):
     return pl.pallas_call(
         total_kernel,
-        grid=(1,),
-        in_specs=[pl.BlockSpec(shape, lambda i: (0, 0, half // 256))],
-        out_specs=pl.BlockSpec(shape, lambda i: (0, 0, 0)),
-        out_shape=jax.ShapeDtypeStruct(shape, bf16),
+        in_specs=in_vmem(1),
+        out_specs=in_vmem(1)[0],
+        out_shape=jax.ShapeDtypeStruct((back.shape[0], 8, 256), bf16),
     )(back)
 
 
@@ -275,20 +287,28 @@
     )(core, rows, gate, up, down)
 
 
-def hot_kernel(units, core_ref, rows_ref, blocks_ref, kept_ref, passed_ref, grads_ref, part, pair_part):
+def hot_kernel(
+    units, core_ref, rows_hbm, blocks_ref, kept_ref, passed_ref, grads_ref, part, pair_part, inputs_ref, scaled_ref, sems
+):
     features = part.shape[1]
     depth = kept_ref.shape[0]
     group = part.shape[0] // (2 * depth)
     spans = features // 256
     height = -(-3 * units // 16) * 16
     core = core_ref[0]
-    inputs = rows_ref[:, :features]
-    scaled = rows_ref[:, features:]
+    first = pltpu.make_async_copy(rows_hbm.at[:, :features], inputs_ref, sems.at[0])
+    second = pltpu.make_async_copy(rows_hbm.at[:, features:], scaled_ref, sems.at[1])
+    first.start()
+    second.start()
     sliced = jnp.concatenate(
         [blocks_ref[span * height : span * height + height, :] for span in range(spans)], axis=1
     )
     down = sliced[2 * units :]
+    first.wait()
+    inputs = inputs_ref[...]
     both = dot(sliced[: 2 * units], inputs, 1, 1)
+    second.wait()
+    scaled = scaled_ref[...]
     upstream = dot(down, scaled, 1, 1)[:units]
     gate_value, up_value = both[:units], both[units:]
     sigmoid = jax.nn.sigmoid(gate_value)
@@ -334,11 +354,128 @@
     return pl.pallas_call(
         functools.partial(hot_kernel, units),
         out_shape=(side, side, jax.ShapeDtypeStruct((blocks.shape[0], 128), bf16)),
-        in_specs=[pl.BlockSpec(memory_space=pltpu.SMEM)] + in_vmem(2),
+        in_specs=[pl.BlockSpec(memory_space=pltpu.SMEM), pl.BlockSpec(memory_space=pl.ANY)]
+        + in_vmem(1),
         out_specs=tuple(in_vmem(3)),
-        scratch_shapes=[pltpu.VMEM((total, features), f32), pltpu.VMEM((features, 128), f32)],
+        scratch_shapes=[
+            pltpu.VMEM((total, features), f32),
+            pltpu.VMEM((features, 128), f32),
+            pltpu.VMEM((total, features), bf16),
+            pltpu.VMEM((total, features), bf16),
+            pltpu.SemaphoreType.DMA((2,)),
+        ],
         compiler_params=pltpu.CompilerParams(vmem_limit_bytes=48 * 2**20),
     )(core, gathered, blocks)
+
+
+def middle_kernel(
+    units, routed_ref, weight_ref, cotangent_ref, back_ref, summed_ref,
+    layer_ref, route_ref, gate_ref, up_ref, down_ref, spread_ref
+):
+    rows, features = cotangent_ref.shape
+    half = features // 2
+    strip, width = gate_ref.shape
+    experts = back_ref.shape[0] // 8
+    hot_weight, busiest, place, is_token, spots = tables(routed_ref, weight_ref, experts)
+    cotangent = cotangent_ref[...]
+    results = back_ref[:, :half]
+    own_rows = summed_ref.shape[0] - rows * (features // 128)
+    blocks = [
+        summed_ref[own_rows + i * rows : own_rows + (i + 1) * rows, :]
+        for i in range(features // 128)
+    ]
+    hot_out = jnp.concatenate(blocks, axis=1).astype(f32)
+    sides = []
+    for side in (jnp.where(is_token, spots, 0.0), jnp.where(is_token, 0.0, spots)):
+        high = side.astype(bf16)
+        low = (side - high.astype(f32)).astype(bf16)
+        sides.append(dot(high, results, 0, 0) + dot(low, results, 0, 0))
+    layer = jnp.concatenate(sides, axis=1) + hot_weight * hot_out
+    layer_ref[...] = layer.astype(bf16)
+
+    left = dot(results, cotangent[:, :half], 1, 1)
+    right = dot(results, cotangent[:, half:], 1, 1)
+    products = jnp.where(place, jnp.where(is_token, left, right), 0.0)
+    hot_column = jnp.sum(hot_out * cotangent.astype(f32), axis=1, keepdims=True)
+    first = lax.broadcasted_iota(jnp.int32, (rows, rows), 0)
+    second = lax.broadcasted_iota(jnp.int32, (rows, rows), 1)
+    hot_row = jnp.sum(jnp.where(first == second, hot_column, 0.0), axis=0, keepdims=True)
+    owner = lax.broadcasted_iota(jnp.int32, products.shape, 0) // 8
+    for k in range(routed_ref.shape[0]):
+        named = routed_ref[k : k + 1, :]
+        cold = jnp.sum(jnp.where(owner == named, products, 0.0), axis=0, keepdims=True)
+        route_ref[k : k + 1, :] = cold + jnp.where(named == busiest, hot_row, 0.0)
+
+    lanes = width // 128
+    for index, ref in enumerate((gate_ref, up_ref)):
+        for lane in range(lanes):
+            at = (index * lanes + lane) * strip
+            ref[:, lane * 128 : lane * 128 + 128] = summed_ref[at : at + strip, :].astype(f32)
+    base = 2 * lanes * strip
+    unpair(down_ref, summed_ref, base, 0, units)
+
+    shape = (spread_ref.shape[0], 2 * width)
+    lane = lax.broadcasted_iota(jnp.int32, (shape[0], 1), 0)
+    within = lane % 128
+    column = (within % (2 * units)) // units * width + within % units
+    column = column + (lane // 128 * 2 + within // (2 * units)) * units
+    column = jnp.where(within < 4 * units, column, -1)
+    match = lax.broadcasted_iota(jnp.int32, shape, 1) == column
+    spread_ref[...] = jnp.where(match, 1.0, 0.0).astype(bf16)
+
+
+def unpair(out_ref, from_ref, base, lane_base, units):
+    for lane in range(0, out_ref.shape[1] // 128, 2):
+        at = base + lane * units
+        pair = from_ref[at : at + 2 * units, lane_base : lane_base + 128].astype(f32)
+        out_ref[:, lane * 128 : lane * 128 + 128] = pair[:units]
+        out_ref[:, lane * 128 + 128 : lane * 128 + 256] = pair[units:]
+
+
+def middle(routed, weight, cotangent, back, summed, units, strip, depth):
+    rows, features = cotangent.shape
+    width = units * 2 * depth
+    return pl.pallas_call(
+        functools.partial(middle_kernel, units),
+        out_shape=(
+            jax.ShapeDtypeStruct((rows, features), bf16),
+            jax.ShapeDtypeStruct(weight.shape, f32),
+            jax.ShapeDtypeStruct((strip, width), f32),
+            jax.ShapeDtypeStruct((strip, width), f32),
+            jax.ShapeDtypeStruct((units, features), f32),
+            jax.ShapeDtypeStruct((depth * 128, 2 * width), bf16),
+        ),
+        in_specs=in_vmem(5),
+        out_specs=tuple(in_vmem(6)),
+        compiler_params=pltpu.CompilerParams(vmem_limit_bytes=48 * 2**20),
+    )(routed, weight, cotangent, back, summed)
+
+
+def last_kernel(
+    units, home_ref, blocks_ref, gate_ref, up_ref, down_ref, spread_ref,
+    gate_out, up_out, down_out, scratch
+):
+    strip, width = gate_ref.shape
+    depth = spread_ref.shape[0] // 128
+    home = home_ref[0] == 1
+    blocks = [blocks_ref[z * strip : (z + 1) * strip, :128] for z in range(depth)]
+    pair = dot(jnp.concatenate(blocks, axis=1), spread_ref[...], 1, 0)
+    gate_out[...] = gate_ref[...] + jnp.where(home, pair[:, :width], 0.0)
+    up_out[...] = up_ref[...] + jnp.where(home, pair[:, width:], 0.0)
+    unpair(scratch, blocks_ref, 0, 128, units)
+    down_out[...] = down_ref[...] + jnp.where(home, scratch[...], 0.0)
+
+
+def last(home, blocks, gate, up, down, spread):
+    units = down.shape[0]
+    return pl.pallas_call(
+        functools.partial(last_kernel, units),
+        out_shape=tuple(jax.ShapeDtypeStruct(x.shape, f32) for x in (gate, up, down)),
+        in_specs=[pl.BlockSpec(memory_space=pltpu.SMEM)] + in_vmem(5),
+        out_specs=tuple(in_vmem(3)),
+        scratch_shapes=[pltpu.VMEM(down.shape, f32)],
+        compiler_params=pltpu.CompilerParams(vmem_limit_bytes=48 * 2**20),
+    )(home, blocks, gate, up, down, spread)
 
 
 def on_device(
@@ -378,10 +515,6 @@
         (arrived, picked, routed_experts.T, route_weight.T)
     )
     blocks = plane_exchange(picked)
-    busiest, hits, table, place = routing(routed, weight, experts)
-    is_token = (jnp.arange(8) < 4)[None, :, None]
-    hot_weight = lax.dynamic_index_in_dim(table, busiest, 0, keepdims=False)
-    wide_cotangent = cotangent.astype(f32)
     returning, own_kept, own_passed = own_expert(
         core_word, arrived.reshape(experts * 8, features + 256), gate, up, down, depth
     )
@@ -393,10 +526,6 @@
     hot_came = core_swap(hot_passed)
     joined, pair = join(own_kept, own_came, hot_kept, hot_came, strip)
     summed = z_reduce_scatter(joined)[0]
-    own_rows = own_kept.shape[1]
-    own_sum = summed[:own_rows].astype(f32)
-    hot_out = summed[own_rows:].reshape(features // 128, rows, 128)
-    hot_out = hot_out.transpose(1, 0, 2).reshape(rows, features)
     pair = pad_blocks(z_exchange(pair).reshape(depth * strip // 8, 8, 128), experts)
 
     back = plane_exchange(
@@ -404,54 +533,21 @@
             [returning.reshape(experts, 8, half), pair, hot_grads.reshape(experts, 8, 128)], axis=2
         )
     )
-    hot_blocks = plane_exchange(total(back, half))
-
-    lane = np.arange(depth * 128)
-    within = lane % 128
-    column = (within % (2 * units)) // units * width
-    column = column + (lane // 128 * 2 + within // (2 * units)) * units + within % units
-    column = np.where(within < 4 * units, column, -1).astype(np.int32)
-    spread = (jnp.asarray(column)[:, None] == jnp.arange(2 * width, dtype=jnp.int32)).astype(bf16)
-    hot_pair = hot_blocks[: depth * strip // 8, :, :128].reshape(depth, strip, 128)
-    hot_pair = dot(hot_pair.transpose(1, 0, 2).reshape(strip, depth * 128), spread, 1, 0)
-    hot_down = hot_blocks.reshape(experts * 8, 256)[: features // 128 * units, 128:]
-    hot_down = hot_down.reshape(features // 128, units, 128).transpose(1, 0, 2)
-    hot_down = hot_down.reshape(units, features).astype(f32)
-
-    results = back[:, :, :half].reshape(experts * 8, half)
-    weighting = jnp.where(place, table[:, None, :], 0.0)
-    halves = jnp.concatenate(
-        [jnp.where(is_token, weighting, 0.0), jnp.where(is_token, 0.0, weighting)], axis=2
-    ).reshape(experts * 8, 2 * rows)
-    weighed = dot(halves, results.astype(f32), 0, 0, highest)
-    wide_hot = hot_out.astype(f32)
-    layer_out = jnp.concatenate([weighed[:rows], weighed[rows:]], axis=1)
-    layer_out = (layer_out + hot_weight[:, None] * wide_hot).astype(bf16)
-
-    products = jnp.where(
-        is_token,
-        dot(results, cotangent[:, :half], 1, 1).reshape(experts, 8, rows),
-        dot(results, cotangent[:, half:], 1, 1).reshape(experts, 8, rows),
-    )
-    by_expert = jnp.sum(jnp.where(place, products, 0.0), axis=1)
-    hot_product = jnp.sum(wide_hot * wide_cotangent, axis=1)
-    is_busiest = jnp.arange(experts, dtype=jnp.int32)[:, None] == busiest
-    by_expert = by_expert + jnp.where(is_busiest, hot_product[None], 0.0)
-    route_gradient = jnp.sum(jnp.where(hits, by_expert[:, None, :], 0.0), axis=0).T
-
-    def unstripe(block, tall):
-        return block.reshape(-1, tall, 128).transpose(1, 0, 2).reshape(tall, -1)
-
-    count = strip * width // 128
-    home = mine == busiest
-    gate_gradient = unstripe(own_sum[:count], strip) + jnp.where(
-        home, hot_pair[:, :width], 0.0
-    )
-    up_gradient = unstripe(own_sum[count : 2 * count], strip) + jnp.where(
-        home, hot_pair[:, width:], 0.0
-    )
-    down_gradient = unstripe(own_sum[2 * count :], units) + jnp.where(home, hot_down, 0.0)
-    return (layer_out, route_gradient, gate_gradient[None], up_gradient[None], down_gradient[None])
+    hot_blocks = plane_exchange(total(back))
+    layer_out, route_gradient, own_gate, own_up, own_down, spread = middle(
+        routed, weight, cotangent, back.reshape(experts * 8, -1), summed, units, strip, depth
+    )
+    home = (mine == found[0, 0]).astype(jnp.int32).reshape(1)
+    gate_gradient, up_gradient, down_gradient = last(
+        home, hot_blocks.reshape(experts * 8, 256), own_gate, own_up, own_down, spread
+    )
+    return (
+        layer_out,
+        route_gradient.T,
+        gate_gradient[None],
+        up_gradient[None],
+        down_gradient[None],
+    )
 
 
 def solution(mesh):

time: 195 us -> 188 us (0.964)
  blocking collectives: 25.5 us -> 52.3 us
  waiting for transfers between devices: 60.2 us -> 41.4 us
  other arithmetic: 6.68 us -> 0.06 us
  starting transfers between devices: 50.2 us -> 43.9 us
  Pallas kernels: 16 us -> 22.3 us
  matrix products: 3.09 us -> 0 us
  local copies, waits for them, and re-layouts: 13.5 us -> 11.3 us
  between operations: 17 us -> 14.9 us
    all_to_all x0 -> x1, blocking collectives: none -> 26.8 us  [plane_exchange(): lax.all_to_all(blocks, 'expert', split_axis=0, concat_axis=0, tiled=True)]
    all_to_all x4 -> x3, waiting for transfers between devices: 58 us -> 39.3 us  [plane_exchange(): lax.all_to_all(blocks, 'expert', split_axis=0, concat_axis=0, tiled=True)]
    all_to_all x4 -> x3, starting transfers between devices: 42.8 us -> 36.5 us  [plane_exchange(): lax.all_to_all(blocks, 'expert', split_axis=0, concat_axis=0, tiled=True)]
    pallas_call x1 -> x3, Pallas kernels: 1.73 us -> 6.42 us  [the longest x1 3.29 us: middle(): pl.pallas_call(functools.partial(middle_kernel, units), out_shape=(jax.Sh...]
    dot_general x5 -> x0, matrix products: 3.09 us -> none  [dot(): lax.dot_general(lhs, rhs, dims, precision=precision, preferred_element_ty...]
    unnamed x40 -> x38, local copies, waits for them, and re-layouts: 10.8 us -> 10.8 us
  transfers between devices with their start and end apart: 8 -> 7, of which waited for: 5 -> 4; matrix products, arithmetic and copies ran while one was open for 3% -> 0% of each run, Pallas kernels for 6% -> 8%
where the time goes in v4:
time: 188 us; the launch traced here: 186 us
  blocking collectives  52.3 us (28%)
  starting transfers between devices  43.9 us (23%)
  waiting for transfers between devices  41.4 us (22%)
  Pallas kernels  22.3 us (12%)
  between operations  14.9 us (8%)
  local copies, waits for them, and re-layouts  11.3 us (6%)
    all_to_all x3, waiting for transfers between devices, plane_exchange(): lax.all_to_all(blocks, 'expert', split_axis=0, concat_axis=0, tiled=True)  39.3 us
    all_to_all x3, starting transfers between devices, plane_exchange(): lax.all_to_all(blocks, 'expert', split_axis=0, concat_axis=0, tiled=True)  36.5 us
    all_to_all x1, blocking collectives, plane_exchange(): lax.all_to_all(blocks, 'expert', split_axis=0, concat_axis=0, tiled=True)  26.8 us
    all_to_all x1, blocking collectives, z_exchange(): lax.all_to_all(blocks, 'dp', split_axis=0, concat_axis=0, tiled=True, axi...  25.5 us
    unnamed x38, local copies, waits for them, and re-layouts  10.8 us
    ppermute x2, starting transfers between devices, core_swap(): return lax.ppermute(block, 'dp', [(i, i ^ 1) for i in range(size)])  7.39 us
    pallas_call x1, Pallas kernels, own_expert(): pl.pallas_call(own_kernel, out_shape=(jax.ShapeDtypeStruct((rows.shape[0]...  5.41 us
    pallas_call x1, Pallas kernels, pack(): pl.pallas_call(functools.partial(pack_kernel, size=size), out_shape=(jax....  3.8 us
  transfers between devices with their start and end apart: 7, of which 4 were waited for; matrix products, arithmetic and copies ran while one was open for 0% of the time, Pallas kernels for 8%

profile of v4, /device:TPU:1, one launch (start us, length us, event | category | flops | bytes accessed | tf_op | source)
XLA Modules:
  0.0 186.3 jit_solution(9920311058760825699)
XLA Ops:
  7.2 1.1 copy-done.1
  8.4 1.1 copy-done.3
  9.5 1.1 copy-done.5
  10.6 0.8 copy-done.10
  11.5 0.8 copy-done.13
  12.3 0.7 copy-done.14
  13.0 0.7 copy-done.16
  13.7 3.8 %shard_map.110 = (bf16[512,1280]{1,0:T(8,128)(2,1)}, bf16[32,2048]{1,0:T(8,128)(2,1)}, s32[8,128]{1,0:T(8,128)S(1)}) custom-call(s32[1]{0:T(128)} %bitcast.shard_ref, s32[8,32]{1,0:T(8,128)S(1)} %bitcast.34, f32[8,32]{1,0:T(8,128)S(1)} %bitcast.36, bf16[32,1024]{1,0:T(8,128)(2,1)S(1)} %copy-done.13, bf16[32,1024]{1,0:T(8,128)(2,1)S(1)} %copy-done.10, ...), custom_call_target="tpu_custom_call" | custom-call | tf_op jit(solution)/shard_map/pallas_call | solution.py:146
  17.5 14.4 %all-to-all-start = ((bf16[64,8,1280]{2,1,0:T(8,128)(2,1)}), bf16[64,8,1280]{2,1,0:T(8,128)(2,1)}, u32[]{:S(2)}, u32[]{:S(2)}) async-start(bf16[64,8,1280]{2,1,0:T(8,128)(2,1)} %bitcast.6), calls=%async_computation | async-start | bytes 2621440 | tf_op jit(solution)/shard_map/all_to_all | solution.py:21
  32.0 0.5 slice.4
  32.5 26.9 %all-to-all-done.piece_ref = bf16[64,8,1280]{2,1,0:T(8,128)(2,1)} async-done(((bf16[64,8,1280]{2,1,0:T(8,128)(2,1)}), bf16[64,8,1280]{2,1,0:T(8,128)(2,1)}, u32[]{:S(2)}, u32[]{:S(2)}) %all-to-all-start) | async-done | bytes 1310752 | tf_op jit(solution)/shard_map/all_to_all | solution.py:21
  59.4 2.0 %shard_map.111 = bf16[64,8,256]{2,1,0:T(8,128)(2,1)} custom-call(s32[1]{0:T(128)} %bitcast.7.busiest_ref, bf16[64,8,1280]{2,1,0:T(8,128)(2,1)} %all-to-all-done.piece_ref), custom_call_target="tpu_custom_call" | custom-call | tf_op jit(solution)/shard_map/pallas_call | solution.py:207
  61.5 13.3 %all-to-all-start.1 = ((bf16[64,8,256]{2,1,0:T(8,128)(2,1)}), bf16[64,8,256]{2,1,0:T(8,128)(2,1)}, u32[]{:S(2)}, u32[]{:S(2)}) async-start(bf16[64,8,256]{2,1,0:T(8,128)(2,1)} %shard_map.111), calls=%async_computation.1 | async-start | bytes 524288 | tf_op jit(solution)/shard_map/all_to_all | solution.py:21
  74.9 5.4 %shard_map.112 = (bf16[512,512]{1,0:T(8,128)(2,1)S(1)}, bf16[8,576,128]{2,1,0:T(8,128)(2,1)S(1)}, bf16[8,576,128]{2,1,0:T(8,128)(2,1)S(1)}) custom-call(s32[1]{0:T(128)} %bitcast.8.core_ref, bf16[512,1280]{1,0:T(8,128)(2,1)} %bitcast.9.rows_ref, bf16[1024,384]{1,0:T(8,128)(2,1)S(1)} %bitcast.25, bf16[1024,384]{1,0:T(8,128)(2,1)S(1)} %bitcast.27, ...), custom_call_target="tpu_custom_call" | custom-call | tf_op jit(solution)/shard_map/pallas_call | solution.py:280
  80.3 0.8 copy-done.8
  81.1 1.0 copy-done.18
  82.2 5.0 %all-to-all-done.1 = bf16[64,8,256]{2,1,0:T(8,128)(2,1)} async-done(((bf16[64,8,256]{2,1,0:T(8,128)(2,1)}), bf16[64,8,256]{2,1,0:T(8,128)(2,1)}, u32[]{:S(2)}, u32[]{:S(2)}) %all-to-all-start.1) | async-done | bytes 262176 | tf_op jit(solution)/shard_map/all_to_all | solution.py:21
  87.1 5.5 %collective-permute-start = (bf16[8,576,128]{2,1,0:T(8,128)(2,1)}, bf16[8,576,128]{2,1,0:T(8,128)(2,1)S(1)}, u32[]{:S(2)}, u32[]{:S(2)}) collective-permute-start(bf16[8,576,128]{2,1,0:T(8,128)(2,1)} %copy-done.18), channel_id=1, source_target_pairs={{0,64},{64,0},{128,192},{192,128},{256,320},{320,256},{384,448},{4... | collective-permute-start | bytes 3538952 | tf_op jit(solution)/shard_map/ppermute | solution.py:26
  92.6 1.6 copy-done.7
  94.2 3.0 %shard_map.113 = (bf16[8,320,128]{2,1,0:T(8,128)(2,1)S(1)}, bf16[8,320,128]{2,1,0:T(8,128)(2,1)S(1)}, bf16[512,128]{1,0:T(8,128)(2,1)S(1)}) custom-call(s32[1]{0:T(128)} %bitcast.8.core_ref, bf16[512,2048]{1,0:T(8,128)(2,1)S(1)} %copy-done.7, bf16[512,256]{1,0:T(8,128)(2,1)} %bitcast.11.blocks_ref), custom_call_target="tpu_custom_call" | custom-call | tf_op jit(solution)/shard_map/pallas_call | solution.py:354
  97.2 1.9 %collective-permute-start.1 = (bf16[8,320,128]{2,1,0:T(8,128)(2,1)S(1)}, bf16[8,320,128]{2,1,0:T(8,128)(2,1)S(1)}, u32[]{:S(2)}, u32[]{:S(2)}) collective-permute-start(bf16[8,320,128]{2,1,0:T(8,128)(2,1)S(1)} %get-tuple-element.44), channel_id=1, source_target_pairs={{0,64},{64,0},{128,192},{192,128},{256,320},{320,256},{384,448},{4... | collective-permute-start | bytes 1966088 | tf_op jit(solution)/shard_map/ppermute | solution.py:26
  99.2 2.1 %collective-permute-done.1.hot_came = bf16[8,320,128]{2,1,0:T(8,128)(2,1)S(1)} collective-permute-done((bf16[8,320,128]{2,1,0:T(8,128)(2,1)S(1)}, bf16[8,320,128]{2,1,0:T(8,128)(2,1)S(1)}, u32[]{:S(2)}, u32[]{:S(2)}) %collective-permute-start.1) | collective-permute-done | bytes 655392 | tf_op jit(solution)/shard_map/ppermute | solution.py:26
  101.2 1.6 shard_map.114
  102.8 25.5 %all_to_all.25 = bf16[8,64,128]{2,1,0:T(8,128)(2,1)S(1)} all-to-all(bf16[8,64,128]{2,1,0:T(8,128)(2,1)S(1)} %get-tuple-element.45), channel_id=1, replica_groups={{0,128,256,384,512,640,768,896},{64,192,320,448,576,704,832,960},{1,129..., dimensions={0} | all-to-all | bytes 262144 | tf_op jit(solution)/shard_map/all_to_all | solution.py:32
  128.4 0.1 pad_maximum_fusion
  128.5 26.8 %all_to_all.26.parts_ref = bf16[64,8,768]{2,1,0:T(8,128)(2,1)} all-to-all(bf16[64,8,768]{2,1,0:T(8,128)(2,1)S(1)} %pad_maximum_fusion), channel_id=1, replica_groups=mesh['dp'=16,'expert'=64] {'expert'}, dimensions={0} | all-to-all | bytes 1572864 | tf_op jit(solution)/shard_map/all_to_all | solution.py:21
  155.3 2.0 %shard_map.116 = bf16[64,8,256]{2,1,0:T(8,128)(2,1)} custom-call(bf16[64,8,768]{2,1,0:T(8,128)(2,1)} %all_to_all.26.parts_ref), custom_call_target="tpu_custom_call" | custom-call | tf_op jit(solution)/shard_map/pallas_call | solution.py:219
  157.3 8.7 %all-to-all-start.4 = ((bf16[64,8,256]{2,1,0:T(8,128)(2,1)}), bf16[64,8,256]{2,1,0:T(8,128)(2,1)S(1)}, u32[]{:S(2)}, u32[]{:S(2)}) async-start(bf16[64,8,256]{2,1,0:T(8,128)(2,1)} %shard_map.116), calls=%async_computation.5 | async-start | bytes 524288 | tf_op jit(solution)/shard_map/all_to_all | solution.py:21
  166.8 0.9 copy-done.12
  167.7 3.3 %shard_map.115 = (bf16[32,1024]{1,0:T(8,128)(2,1)}, f32[8,32]{1,0:T(8,128)}, f32[64,384]{1,0:T(8,128)S(1)}, f32[64,384]{1,0:T(8,128)S(1)}, f32[24,1024]{1,0:T(8,128)S(1)}, /*index=5*/bf16[1024,768]{1,0:T(8,128)(2,1)S(1)}) custom-call(s32[8,32]{1,0:T(8,128)S(1)} %bitcast.35, f32[8,32]{1,0:T(8,128)S(1)} %bitcast.37, bf16[32,1024]{1,0:T(8,128)(2,1)S(1)} %copy-done.11, ...), custom_call_target="tpu_custom_call" | custom-call | tf_op jit(solution)/shard_map/pallas_call | solution.py:438
  171.0 7.4 %all-to-all-done.4 = bf16[64,8,256]{2,1,0:T(8,128)(2,1)S(1)} async-done(((bf16[64,8,256]{2,1,0:T(8,128)(2,1)}), bf16[64,8,256]{2,1,0:T(8,128)(2,1)S(1)}, u32[]{:S(2)}, u32[]{:S(2)}) %all-to-all-start.4) | async-done | bytes 262176 | tf_op jit(solution)/shard_map/all_to_all | solution.py:21
  178.4 1.1 shard_map.117
  (34 shorter events, 0.2 us)
Async XLA Ops:
  7.2 85.5 %all-gather.2.cloned.1.call-start = ((), (), s32[]{:S(2)}) async-start(), calls=%async_computation.6 | async-start | bytes 2228224 | tf_op jit(solution)/shard_map/all_gather | solution.py:511
  7.2 1.1 copy-start.1
  8.4 1.1 copy-start.3
  9.5 1.1 copy-start.5
  10.6 0.8 copy-start.10
  11.5 0.8 copy-start.13
  12.3 0.7 copy-start.14
  13.0 0.7 copy-start.16
  17.5 57.4 %copy-start.6 = (bf16[1,384,1024]{2,1,0:T(8,128)(2,1)S(1)}, bf16[1,384,1024]{2,1,0:T(8,128)(2,1)}, u32[]{:S(2)}) copy-start(bf16[1,384,1024]{2,1,0:T(8,128)(2,1)} %param.13) | copy-start | bytes 2359300
  17.5 41.9 %all-to-all-start = ((bf16[64,8,1280]{2,1,0:T(8,128)(2,1)}), bf16[64,8,1280]{2,1,0:T(8,128)(2,1)}, u32[]{:S(2)}, u32[]{:S(2)}) async-start(bf16[64,8,1280]{2,1,0:T(8,128)(2,1)} %bitcast.6), calls=%async_computation | async-start | bytes 2621440 | tf_op jit(solution)/shard_map/all_to_all | solution.py:21
  31.9 42.9 %copy-start.2 = (bf16[1,1024,384]{2,1,0:T(8,128)(2,1)S(1)}, bf16[1,1024,384]{2,1,0:T(8,128)(2,1)}, u32[]{:S(2)}) copy-start(bf16[1,1024,384]{2,1,0:T(8,128)(2,1)} %param.11) | copy-start | bytes 2359300
  31.9 42.9 %copy-start.4 = (bf16[1,1024,384]{2,1,0:T(8,128)(2,1)S(1)}, bf16[1,1024,384]{2,1,0:T(8,128)(2,1)}, u32[]{:S(2)}) copy-start(bf16[1,1024,384]{2,1,0:T(8,128)(2,1)} %param.12) | copy-start | bytes 2359300
  61.5 25.7 %all-to-all-start.1 = ((bf16[64,8,256]{2,1,0:T(8,128)(2,1)}), bf16[64,8,256]{2,1,0:T(8,128)(2,1)}, u32[]{:S(2)}, u32[]{:S(2)}) async-start(bf16[64,8,256]{2,1,0:T(8,128)(2,1)} %shard_map.111), calls=%async_computation.1 | async-start | bytes 524288 | tf_op jit(solution)/shard_map/all_to_all | solution.py:21
  74.8 91.9 %reduce-scatter.2.cloned.1.call-start = ((), (), s32[]{:S(2)}) async-start(), calls=%async_computation.7 | async-start | bytes 1916928 | tf_op jit(solution)/shard_map/reduce_scatter | solution.py:40
  80.3 0.8 copy-start.8
  81.1 1.0 copy-start.18
  87.1 12.0 %collective-permute-start = (bf16[8,576,128]{2,1,0:T(8,128)(2,1)}, bf16[8,576,128]{2,1,0:T(8,128)(2,1)S(1)}, u32[]{:S(2)}, u32[]{:S(2)}) collective-permute-start(bf16[8,576,128]{2,1,0:T(8,128)(2,1)} %copy-done.18), channel_id=1, source_target_pairs={{0,64},{64,0},{128,192},{192,128},{256,320},{320,256},{384,448},{4... | collective-permute-start | bytes 3538952 | tf_op jit(solution)/shard_map/ppermute | solution.py:26
  92.6 1.6 copy-start.7
  97.2 4.0 %collective-permute-start.1 = (bf16[8,320,128]{2,1,0:T(8,128)(2,1)S(1)}, bf16[8,320,128]{2,1,0:T(8,128)(2,1)S(1)}, u32[]{:S(2)}, u32[]{:S(2)}) collective-permute-start(bf16[8,320,128]{2,1,0:T(8,128)(2,1)S(1)} %get-tuple-element.44), channel_id=1, source_target_pairs={{0,64},{64,0},{128,192},{192,128},{256,320},{320,256},{384,448},{4... | collective-permute-start | bytes 1966088 | tf_op jit(solution)/shard_map/ppermute | solution.py:26
  102.8 25.6 %copy-start.9 = (bf16[512,512]{1,0:T(8,128)(2,1)S(1)}, bf16[512,512]{1,0:T(8,128)(2,1)}, u32[]{:S(2)}) copy-start(bf16[512,512]{1,0:T(8,128)(2,1)} %copy-done.8) | copy-start | bytes 1572868
  128.4 38.3 %copy-start.11 = (bf16[32,1024]{1,0:T(8,128)(2,1)S(1)}, bf16[32,1024]{1,0:T(8,128)(2,1)}, u32[]{:S(2)}) copy-start(bf16[32,1024]{1,0:T(8,128)(2,1)} %cotangent_ref.1) | copy-start | bytes 196612
  128.4 38.3 %copy-start.15 = (s32[32,8]{0,1:T(8,128)S(1)}, s32[32,8]{0,1:T(8,128)}, u32[]{:S(2)}) copy-start(s32[32,8]{0,1:T(8,128)} %param.10) | copy-start | bytes 3076
  128.5 38.3 %copy-start.17 = (f32[32,8]{0,1:T(8,128)S(1)}, f32[32,8]{0,1:T(8,128)}, u32[]{:S(2)}) copy-start(f32[32,8]{0,1:T(8,128)} %param.9) | copy-start | bytes 3076
  155.3 11.5 %copy-start = (bf16[64,8,768]{2,1,0:T(8,128)(2,1)S(1)}, bf16[64,8,768]{2,1,0:T(8,128)(2,1)}, u32[]{:S(2)}) copy-start(bf16[64,8,768]{2,1,0:T(8,128)(2,1)} %all_to_all.26.parts_ref) | copy-start | bytes 2359300
  157.3 21.0 %all-to-all-start.4 = ((bf16[64,8,256]{2,1,0:T(8,128)(2,1)}), bf16[64,8,256]{2,1,0:T(8,128)(2,1)S(1)}, u32[]{:S(2)}, u32[]{:S(2)}) async-start(bf16[64,8,256]{2,1,0:T(8,128)(2,1)} %shard_map.116), calls=%async_computation.5 | async-start | bytes 524288 | tf_op jit(solution)/shard_map/all_to_all | solution.py:21
  166.8 0.9 copy-start.12
Sparse Core Ops, SparseCore 0:
  17.6 59.4 all-gather.1
  103.0 48.7 reduce-scatter.1

commit v5 on v4

--- a/solution.py
+++ b/solution.py
@@ -163,7 +163,7 @@
             pltpu.VMEM(down.shape, bf16),
             pltpu.SemaphoreType.DMA((7,)),
         ],
-        compiler_params=pltpu.CompilerParams(vmem_limit_bytes=48 * 2**20),
+        compiler_params=pltpu.CompilerParams(vmem_limit_bytes=60 * 2**20),
     )(shard, routed, weight, tokens, cotangent, gate, up, down)
 
 
@@ -364,7 +364,7 @@
             pltpu.VMEM((total, features), bf16),
             pltpu.SemaphoreType.DMA((2,)),
         ],
-        compiler_params=pltpu.CompilerParams(vmem_limit_bytes=48 * 2**20),
+        compiler_params=pltpu.CompilerParams(vmem_limit_bytes=59 * 2**20),
     )(core, gathered, blocks)
 
 

time: 188 us -> 184 us (0.979)
  local copies, waits for them, and re-layouts: 11.3 us -> 5.19 us
  Pallas kernels: 22.3 us -> 24.7 us
    unnamed x38 -> x26, local copies, waits for them, and re-layouts: 10.8 us -> 3.88 us
    pallas_call x1, Pallas kernels: 2.99 us -> 4.94 us  [hot_expert(): pl.pallas_call(functools.partial(hot_kernel, units), out_shape=(side, sid...]
  transfers between devices with their start and end apart: 7 -> 7, of which waited for: 4 -> 4; matrix products, arithmetic and copies ran while one was open for 0% -> 1% of each run, Pallas kernels for 8% -> 10%
where the time goes in v5:
time: 184 us; the launch traced here: 182 us
  blocking collectives  52.3 us (28%)
  starting transfers between devices  44 us (24%)
  waiting for transfers between devices  40.8 us (22%)
  Pallas kernels  24.7 us (13%)
  between operations  14.9 us (8%)
  local copies, waits for them, and re-layouts  5.19 us (3%)
    all_to_all x3, waiting for transfers between devices, plane_exchange(): lax.all_to_all(blocks, 'expert', split_axis=0, concat_axis=0, tiled=True)  38.5 us
    all_to_all x3, starting transfers between devices, plane_exchange(): lax.all_to_all(blocks, 'expert', split_axis=0, concat_axis=0, tiled=True)  36.5 us
    all_to_all x1, blocking collectives, plane_exchange(): lax.all_to_all(blocks, 'expert', split_axis=0, concat_axis=0, tiled=True)  26.8 us
    all_to_all x1, blocking collectives, z_exchange(): lax.all_to_all(blocks, 'dp', split_axis=0, concat_axis=0, tiled=True, axi...  25.5 us
    ppermute x2, starting transfers between devices, core_swap(): return lax.ppermute(block, 'dp', [(i, i ^ 1) for i in range(size)])  7.39 us
    pallas_call x1, Pallas kernels, own_expert(): pl.pallas_call(own_kernel, out_shape=(jax.ShapeDtypeStruct((rows.shape[0]...  5.42 us
    pallas_call x1, Pallas kernels, hot_expert(): pl.pallas_call(functools.partial(hot_kernel, units), out_shape=(side, sid...  4.94 us
    pallas_call x1, Pallas kernels, pack(): pl.pallas_call(functools.partial(pack_kernel, size=size), out_shape=(jax....  4.2 us
  transfers between devices with their start and end apart: 7, of which 4 were waited for; matrix products, arithmetic and copies ran while one was open for 1% of the time, Pallas kernels for 10%

profile of v5, /device:TPU:1, one launch (start us, length us, event | category | flops | bytes accessed | tf_op | source)
XLA Modules:
  0.0 181.9 jit_solution(8438334022253848911)
XLA Ops:
  7.2 0.0 all-gather.2.cloned.1.call-start
  7.2 4.2 %shard_map.110 = (bf16[512,1280]{1,0:T(8,128)(2,1)}, bf16[32,2048]{1,0:T(8,128)(2,1)}, s32[8,128]{1,0:T(8,128)}) custom-call(s32[1]{0:T(128)} %bitcast.shard_ref, s32[8,32]{1,0:T(8,128)} %bitcast.33, f32[8,32]{1,0:T(8,128)} %bitcast.35, bf16[32,1024]{1,0:T(8,128)(2,1)} %tokens_hbm.1, bf16[32,1024]{1,0:T(8,128)(2,1)} %cotangent_ref.1, ...), custom_call_target="tpu_custom_call" | custom-call | tf_op jit(solution)/shard_map/pallas_call | solution.py:146
  11.4 0.0 all-gather.2.cloned.1.call-update
  11.5 14.4 %all-to-all-start = ((bf16[64,8,1280]{2,1,0:T(8,128)(2,1)}), bf16[64,8,1280]{2,1,0:T(8,128)(2,1)}, u32[]{:S(2)}, u32[]{:S(2)}) async-start(bf16[64,8,1280]{2,1,0:T(8,128)(2,1)} %bitcast.37), calls=%async_computation | async-start | bytes 2621440 | tf_op jit(solution)/shard_map/all_to_all | solution.py:21
  25.9 1.3 slice.4
  27.2 26.1 %all-to-all-done.piece_ref = bf16[64,8,1280]{2,1,0:T(8,128)(2,1)} async-done(((bf16[64,8,1280]{2,1,0:T(8,128)(2,1)}), bf16[64,8,1280]{2,1,0:T(8,128)(2,1)}, u32[]{:S(2)}, u32[]{:S(2)}) %all-to-all-start) | async-done | bytes 1310752 | tf_op jit(solution)/shard_map/all_to_all | solution.py:21
  53.3 2.1 %shard_map.111 = bf16[64,8,256]{2,1,0:T(8,128)(2,1)} custom-call(s32[1]{0:T(128)} %bitcast.7.busiest_ref, bf16[64,8,1280]{2,1,0:T(8,128)(2,1)} %all-to-all-done.piece_ref), custom_call_target="tpu_custom_call" | custom-call | tf_op jit(solution)/shard_map/pallas_call | solution.py:207
  55.4 13.3 %all-to-all-start.1 = ((bf16[64,8,256]{2,1,0:T(8,128)(2,1)}), bf16[64,8,256]{2,1,0:T(8,128)(2,1)}, u32[]{:S(2)}, u32[]{:S(2)}) async-start(bf16[64,8,256]{2,1,0:T(8,128)(2,1)} %shard_map.111), calls=%async_computation.1 | async-start | bytes 524288 | tf_op jit(solution)/shard_map/all_to_all | solution.py:21
  68.8 0.0 reduce-scatter.2.cloned.1.call-start
  68.9 5.4 %shard_map.112 = (bf16[512,512]{1,0:T(8,128)(2,1)S(1)}, bf16[8,576,128]{2,1,0:T(8,128)(2,1)S(1)}, bf16[8,576,128]{2,1,0:T(8,128)(2,1)S(1)}) custom-call(s32[1]{0:T(128)} %bitcast.8.core_ref, bf16[512,1280]{1,0:T(8,128)(2,1)} %bitcast.9.rows_ref, bf16[1024,384]{1,0:T(8,128)(2,1)S(1)} %bitcast.25, bf16[1024,384]{1,0:T(8,128)(2,1)S(1)} %bitcast.27, ...), custom_call_target="tpu_custom_call" | custom-call | tf_op jit(solution)/shard_map/pallas_call | solution.py:280
  74.3 0.8 copy-done.5
  75.1 1.0 copy-done.11
  76.1 5.0 %all-to-all-done.1 = bf16[64,8,256]{2,1,0:T(8,128)(2,1)} async-done(((bf16[64,8,256]{2,1,0:T(8,128)(2,1)}), bf16[64,8,256]{2,1,0:T(8,128)(2,1)}, u32[]{:S(2)}, u32[]{:S(2)}) %all-to-all-start.1) | async-done | bytes 262176 | tf_op jit(solution)/shard_map/all_to_all | solution.py:21
  81.1 5.5 %collective-permute-start = (bf16[8,576,128]{2,1,0:T(8,128)(2,1)}, bf16[8,576,128]{2,1,0:T(8,128)(2,1)S(1)}, u32[]{:S(2)}, u32[]{:S(2)}) collective-permute-start(bf16[8,576,128]{2,1,0:T(8,128)(2,1)} %copy-done.11), channel_id=1, source_target_pairs={{0,64},{64,0},{128,192},{192,128},{256,320},{320,256},{384,448},{4... | collective-permute-start | bytes 3538952 | tf_op jit(solution)/shard_map/ppermute | solution.py:26
  86.6 0.0 all-gather.2.cloned.1.call-done.rows_hbm
  86.6 4.9 %shard_map.113 = (bf16[8,320,128]{2,1,0:T(8,128)(2,1)}, bf16[8,320,128]{2,1,0:T(8,128)(2,1)}, bf16[512,128]{1,0:T(8,128)(2,1)}) custom-call(s32[1]{0:T(128)} %bitcast.8.core_ref, bf16[512,2048]{1,0:T(8,128)(2,1)} %all-gather.2.cloned.1.call-done.rows_hbm, bf16[512,256]{1,0:T(8,128)(2,1)} %bitcast.11.blocks_ref), custom_call_target="tpu_custom_call" | custom-call | tf_op jit(solution)/shard_map/pallas_call | solution.py:354
  91.5 1.9 %collective-permute-start.1 = (bf16[8,320,128]{2,1,0:T(8,128)(2,1)}, bf16[8,320,128]{2,1,0:T(8,128)(2,1)S(1)}, u32[]{:S(2)}, u32[]{:S(2)}) collective-permute-start(bf16[8,320,128]{2,1,0:T(8,128)(2,1)} %get-tuple-element.44), channel_id=1, source_target_pairs={{0,64},{64,0},{128,192},{192,128},{256,320},{320,256},{384,448},{4... | collective-permute-start | bytes 1966088 | tf_op jit(solution)/shard_map/ppermute | solution.py:26
  93.5 2.3 %collective-permute-done.1.hot_came = bf16[8,320,128]{2,1,0:T(8,128)(2,1)S(1)} collective-permute-done((bf16[8,320,128]{2,1,0:T(8,128)(2,1)}, bf16[8,320,128]{2,1,0:T(8,128)(2,1)S(1)}, u32[]{:S(2)}, u32[]{:S(2)}) %collective-permute-start.1) | collective-permute-done | bytes 655392 | tf_op jit(solution)/shard_map/ppermute | solution.py:26
  95.7 1.1 copy-done.4
  96.8 1.6 shard_map.114
  98.5 0.0 reduce-scatter.2.cloned.1.call-update
  98.5 25.5 %all_to_all.25 = bf16[8,64,128]{2,1,0:T(8,128)(2,1)S(1)} all-to-all(bf16[8,64,128]{2,1,0:T(8,128)(2,1)S(1)} %get-tuple-element.45), channel_id=1, replica_groups={{0,128,256,384,512,640,768,896},{64,192,320,448,576,704,832,960},{1,129..., dimensions={0} | all-to-all | bytes 262144 | tf_op jit(solution)/shard_map/all_to_all | solution.py:32
  124.0 0.1 pad_maximum_fusion
  124.1 0.0 copy-start.7
  124.1 26.8 %all_to_all.26.parts_ref = bf16[64,8,768]{2,1,0:T(8,128)(2,1)} all-to-all(bf16[64,8,768]{2,1,0:T(8,128)(2,1)S(1)} %pad_maximum_fusion), channel_id=1, replica_groups=mesh['dp'=16,'expert'=64] {'expert'}, dimensions={0} | all-to-all | bytes 1572864 | tf_op jit(solution)/shard_map/all_to_all | solution.py:21
  150.9 2.0 %shard_map.116 = bf16[64,8,256]{2,1,0:T(8,128)(2,1)} custom-call(bf16[64,8,768]{2,1,0:T(8,128)(2,1)} %all_to_all.26.parts_ref), custom_call_target="tpu_custom_call" | custom-call | tf_op jit(solution)/shard_map/pallas_call | solution.py:219
  153.0 8.7 %all-to-all-start.4 = ((bf16[64,8,256]{2,1,0:T(8,128)(2,1)}), bf16[64,8,256]{2,1,0:T(8,128)(2,1)S(1)}, u32[]{:S(2)}, u32[]{:S(2)}) async-start(bf16[64,8,256]{2,1,0:T(8,128)(2,1)} %shard_map.116), calls=%async_computation.5 | async-start | bytes 524288 | tf_op jit(solution)/shard_map/all_to_all | solution.py:21
  162.4 0.0 reduce-scatter.2.cloned.1.call-done
  162.4 0.9 copy-done.8
  163.4 3.3 %shard_map.115 = (bf16[32,1024]{1,0:T(8,128)(2,1)}, f32[8,32]{1,0:T(8,128)}, f32[64,384]{1,0:T(8,128)S(1)}, f32[64,384]{1,0:T(8,128)S(1)}, f32[24,1024]{1,0:T(8,128)S(1)}, /*index=5*/bf16[1024,768]{1,0:T(8,128)(2,1)S(1)}) custom-call(s32[8,32]{1,0:T(8,128)S(1)} %bitcast.34, f32[8,32]{1,0:T(8,128)S(1)} %bitcast.36, bf16[32,1024]{1,0:T(8,128)(2,1)S(1)} %copy-done.7, ...), custom_call_target="tpu_custom_call" | custom-call | tf_op jit(solution)/shard_map/pallas_call | solution.py:438
  166.6 7.4 %all-to-all-done.4 = bf16[64,8,256]{2,1,0:T(8,128)(2,1)S(1)} async-done(((bf16[64,8,256]{2,1,0:T(8,128)(2,1)}), bf16[64,8,256]{2,1,0:T(8,128)(2,1)S(1)}, u32[]{:S(2)}, u32[]{:S(2)}) %all-to-all-start.4) | async-done | bytes 262176 | tf_op jit(solution)/shard_map/all_to_all | solution.py:21
  174.0 1.1 shard_map.117
  (22 shorter events, 0.1 us)
Async XLA Ops:
  7.2 79.4 %all-gather.2.cloned.1.call-start = ((), (), s32[]{:S(2)}) async-start(), calls=%async_computation.6 | async-start | bytes 2228224 | tf_op jit(solution)/shard_map/all_gather | solution.py:511
  11.4 57.4 %copy-start.3 = (bf16[1,384,1024]{2,1,0:T(8,128)(2,1)S(1)}, bf16[1,384,1024]{2,1,0:T(8,128)(2,1)}, u32[]{:S(2)}) copy-start(bf16[1,384,1024]{2,1,0:T(8,128)(2,1)} %param.13) | copy-start | bytes 2359300
  11.5 41.9 %all-to-all-start = ((bf16[64,8,1280]{2,1,0:T(8,128)(2,1)}), bf16[64,8,1280]{2,1,0:T(8,128)(2,1)}, u32[]{:S(2)}, u32[]{:S(2)}) async-start(bf16[64,8,1280]{2,1,0:T(8,128)(2,1)} %bitcast.37), calls=%async_computation | async-start | bytes 2621440 | tf_op jit(solution)/shard_map/all_to_all | solution.py:21
  25.9 43.0 %copy-start.1 = (bf16[1,1024,384]{2,1,0:T(8,128)(2,1)S(1)}, bf16[1,1024,384]{2,1,0:T(8,128)(2,1)}, u32[]{:S(2)}) copy-start(bf16[1,1024,384]{2,1,0:T(8,128)(2,1)} %param.11) | copy-start | bytes 2359300
  25.9 43.0 %copy-start.2 = (bf16[1,1024,384]{2,1,0:T(8,128)(2,1)S(1)}, bf16[1,1024,384]{2,1,0:T(8,128)(2,1)}, u32[]{:S(2)}) copy-start(bf16[1,1024,384]{2,1,0:T(8,128)(2,1)} %param.12) | copy-start | bytes 2359300
  55.4 25.7 %all-to-all-start.1 = ((bf16[64,8,256]{2,1,0:T(8,128)(2,1)}), bf16[64,8,256]{2,1,0:T(8,128)(2,1)}, u32[]{:S(2)}, u32[]{:S(2)}) async-start(bf16[64,8,256]{2,1,0:T(8,128)(2,1)} %shard_map.111), calls=%async_computation.1 | async-start | bytes 524288 | tf_op jit(solution)/shard_map/all_to_all | solution.py:21
  68.8 93.6 %reduce-scatter.2.cloned.1.call-start = ((), (), s32[]{:S(2)}) async-start(), calls=%async_computation.7 | async-start | bytes 1916928 | tf_op jit(solution)/shard_map/reduce_scatter | solution.py:40
  74.3 0.8 copy-start.5
  75.1 1.0 copy-start.11
  81.1 12.4 %collective-permute-start = (bf16[8,576,128]{2,1,0:T(8,128)(2,1)}, bf16[8,576,128]{2,1,0:T(8,128)(2,1)S(1)}, u32[]{:S(2)}, u32[]{:S(2)}) collective-permute-start(bf16[8,576,128]{2,1,0:T(8,128)(2,1)} %copy-done.11), channel_id=1, source_target_pairs={{0,64},{64,0},{128,192},{192,128},{256,320},{320,256},{384,448},{4... | collective-permute-start | bytes 3538952 | tf_op jit(solution)/shard_map/ppermute | solution.py:26
  91.5 4.2 %collective-permute-start.1 = (bf16[8,320,128]{2,1,0:T(8,128)(2,1)}, bf16[8,320,128]{2,1,0:T(8,128)(2,1)S(1)}, u32[]{:S(2)}, u32[]{:S(2)}) collective-permute-start(bf16[8,320,128]{2,1,0:T(8,128)(2,1)} %get-tuple-element.44), channel_id=1, source_target_pairs={{0,64},{64,0},{128,192},{192,128},{256,320},{320,256},{384,448},{4... | collective-permute-start | bytes 1966088 | tf_op jit(solution)/shard_map/ppermute | solution.py:26
  95.7 1.1 copy-start.4
  98.5 25.6 %copy-start.6 = (bf16[512,512]{1,0:T(8,128)(2,1)S(1)}, bf16[512,512]{1,0:T(8,128)(2,1)}, u32[]{:S(2)}) copy-start(bf16[512,512]{1,0:T(8,128)(2,1)} %copy-done.5) | copy-start | bytes 1572868
  98.5 25.6 %copy-start.12 = (bf16[512,128]{1,0:T(8,128)(2,1)S(1)}, bf16[512,128]{1,0:T(8,128)(2,1)}, u32[]{:S(2)}) copy-start(bf16[512,128]{1,0:T(8,128)(2,1)} %get-tuple-element.46) | copy-start | bytes 393220
  124.1 38.3 %copy-start.7 = (bf16[32,1024]{1,0:T(8,128)(2,1)S(1)}, bf16[32,1024]{1,0:T(8,128)(2,1)}, u32[]{:S(2)}) copy-start(bf16[32,1024]{1,0:T(8,128)(2,1)} %cotangent_ref.1) | copy-start | bytes 196612
  124.1 38.3 %copy-start.9 = (s32[32,8]{0,1:T(8,128)S(1)}, s32[32,8]{0,1:T(8,128)}, u32[]{:S(2)}) copy-start(s32[32,8]{0,1:T(8,128)} %param.10) | copy-start | bytes 3076
  124.1 38.3 %copy-start.10 = (f32[32,8]{0,1:T(8,128)S(1)}, f32[32,8]{0,1:T(8,128)}, u32[]{:S(2)}) copy-start(f32[32,8]{0,1:T(8,128)} %param.9) | copy-start | bytes 3076
  150.9 11.5 %copy-start = (bf16[64,8,768]{2,1,0:T(8,128)(2,1)S(1)}, bf16[64,8,768]{2,1,0:T(8,128)(2,1)}, u32[]{:S(2)}) copy-start(bf16[64,8,768]{2,1,0:T(8,128)(2,1)} %all_to_all.26.parts_ref) | copy-start | bytes 2359300
  153.0 21.1 %all-to-all-start.4 = ((bf16[64,8,256]{2,1,0:T(8,128)(2,1)}), bf16[64,8,256]{2,1,0:T(8,128)(2,1)S(1)}, u32[]{:S(2)}, u32[]{:S(2)}) async-start(bf16[64,8,256]{2,1,0:T(8,128)(2,1)} %shard_map.116), calls=%async_computation.5 | async-start | bytes 524288 | tf_op jit(solution)/shard_map/all_to_all | solution.py:21
  162.4 0.9 copy-start.8
Sparse Core Ops, SparseCore 0:
  11.6 59.4 all-gather.1
  98.6 48.9 reduce-scatter.1

commit v6 on v5

--- a/solution.py
+++ b/solution.py
@@ -364,7 +364,7 @@
             pltpu.VMEM((total, features), bf16),
             pltpu.SemaphoreType.DMA((2,)),
         ],
-        compiler_params=pltpu.CompilerParams(vmem_limit_bytes=59 * 2**20),
+        compiler_params=pltpu.CompilerParams(vmem_limit_bytes=48 * 2**20),
     )(core, gathered, blocks)
 
 

time: 184 us -> 182 us (0.989)
  Pallas kernels: 24.7 us -> 22.7 us
    pallas_call x1, Pallas kernels: 4.94 us -> 2.99 us  [hot_expert(): pl.pallas_call(functools.partial(hot_kernel, units), out_shape=(side, sid...]
    unnamed x26 -> x24, local copies, waits for them, and re-layouts: 3.88 us -> 4.39 us
  transfers between devices with their start and end apart: 7 -> 7, of which waited for: 4 -> 4; matrix products, arithmetic and copies ran while one was open for 1% -> 1% of each run, Pallas kernels for 10% -> 9%
where the time goes in v6:
time: 182 us; the launch traced here: 180 us
  blocking collectives  52.4 us (29%)
  starting transfers between devices  44 us (24%)
  waiting for transfers between devices  40.6 us (22%)
  Pallas kernels  22.7 us (12%)
  between operations  14.9 us (8%)
  local copies, waits for them, and re-layouts  5.7 us (3%)
    all_to_all x3, waiting for transfers between devices, plane_exchange(): lax.all_to_all(blocks, 'expert', split_axis=0, concat_axis=0, tiled=True)  38.5 us
    all_to_all x3, starting transfers between devices, plane_exchange(): lax.all_to_all(blocks, 'expert', split_axis=0, concat_axis=0, tiled=True)  36.5 us
    all_to_all x1, blocking collectives, plane_exchange(): lax.all_to_all(blocks, 'expert', split_axis=0, concat_axis=0, tiled=True)  26.8 us
    all_to_all x1, blocking collectives, z_exchange(): lax.all_to_all(blocks, 'dp', split_axis=0, concat_axis=0, tiled=True, axi...  25.5 us
    ppermute x2, starting transfers between devices, core_swap(): return lax.ppermute(block, 'dp', [(i, i ^ 1) for i in range(size)])  7.38 us
    pallas_call x1, Pallas kernels, own_expert(): pl.pallas_call(own_kernel, out_shape=(jax.ShapeDtypeStruct((rows.shape[0]...  5.42 us
    unnamed x24, local copies, waits for them, and re-layouts  4.39 us
    pallas_call x1, Pallas kernels, pack(): pl.pallas_call(functools.partial(pack_kernel, size=size), out_shape=(jax....  4.2 us
  transfers between devices with their start and end apart: 7, of which 4 were waited for; matrix products, arithmetic and copies ran while one was open for 1% of the time, Pallas kernels for 9%

profile of v6, /device:TPU:1, one launch (start us, length us, event | category | flops | bytes accessed | tf_op | source)
XLA Modules:
  0.0 180.3 jit_solution(7839706039646940153)
XLA Ops:
  7.2 0.0 all-gather.2.cloned.1.call-start
  7.2 4.2 %shard_map.110 = (bf16[512,1280]{1,0:T(8,128)(2,1)}, bf16[32,2048]{1,0:T(8,128)(2,1)}, s32[8,128]{1,0:T(8,128)}) custom-call(s32[1]{0:T(128)} %bitcast.shard_ref, s32[8,32]{1,0:T(8,128)} %bitcast.34, f32[8,32]{1,0:T(8,128)} %bitcast.36, bf16[32,1024]{1,0:T(8,128)(2,1)} %tokens_hbm.1, bf16[32,1024]{1,0:T(8,128)(2,1)} %cotangent_ref.1, ...), custom_call_target="tpu_custom_call" | custom-call | tf_op jit(solution)/shard_map/pallas_call | solution.py:146
  11.4 0.0 all-gather.2.cloned.1.call-update
  11.5 14.4 %all-to-all-start = ((bf16[64,8,1280]{2,1,0:T(8,128)(2,1)}), bf16[64,8,1280]{2,1,0:T(8,128)(2,1)}, u32[]{:S(2)}, u32[]{:S(2)}) async-start(bf16[64,8,1280]{2,1,0:T(8,128)(2,1)} %bitcast.38), calls=%async_computation | async-start | bytes 2621440 | tf_op jit(solution)/shard_map/all_to_all | solution.py:21
  25.9 0.0 copy-start.1
  25.9 1.3 slice.4
  27.2 26.1 %all-to-all-done.piece_ref = bf16[64,8,1280]{2,1,0:T(8,128)(2,1)} async-done(((bf16[64,8,1280]{2,1,0:T(8,128)(2,1)}), bf16[64,8,1280]{2,1,0:T(8,128)(2,1)}, u32[]{:S(2)}, u32[]{:S(2)}) %all-to-all-start) | async-done | bytes 1310752 | tf_op jit(solution)/shard_map/all_to_all | solution.py:21
  53.4 2.1 %shard_map.111 = bf16[64,8,256]{2,1,0:T(8,128)(2,1)} custom-call(s32[1]{0:T(128)} %bitcast.7.busiest_ref, bf16[64,8,1280]{2,1,0:T(8,128)(2,1)} %all-to-all-done.piece_ref), custom_call_target="tpu_custom_call" | custom-call | tf_op jit(solution)/shard_map/pallas_call | solution.py:207
  55.4 13.4 %all-to-all-start.1 = ((bf16[64,8,256]{2,1,0:T(8,128)(2,1)}), bf16[64,8,256]{2,1,0:T(8,128)(2,1)}, u32[]{:S(2)}, u32[]{:S(2)}) async-start(bf16[64,8,256]{2,1,0:T(8,128)(2,1)} %shard_map.111), calls=%async_computation.1 | async-start | bytes 524288 | tf_op jit(solution)/shard_map/all_to_all | solution.py:21
  68.8 0.0 reduce-scatter.2.cloned.1.call-start
  68.9 5.4 %shard_map.112 = (bf16[512,512]{1,0:T(8,128)(2,1)S(1)}, bf16[8,576,128]{2,1,0:T(8,128)(2,1)S(1)}, bf16[8,576,128]{2,1,0:T(8,128)(2,1)S(1)}) custom-call(s32[1]{0:T(128)} %bitcast.8.core_ref, bf16[512,1280]{1,0:T(8,128)(2,1)} %bitcast.9.rows_ref, bf16[1024,384]{1,0:T(8,128)(2,1)S(1)} %bitcast.25, bf16[1024,384]{1,0:T(8,128)(2,1)S(1)} %bitcast.27, ...), custom_call_target="tpu_custom_call" | custom-call | tf_op jit(solution)/shard_map/pallas_call | solution.py:280
  74.3 0.8 copy-done.5
  75.1 1.0 copy-done.11
  76.1 5.0 %all-to-all-done.1 = bf16[64,8,256]{2,1,0:T(8,128)(2,1)} async-done(((bf16[64,8,256]{2,1,0:T(8,128)(2,1)}), bf16[64,8,256]{2,1,0:T(8,128)(2,1)}, u32[]{:S(2)}, u32[]{:S(2)}) %all-to-all-start.1) | async-done | bytes 262176 | tf_op jit(solution)/shard_map/all_to_all | solution.py:21
  81.1 5.5 %collective-permute-start = (bf16[8,576,128]{2,1,0:T(8,128)(2,1)}, bf16[8,576,128]{2,1,0:T(8,128)(2,1)S(1)}, u32[]{:S(2)}, u32[]{:S(2)}) collective-permute-start(bf16[8,576,128]{2,1,0:T(8,128)(2,1)} %copy-done.11), channel_id=1, source_target_pairs={{0,64},{64,0},{128,192},{192,128},{256,320},{320,256},{384,448},{4... | collective-permute-start | bytes 3538952 | tf_op jit(solution)/shard_map/ppermute | solution.py:26
  86.6 0.0 all-gather.2.cloned.1.call-done.rows_hbm
  86.6 1.6 copy-done.4
  88.2 3.0 %shard_map.113 = (bf16[8,320,128]{2,1,0:T(8,128)(2,1)S(1)}, bf16[8,320,128]{2,1,0:T(8,128)(2,1)S(1)}, bf16[512,128]{1,0:T(8,128)(2,1)S(1)}) custom-call(s32[1]{0:T(128)} %bitcast.8.core_ref, bf16[512,2048]{1,0:T(8,128)(2,1)S(1)} %copy-done.4, bf16[512,256]{1,0:T(8,128)(2,1)} %bitcast.11.blocks_ref), custom_call_target="tpu_custom_call" | custom-call | tf_op jit(solution)/shard_map/pallas_call | solution.py:354
  91.2 1.9 %collective-permute-start.1 = (bf16[8,320,128]{2,1,0:T(8,128)(2,1)S(1)}, bf16[8,320,128]{2,1,0:T(8,128)(2,1)S(1)}, u32[]{:S(2)}, u32[]{:S(2)}) collective-permute-start(bf16[8,320,128]{2,1,0:T(8,128)(2,1)S(1)} %get-tuple-element.44), channel_id=1, source_target_pairs={{0,64},{64,0},{128,192},{192,128},{256,320},{320,256},{384,448},{4... | collective-permute-start | bytes 1966088 | tf_op jit(solution)/shard_map/ppermute | solution.py:26
  93.1 2.1 %collective-permute-done.1.hot_came = bf16[8,320,128]{2,1,0:T(8,128)(2,1)S(1)} collective-permute-done((bf16[8,320,128]{2,1,0:T(8,128)(2,1)S(1)}, bf16[8,320,128]{2,1,0:T(8,128)(2,1)S(1)}, u32[]{:S(2)}, u32[]{:S(2)}) %collective-permute-start.1) | collective-permute-done | bytes 655392 | tf_op jit(solution)/shard_map/ppermute | solution.py:26
  95.2 1.6 shard_map.114
  96.8 0.0 reduce-scatter.2.cloned.1.call-update
  96.8 25.5 %all_to_all.25 = bf16[8,64,128]{2,1,0:T(8,128)(2,1)S(1)} all-to-all(bf16[8,64,128]{2,1,0:T(8,128)(2,1)S(1)} %get-tuple-element.45), channel_id=1, replica_groups={{0,128,256,384,512,640,768,896},{64,192,320,448,576,704,832,960},{1,129..., dimensions={0} | all-to-all | bytes 262144 | tf_op jit(solution)/shard_map/all_to_all | solution.py:32
  122.3 0.1 pad_maximum_fusion
  122.4 26.8 %all_to_all.26.parts_ref = bf16[64,8,768]{2,1,0:T(8,128)(2,1)} all-to-all(bf16[64,8,768]{2,1,0:T(8,128)(2,1)S(1)} %pad_maximum_fusion), channel_id=1, replica_groups=mesh['dp'=16,'expert'=64] {'expert'}, dimensions={0} | all-to-all | bytes 1572864 | tf_op jit(solution)/shard_map/all_to_all | solution.py:21
  149.3 2.0 %shard_map.116 = bf16[64,8,256]{2,1,0:T(8,128)(2,1)} custom-call(bf16[64,8,768]{2,1,0:T(8,128)(2,1)} %all_to_all.26.parts_ref), custom_call_target="tpu_custom_call" | custom-call | tf_op jit(solution)/shard_map/pallas_call | solution.py:219
  151.3 8.7 %all-to-all-start.4 = ((bf16[64,8,256]{2,1,0:T(8,128)(2,1)}), bf16[64,8,256]{2,1,0:T(8,128)(2,1)S(1)}, u32[]{:S(2)}, u32[]{:S(2)}) async-start(bf16[64,8,256]{2,1,0:T(8,128)(2,1)} %shard_map.116), calls=%async_computation.5 | async-start | bytes 524288 | tf_op jit(solution)/shard_map/all_to_all | solution.py:21
  160.7 0.0 reduce-scatter.2.cloned.1.call-done
  160.8 0.9 copy-done.8
  161.7 3.3 %shard_map.115 = (bf16[32,1024]{1,0:T(8,128)(2,1)}, f32[8,32]{1,0:T(8,128)}, f32[64,384]{1,0:T(8,128)S(1)}, f32[64,384]{1,0:T(8,128)S(1)}, f32[24,1024]{1,0:T(8,128)S(1)}, /*index=5*/bf16[1024,768]{1,0:T(8,128)(2,1)S(1)}) custom-call(s32[8,32]{1,0:T(8,128)S(1)} %bitcast.35, f32[8,32]{1,0:T(8,128)S(1)} %bitcast.37, bf16[32,1024]{1,0:T(8,128)(2,1)S(1)} %copy-done.7, ...), custom_call_target="tpu_custom_call" | custom-call | tf_op jit(solution)/shard_map/pallas_call | solution.py:438
  165.0 7.4 %all-to-all-done.4 = bf16[64,8,256]{2,1,0:T(8,128)(2,1)S(1)} async-done(((bf16[64,8,256]{2,1,0:T(8,128)(2,1)}), bf16[64,8,256]{2,1,0:T(8,128)(2,1)S(1)}, u32[]{:S(2)}, u32[]{:S(2)}) %all-to-all-start.4) | async-done | bytes 262176 | tf_op jit(solution)/shard_map/all_to_all | solution.py:21
  172.3 1.1 shard_map.117
  (20 shorter events, 0.1 us)
Async XLA Ops:
  7.2 79.4 %all-gather.2.cloned.1.call-start = ((), (), s32[]{:S(2)}) async-start(), calls=%async_computation.6 | async-start | bytes 2228224 | tf_op jit(solution)/shard_map/all_gather | solution.py:511
  11.4 57.4 %copy-start.3 = (bf16[1,384,1024]{2,1,0:T(8,128)(2,1)S(1)}, bf16[1,384,1024]{2,1,0:T(8,128)(2,1)}, u32[]{:S(2)}) copy-start(bf16[1,384,1024]{2,1,0:T(8,128)(2,1)} %param.13) | copy-start | bytes 2359300
  11.5 41.9 %all-to-all-start = ((bf16[64,8,1280]{2,1,0:T(8,128)(2,1)}), bf16[64,8,1280]{2,1,0:T(8,128)(2,1)}, u32[]{:S(2)}, u32[]{:S(2)}) async-start(bf16[64,8,1280]{2,1,0:T(8,128)(2,1)} %bitcast.38), calls=%async_computation | async-start | bytes 2621440 | tf_op jit(solution)/shard_map/all_to_all | solution.py:21
  25.9 43.0 %copy-start.1 = (bf16[1,1024,384]{2,1,0:T(8,128)(2,1)S(1)}, bf16[1,1024,384]{2,1,0:T(8,128)(2,1)}, u32[]{:S(2)}) copy-start(bf16[1,1024,384]{2,1,0:T(8,128)(2,1)} %param.11) | copy-start | bytes 2359300
  25.9 43.0 %copy-start.2 = (bf16[1,1024,384]{2,1,0:T(8,128)(2,1)S(1)}, bf16[1,1024,384]{2,1,0:T(8,128)(2,1)}, u32[]{:S(2)}) copy-start(bf16[1,1024,384]{2,1,0:T(8,128)(2,1)} %param.12) | copy-start | bytes 2359300
  55.4 25.7 %all-to-all-start.1 = ((bf16[64,8,256]{2,1,0:T(8,128)(2,1)}), bf16[64,8,256]{2,1,0:T(8,128)(2,1)}, u32[]{:S(2)}, u32[]{:S(2)}) async-start(bf16[64,8,256]{2,1,0:T(8,128)(2,1)} %shard_map.111), calls=%async_computation.1 | async-start | bytes 524288 | tf_op jit(solution)/shard_map/all_to_all | solution.py:21
  68.8 91.9 %reduce-scatter.2.cloned.1.call-start = ((), (), s32[]{:S(2)}) async-start(), calls=%async_computation.7 | async-start | bytes 1916928 | tf_op jit(solution)/shard_map/reduce_scatter | solution.py:40
  74.3 0.8 copy-start.5
  75.1 1.0 copy-start.11
  81.1 12.0 %collective-permute-start = (bf16[8,576,128]{2,1,0:T(8,128)(2,1)}, bf16[8,576,128]{2,1,0:T(8,128)(2,1)S(1)}, u32[]{:S(2)}, u32[]{:S(2)}) collective-permute-start(bf16[8,576,128]{2,1,0:T(8,128)(2,1)} %copy-done.11), channel_id=1, source_target_pairs={{0,64},{64,0},{128,192},{192,128},{256,320},{320,256},{384,448},{4... | collective-permute-start | bytes 3538952 | tf_op jit(solution)/shard_map/ppermute | solution.py:26
  86.6 1.6 copy-start.4
  91.2 4.0 %collective-permute-start.1 = (bf16[8,320,128]{2,1,0:T(8,128)(2,1)S(1)}, bf16[8,320,128]{2,1,0:T(8,128)(2,1)S(1)}, u32[]{:S(2)}, u32[]{:S(2)}) collective-permute-start(bf16[8,320,128]{2,1,0:T(8,128)(2,1)S(1)} %get-tuple-element.44), channel_id=1, source_target_pairs={{0,64},{64,0},{128,192},{192,128},{256,320},{320,256},{384,448},{4... | collective-permute-start | bytes 1966088 | tf_op jit(solution)/shard_map/ppermute | solution.py:26
  96.8 25.6 %copy-start.6 = (bf16[512,512]{1,0:T(8,128)(2,1)S(1)}, bf16[512,512]{1,0:T(8,128)(2,1)}, u32[]{:S(2)}) copy-start(bf16[512,512]{1,0:T(8,128)(2,1)} %copy-done.5) | copy-start | bytes 1572868
  122.4 38.3 %copy-start.7 = (bf16[32,1024]{1,0:T(8,128)(2,1)S(1)}, bf16[32,1024]{1,0:T(8,128)(2,1)}, u32[]{:S(2)}) copy-start(bf16[32,1024]{1,0:T(8,128)(2,1)} %cotangent_ref.1) | copy-start | bytes 196612
  122.4 38.3 %copy-start.9 = (s32[32,8]{0,1:T(8,128)S(1)}, s32[32,8]{0,1:T(8,128)}, u32[]{:S(2)}) copy-start(s32[32,8]{0,1:T(8,128)} %param.10) | copy-start | bytes 3076
  122.4 38.3 %copy-start.10 = (f32[32,8]{0,1:T(8,128)S(1)}, f32[32,8]{0,1:T(8,128)}, u32[]{:S(2)}) copy-start(f32[32,8]{0,1:T(8,128)} %param.9) | copy-start | bytes 3076
  149.3 11.5 %copy-start = (bf16[64,8,768]{2,1,0:T(8,128)(2,1)S(1)}, bf16[64,8,768]{2,1,0:T(8,128)(2,1)}, u32[]{:S(2)}) copy-start(bf16[64,8,768]{2,1,0:T(8,128)(2,1)} %all_to_all.26.parts_ref) | copy-start | bytes 2359300
  151.3 21.1 %all-to-all-start.4 = ((bf16[64,8,256]{2,1,0:T(8,128)(2,1)}), bf16[64,8,256]{2,1,0:T(8,128)(2,1)S(1)}, u32[]{:S(2)}, u32[]{:S(2)}) async-start(bf16[64,8,256]{2,1,0:T(8,128)(2,1)} %shard_map.116), calls=%async_computation.5 | async-start | bytes 524288 | tf_op jit(solution)/shard_map/all_to_all | solution.py:21
  160.7 0.9 copy-start.8
Sparse Core Ops, SparseCore 0:
  11.6 59.4 all-gather.1
  96.9 48.7 reduce-scatter.1

commit v7 on v6

--- a/solution.py
+++ b/solution.py
@@ -210,17 +210,19 @@
 
 
 def total_kernel(parts_ref, out_ref):
-    half = parts_ref.shape[2] - 256
-    sums = jnp.sum(parts_ref[:, :, half:].astype(f32), axis=0, keepdims=True).astype(bf16)
+    sums = jnp.sum(parts_ref[...].astype(f32), axis=0, keepdims=True).astype(bf16)
     out_ref[...] = jnp.broadcast_to(sums, out_ref.shape)
 
 
 def total(back):
+    shape = (back.shape[0], 8, 256)
+    block = back.shape[2] // 256 - 1
     return pl.pallas_call(
         total_kernel,
-        in_specs=in_vmem(1),
-        out_specs=in_vmem(1)[0],
-        out_shape=jax.ShapeDtypeStruct((back.shape[0], 8, 256), bf16),
+        grid=(1,),
+        in_specs=[pl.BlockSpec(shape, lambda i: (0, 0, block))],
+        out_specs=pl.BlockSpec(shape, lambda i: (0, 0, 0)),
+        out_shape=jax.ShapeDtypeStruct(shape, bf16),
     )(back)
 
 
@@ -288,7 +290,7 @@
 
 
 def hot_kernel(
-    units, core_ref, rows_hbm, blocks_ref, kept_ref, passed_ref, grads_ref, part, pair_part, inputs_ref, scaled_ref, sems
+    units, core_ref, rows_ref, blocks_ref, kept_ref, passed_ref, grads_ref, part, pair_part
 ):
     features = part.shape[1]
     depth = kept_ref.shape[0]
@@ -296,19 +298,13 @@
     spans = features // 256
     height = -(-3 * units // 16) * 16
     core = core_ref[0]
-    first = pltpu.make_async_copy(rows_hbm.at[:, :features], inputs_ref, sems.at[0])
-    second = pltpu.make_async_copy(rows_hbm.at[:, features:], scaled_ref, sems.at[1])
-    first.start()
-    second.start()
+    inputs = rows_ref[:, :features]
+    scaled = rows_ref[:, features:]
     sliced = jnp.concatenate(
         [blocks_ref[span * height : span * height + height, :] for span in range(spans)], axis=1
     )
     down = sliced[2 * units :]
-    first.wait()
-    inputs = inputs_ref[...]
     both = dot(sliced[: 2 * units], inputs, 1, 1)
-    second.wait()
-    scaled = scaled_ref[...]
     upstream = dot(down, scaled, 1, 1)[:units]
     gate_value, up_value = both[:units], both[units:]
     sigmoid = jax.nn.sigmoid(gate_value)
@@ -354,15 +350,11 @@
     return pl.pallas_call(
         functools.partial(hot_kernel, units),
         out_shape=(side, side, jax.ShapeDtypeStruct((blocks.shape[0], 128), bf16)),
-        in_specs=[pl.BlockSpec(memory_space=pltpu.SMEM), pl.BlockSpec(memory_space=pl.ANY)]
-        + in_vmem(1),
+        in_specs=[pl.BlockSpec(memory_space=pltpu.SMEM)] + in_vmem(2),
         out_specs=tuple(in_vmem(3)),
         scratch_shapes=[
             pltpu.VMEM((total, features), f32),
             pltpu.VMEM((features, 128), f32),
-            pltpu.VMEM((total, features), bf16),
-            pltpu.VMEM((total, features), bf16),
-            pltpu.SemaphoreType.DMA((2,)),
         ],
         compiler_params=pltpu.CompilerParams(vmem_limit_bytes=48 * 2**20),
     )(core, gathered, blocks)

time: 182 us -> 181 us (level)
  transfers between devices with their start and end apart: 7 -> 7, of which waited for: 4 -> 4; matrix products, arithmetic and copies ran while one was open for 1% -> 1% of each run, Pallas kernels for 9% -> 8%
where the time goes in v7:
time: 181 us; the launch traced here: 180 us
  blocking collectives  52.4 us (29%)
  starting transfers between devices  44 us (24%)
  waiting for transfers between devices  40.6 us (22%)
  Pallas kernels  22 us (12%)
  between operations  14.9 us (8%)
  local copies, waits for them, and re-layouts  5.7 us (3%)
    all_to_all x3, waiting for transfers between devices, plane_exchange(): lax.all_to_all(blocks, 'expert', split_axis=0, concat_axis=0, tiled=True)  38.5 us
    all_to_all x3, starting transfers between devices, plane_exchange(): lax.all_to_all(blocks, 'expert', split_axis=0, concat_axis=0, tiled=True)  36.5 us
    all_to_all x1, blocking collectives, plane_exchange(): lax.all_to_all(blocks, 'expert', split_axis=0, concat_axis=0, tiled=True)  26.8 us
    all_to_all x1, blocking collectives, z_exchange(): lax.all_to_all(blocks, 'dp', split_axis=0, concat_axis=0, tiled=True, axi...  25.5 us
    ppermute x2, starting transfers between devices, core_swap(): return lax.ppermute(block, 'dp', [(i, i ^ 1) for i in range(size)])  7.38 us
    pallas_call x1, Pallas kernels, own_expert(): pl.pallas_call(own_kernel, out_shape=(jax.ShapeDtypeStruct((rows.shape[0]...  5.42 us
    unnamed x24, local copies, waits for them, and re-layouts  4.39 us
    pallas_call x1, Pallas kernels, pack(): pl.pallas_call(functools.partial(pack_kernel, size=size), out_shape=(jax....  4.2 us
  transfers between devices with their start and end apart: 7, of which 4 were waited for; matrix products, arithmetic and copies ran while one was open for 1% of the time, Pallas kernels for 8%

profile of v7, /device:TPU:1, one launch (start us, length us, event | category | flops | bytes accessed | tf_op | source)
XLA Modules:
  0.0 179.6 jit_solution(2009350442635056590)
XLA Ops:
  7.2 0.0 all-gather.2.cloned.1.call-start
  7.2 4.2 %shard_map.110 = (bf16[512,1280]{1,0:T(8,128)(2,1)}, bf16[32,2048]{1,0:T(8,128)(2,1)}, s32[8,128]{1,0:T(8,128)}) custom-call(s32[1]{0:T(128)} %bitcast.shard_ref, s32[8,32]{1,0:T(8,128)} %bitcast.34, f32[8,32]{1,0:T(8,128)} %bitcast.36, bf16[32,1024]{1,0:T(8,128)(2,1)} %tokens_hbm.1, bf16[32,1024]{1,0:T(8,128)(2,1)} %cotangent_ref.1, ...), custom_call_target="tpu_custom_call" | custom-call | tf_op jit(solution)/shard_map/pallas_call | solution.py:146
  11.4 0.0 all-gather.2.cloned.1.call-update
  11.4 0.0 copy-start.3
  11.5 14.4 %all-to-all-start = ((bf16[64,8,1280]{2,1,0:T(8,128)(2,1)}), bf16[64,8,1280]{2,1,0:T(8,128)(2,1)}, u32[]{:S(2)}, u32[]{:S(2)}) async-start(bf16[64,8,1280]{2,1,0:T(8,128)(2,1)} %bitcast.38), calls=%async_computation | async-start | bytes 2621440 | tf_op jit(solution)/shard_map/all_to_all | solution.py:21
  25.9 1.3 slice.4
  27.2 26.1 %all-to-all-done.piece_ref = bf16[64,8,1280]{2,1,0:T(8,128)(2,1)} async-done(((bf16[64,8,1280]{2,1,0:T(8,128)(2,1)}), bf16[64,8,1280]{2,1,0:T(8,128)(2,1)}, u32[]{:S(2)}, u32[]{:S(2)}) %all-to-all-start) | async-done | bytes 1310752 | tf_op jit(solution)/shard_map/all_to_all | solution.py:21
  53.4 2.1 %shard_map.111 = bf16[64,8,256]{2,1,0:T(8,128)(2,1)} custom-call(s32[1]{0:T(128)} %bitcast.7.busiest_ref, bf16[64,8,1280]{2,1,0:T(8,128)(2,1)} %all-to-all-done.piece_ref), custom_call_target="tpu_custom_call" | custom-call | tf_op jit(solution)/shard_map/pallas_call | solution.py:207
  55.4 13.4 %all-to-all-start.1 = ((bf16[64,8,256]{2,1,0:T(8,128)(2,1)}), bf16[64,8,256]{2,1,0:T(8,128)(2,1)}, u32[]{:S(2)}, u32[]{:S(2)}) async-start(bf16[64,8,256]{2,1,0:T(8,128)(2,1)} %shard_map.111), calls=%async_computation.1 | async-start | bytes 524288 | tf_op jit(solution)/shard_map/all_to_all | solution.py:21
  68.8 0.0 reduce-scatter.2.cloned.1.call-start
  68.9 5.4 %shard_map.112 = (bf16[512,512]{1,0:T(8,128)(2,1)S(1)}, bf16[8,576,128]{2,1,0:T(8,128)(2,1)S(1)}, bf16[8,576,128]{2,1,0:T(8,128)(2,1)S(1)}) custom-call(s32[1]{0:T(128)} %bitcast.8.core_ref, bf16[512,1280]{1,0:T(8,128)(2,1)} %bitcast.9.rows_ref, bf16[1024,384]{1,0:T(8,128)(2,1)S(1)} %bitcast.25, bf16[1024,384]{1,0:T(8,128)(2,1)S(1)} %bitcast.27, ...), custom_call_target="tpu_custom_call" | custom-call | tf_op jit(solution)/shard_map/pallas_call | solution.py:282
  74.3 0.8 copy-done.5
  75.1 1.0 copy-done.11
  76.1 5.0 %all-to-all-done.1 = bf16[64,8,256]{2,1,0:T(8,128)(2,1)} async-done(((bf16[64,8,256]{2,1,0:T(8,128)(2,1)}), bf16[64,8,256]{2,1,0:T(8,128)(2,1)}, u32[]{:S(2)}, u32[]{:S(2)}) %all-to-all-start.1) | async-done | bytes 262176 | tf_op jit(solution)/shard_map/all_to_all | solution.py:21
  81.1 5.5 %collective-permute-start = (bf16[8,576,128]{2,1,0:T(8,128)(2,1)}, bf16[8,576,128]{2,1,0:T(8,128)(2,1)S(1)}, u32[]{:S(2)}, u32[]{:S(2)}) collective-permute-start(bf16[8,576,128]{2,1,0:T(8,128)(2,1)} %copy-done.11), channel_id=1, source_target_pairs={{0,64},{64,0},{128,192},{192,128},{256,320},{320,256},{384,448},{4... | collective-permute-start | bytes 3538952 | tf_op jit(solution)/shard_map/ppermute | solution.py:26
  86.6 0.0 all-gather.2.cloned.1.call-done.rows_ref
  86.6 1.6 copy-done.4
  88.2 2.5 %shard_map.113 = (bf16[8,320,128]{2,1,0:T(8,128)(2,1)S(1)}, bf16[8,320,128]{2,1,0:T(8,128)(2,1)S(1)}, bf16[512,128]{1,0:T(8,128)(2,1)S(1)}) custom-call(s32[1]{0:T(128)} %bitcast.8.core_ref, bf16[512,2048]{1,0:T(8,128)(2,1)S(1)} %copy-done.4, bf16[512,256]{1,0:T(8,128)(2,1)} %bitcast.11.blocks_ref), custom_call_target="tpu_custom_call" | custom-call | tf_op jit(solution)/shard_map/pallas_call | solution.py:350
  90.6 1.9 %collective-permute-start.1 = (bf16[8,320,128]{2,1,0:T(8,128)(2,1)S(1)}, bf16[8,320,128]{2,1,0:T(8,128)(2,1)S(1)}, u32[]{:S(2)}, u32[]{:S(2)}) collective-permute-start(bf16[8,320,128]{2,1,0:T(8,128)(2,1)S(1)} %get-tuple-element.44), channel_id=1, source_target_pairs={{0,64},{64,0},{128,192},{192,128},{256,320},{320,256},{384,448},{4... | collective-permute-start | bytes 1966088 | tf_op jit(solution)/shard_map/ppermute | solution.py:26
  92.6 2.1 %collective-permute-done.1.hot_came = bf16[8,320,128]{2,1,0:T(8,128)(2,1)S(1)} collective-permute-done((bf16[8,320,128]{2,1,0:T(8,128)(2,1)S(1)}, bf16[8,320,128]{2,1,0:T(8,128)(2,1)S(1)}, u32[]{:S(2)}, u32[]{:S(2)}) %collective-permute-start.1) | collective-permute-done | bytes 655392 | tf_op jit(solution)/shard_map/ppermute | solution.py:26
  94.6 1.6 shard_map.114
  96.2 0.0 reduce-scatter.2.cloned.1.call-update
  96.3 25.5 %all_to_all.25 = bf16[8,64,128]{2,1,0:T(8,128)(2,1)S(1)} all-to-all(bf16[8,64,128]{2,1,0:T(8,128)(2,1)S(1)} %get-tuple-element.45), channel_id=1, replica_groups={{0,128,256,384,512,640,768,896},{64,192,320,448,576,704,832,960},{1,129..., dimensions={0} | all-to-all | bytes 262144 | tf_op jit(solution)/shard_map/all_to_all | solution.py:32
  121.8 0.1 pad_maximum_fusion
  121.9 26.8 %all_to_all.26.parts_ref = bf16[64,8,768]{2,1,0:T(8,128)(2,1)} all-to-all(bf16[64,8,768]{2,1,0:T(8,128)(2,1)S(1)} %pad_maximum_fusion), channel_id=1, replica_groups=mesh['dp'=16,'expert'=64] {'expert'}, dimensions={0} | all-to-all | bytes 1572864 | tf_op jit(solution)/shard_map/all_to_all | solution.py:21
  148.7 1.8 %shard_map.116 = bf16[64,8,256]{2,1,0:T(8,128)(2,1)} custom-call(bf16[64,8,768]{2,1,0:T(8,128)(2,1)} %all_to_all.26.parts_ref), custom_call_target="tpu_custom_call" | custom-call | tf_op jit(solution)/shard_map/pallas_call | solution.py:220
  150.6 8.7 %all-to-all-start.4 = ((bf16[64,8,256]{2,1,0:T(8,128)(2,1)}), bf16[64,8,256]{2,1,0:T(8,128)(2,1)S(1)}, u32[]{:S(2)}, u32[]{:S(2)}) async-start(bf16[64,8,256]{2,1,0:T(8,128)(2,1)} %shard_map.116), calls=%async_computation.5 | async-start | bytes 524288 | tf_op jit(solution)/shard_map/all_to_all | solution.py:21
  160.0 0.0 reduce-scatter.2.cloned.1.call-done
  160.0 0.9 copy-done.8
  161.0 3.3 %shard_map.115 = (bf16[32,1024]{1,0:T(8,128)(2,1)}, f32[8,32]{1,0:T(8,128)}, f32[64,384]{1,0:T(8,128)S(1)}, f32[64,384]{1,0:T(8,128)S(1)}, f32[24,1024]{1,0:T(8,128)S(1)}, /*index=5*/bf16[1024,768]{1,0:T(8,128)(2,1)S(1)}) custom-call(s32[8,32]{1,0:T(8,128)S(1)} %bitcast.35, f32[8,32]{1,0:T(8,128)S(1)} %bitcast.37, bf16[32,1024]{1,0:T(8,128)(2,1)S(1)} %copy-done.7, ...), custom_call_target="tpu_custom_call" | custom-call | tf_op jit(solution)/shard_map/pallas_call | solution.py:430
  164.3 7.4 %all-to-all-done.4 = bf16[64,8,256]{2,1,0:T(8,128)(2,1)S(1)} async-done(((bf16[64,8,256]{2,1,0:T(8,128)(2,1)}), bf16[64,8,256]{2,1,0:T(8,128)(2,1)S(1)}, u32[]{:S(2)}, u32[]{:S(2)}) %all-to-all-start.4) | async-done | bytes 262176 | tf_op jit(solution)/shard_map/all_to_all | solution.py:21
  171.6 1.1 shard_map.117
  (20 shorter events, 0.1 us)
Async XLA Ops:
  7.2 79.4 %all-gather.2.cloned.1.call-start = ((), (), s32[]{:S(2)}) async-start(), calls=%async_computation.6 | async-start | bytes 2228224 | tf_op jit(solution)/shard_map/all_gather | solution.py:503
  11.4 57.4 %copy-start.3 = (bf16[1,384,1024]{2,1,0:T(8,128)(2,1)S(1)}, bf16[1,384,1024]{2,1,0:T(8,128)(2,1)}, u32[]{:S(2)}) copy-start(bf16[1,384,1024]{2,1,0:T(8,128)(2,1)} %param.13) | copy-start | bytes 2359300
  11.5 41.9 %all-to-all-start = ((bf16[64,8,1280]{2,1,0:T(8,128)(2,1)}), bf16[64,8,1280]{2,1,0:T(8,128)(2,1)}, u32[]{:S(2)}, u32[]{:S(2)}) async-start(bf16[64,8,1280]{2,1,0:T(8,128)(2,1)} %bitcast.38), calls=%async_computation | async-start | bytes 2621440 | tf_op jit(solution)/shard_map/all_to_all | solution.py:21
  25.9 43.0 %copy-start.1 = (bf16[1,1024,384]{2,1,0:T(8,128)(2,1)S(1)}, bf16[1,1024,384]{2,1,0:T(8,128)(2,1)}, u32[]{:S(2)}) copy-start(bf16[1,1024,384]{2,1,0:T(8,128)(2,1)} %param.11) | copy-start | bytes 2359300
  25.9 43.0 %copy-start.2 = (bf16[1,1024,384]{2,1,0:T(8,128)(2,1)S(1)}, bf16[1,1024,384]{2,1,0:T(8,128)(2,1)}, u32[]{:S(2)}) copy-start(bf16[1,1024,384]{2,1,0:T(8,128)(2,1)} %param.12) | copy-start | bytes 2359300
  55.4 25.7 %all-to-all-start.1 = ((bf16[64,8,256]{2,1,0:T(8,128)(2,1)}), bf16[64,8,256]{2,1,0:T(8,128)(2,1)}, u32[]{:S(2)}, u32[]{:S(2)}) async-start(bf16[64,8,256]{2,1,0:T(8,128)(2,1)} %shard_map.111), calls=%async_computation.1 | async-start | bytes 524288 | tf_op jit(solution)/shard_map/all_to_all | solution.py:21
  68.8 91.2 %reduce-scatter.2.cloned.1.call-start = ((), (), s32[]{:S(2)}) async-start(), calls=%async_computation.7 | async-start | bytes 1916928 | tf_op jit(solution)/shard_map/reduce_scatter | solution.py:40
  74.3 0.8 copy-start.5
  75.1 1.0 copy-start.11
  81.1 11.5 %collective-permute-start = (bf16[8,576,128]{2,1,0:T(8,128)(2,1)}, bf16[8,576,128]{2,1,0:T(8,128)(2,1)S(1)}, u32[]{:S(2)}, u32[]{:S(2)}) collective-permute-start(bf16[8,576,128]{2,1,0:T(8,128)(2,1)} %copy-done.11), channel_id=1, source_target_pairs={{0,64},{64,0},{128,192},{192,128},{256,320},{320,256},{384,448},{4... | collective-permute-start | bytes 3538952 | tf_op jit(solution)/shard_map/ppermute | solution.py:26
  86.6 1.6 copy-start.4
  90.6 4.0 %collective-permute-start.1 = (bf16[8,320,128]{2,1,0:T(8,128)(2,1)S(1)}, bf16[8,320,128]{2,1,0:T(8,128)(2,1)S(1)}, u32[]{:S(2)}, u32[]{:S(2)}) collective-permute-start(bf16[8,320,128]{2,1,0:T(8,128)(2,1)S(1)} %get-tuple-element.44), channel_id=1, source_target_pairs={{0,64},{64,0},{128,192},{192,128},{256,320},{320,256},{384,448},{4... | collective-permute-start | bytes 1966088 | tf_op jit(solution)/shard_map/ppermute | solution.py:26
  96.2 25.6 %copy-start.6 = (bf16[512,512]{1,0:T(8,128)(2,1)S(1)}, bf16[512,512]{1,0:T(8,128)(2,1)}, u32[]{:S(2)}) copy-start(bf16[512,512]{1,0:T(8,128)(2,1)} %copy-done.5) | copy-start | bytes 1572868
  121.9 38.1 %copy-start.7 = (bf16[32,1024]{1,0:T(8,128)(2,1)S(1)}, bf16[32,1024]{1,0:T(8,128)(2,1)}, u32[]{:S(2)}) copy-start(bf16[32,1024]{1,0:T(8,128)(2,1)} %cotangent_ref.1) | copy-start | bytes 196612
  121.9 38.1 %copy-start.9 = (s32[32,8]{0,1:T(8,128)S(1)}, s32[32,8]{0,1:T(8,128)}, u32[]{:S(2)}) copy-start(s32[32,8]{0,1:T(8,128)} %param.10) | copy-start | bytes 3076
  121.9 38.1 %copy-start.10 = (f32[32,8]{0,1:T(8,128)S(1)}, f32[32,8]{0,1:T(8,128)}, u32[]{:S(2)}) copy-start(f32[32,8]{0,1:T(8,128)} %param.9) | copy-start | bytes 3076
  148.7 11.3 %copy-start = (bf16[64,8,768]{2,1,0:T(8,128)(2,1)S(1)}, bf16[64,8,768]{2,1,0:T(8,128)(2,1)}, u32[]{:S(2)}) copy-start(bf16[64,8,768]{2,1,0:T(8,128)(2,1)} %all_to_all.26.parts_ref) | copy-start | bytes 2359300
  150.6 21.1 %all-to-all-start.4 = ((bf16[64,8,256]{2,1,0:T(8,128)(2,1)}), bf16[64,8,256]{2,1,0:T(8,128)(2,1)S(1)}, u32[]{:S(2)}, u32[]{:S(2)}) async-start(bf16[64,8,256]{2,1,0:T(8,128)(2,1)} %shard_map.116), calls=%async_computation.5 | async-start | bytes 524288 | tf_op jit(solution)/shard_map/all_to_all | solution.py:21
  160.0 0.9 copy-start.8
Sparse Core Ops, SparseCore 0:
  11.6 59.4 all-gather.1
  96.4 48.9 reduce-scatter.1
